TPU v7x, 32 devices: a whole 2x2x4 slice. The times are simulated.
32 devices in a mesh: row: 8 (over z, y), proto: 4 (over x, core).
Axes of the slice: x: 2, y: 2, z: 4, core: 2. Of those that a mesh axis runs over, the one named last changes fastest.
Arguments:
- embeddings: bfloat16 [2048, 256], P('row')
- queue_feats: bfloat16 [4096, 256], P('row')
- prototypes: bfloat16 [256, 65536], P('row', 'proto')
- crop_image: int32 [2048], P('row'), may hold values from 0 to 255, as said below
- fill_count: int32 [1], replicated, may hold values from 2048 to 4096
Outputs:
- grad_embed: float32 [2048, 256], P('row')
- grad_proto: float32 [256, 65536], P('row', 'proto')
- loss: float32 [1], replicated
Inputs may be any that keep to these rules, and one draw needn't show every extreme that they name: `crop_image`: each image index is named by exactly 8 crops, all within one aligned block of 256 rows (the rows of one device); block b holds images b * 32 to (b + 1) * 32 - 1.
All inputs are finite; a program needn't handle non-finite values.
Results may differ from a plain program's by a relative error of at most 0.002.
Values may be sent and summed in bfloat16 or wider, within the bound.
No kernel may reach another device: no remote copies, remote signals or barrier semaphores. Data moves between devices by JAX's collectives and lax.ppermute only.
A program may use at most 128 MiB of HBM per device.

v0:
```python
import math

import jax
import jax.numpy as jnp
from jax import lax
from jax.sharding import PartitionSpec as P

CROPS = 8
ITERS = 3


ENTROPY_SMOOTHER = 0.05
SOFTMAX_TEMPER = 0.1


def unit_rows(raw):
    values = raw.astype(jnp.float32)
    inverse = lax.rsqrt(jnp.sum(values * values, axis=1, keepdims=True) + 1e-06)
    return (values * inverse, inverse)


def body(embeddings, queue_feats, prototypes, crop_image, fill_count):
    normed_exact, inverse = unit_rows(embeddings)
    normed = normed_exact.astype(jnp.bfloat16)
    queue_normed = unit_rows(queue_feats)[0].astype(jnp.bfloat16)
    batch_rows = normed.shape[0]
    feat_dim = normed.shape[1]
    image_local = batch_rows // CROPS
    local_image = crop_image - lax.axis_index("row") * image_local
    image_ids = jnp.arange(image_local, dtype=jnp.int32)
    membership = (image_ids[:, None] == local_image[None, :]).astype(jnp.bfloat16)
    columns = lax.all_to_all(prototypes, "row", split_axis=1, concat_axis=0, tiled=True)
    batch_all, queue_all, member_all = (
        lax.all_gather(normed, "row", axis=0, tiled=True),
        lax.all_gather(queue_normed, "row", axis=0, tiled=True),
        lax.all_gather(membership, "row", axis=0, tiled=True),
    )
    total_batch = batch_all.shape[0]
    total_queue = queue_all.shape[0]
    queue_live = (jnp.arange(total_queue, dtype=jnp.int32) < fill_count[0]).astype(jnp.float32)
    live = jnp.concatenate([jnp.ones((total_batch,), jnp.float32), queue_live])
    rows_all = jnp.concatenate([batch_all, queue_all], axis=0)
    total_rows = rows_all.shape[0]
    row_span = math.gcd(total_rows, 2048)
    row_blocks = rows_all.reshape(total_rows // row_span, row_span, feat_dim)
    centroid_matrix = live
    column = jnp.zeros((columns.shape[1],), jnp.float32)
    for sweep_index in range(ITERS):

        def column_block(cumulative_accumulator, inputs_pair):
            row_block, row_scale = inputs_pair
            centroid_similarity = jnp.dot(row_block, columns, preferred_element_type=jnp.float32)
            return (
                cumulative_accumulator
                + jnp.sum(
                    jnp.exp(centroid_similarity / ENTROPY_SMOOTHER) * row_scale[:, None], axis=0
                ),
                None,
            )

        col_total, _ = lax.scan(
            column_block,
            jnp.zeros((columns.shape[1],), jnp.float32),
            (row_blocks, centroid_matrix.reshape(total_rows // row_span, row_span)),
        )
        column = 1.0 / col_total
        if sweep_index + 1 < ITERS:

            def row_block_sums(row_block):
                centroid_similarity = jnp.dot(
                    row_block, columns, preferred_element_type=jnp.float32
                )
                return jnp.sum(
                    jnp.exp(centroid_similarity / ENTROPY_SMOOTHER) * column[None, :], axis=1
                )

            centroid_matrix = live / lax.psum(
                lax.map(row_block_sums, row_blocks).reshape(total_rows), ("row", "proto")
            )
    per_span = math.gcd(lax.axis_size("row"), max(1, 2048 // batch_rows))
    batch_span = batch_rows * per_span
    span_count = total_batch // batch_span
    batch_blocks = batch_all.reshape(span_count, batch_span, feat_dim)

    def batch_sums(row_block):
        centroid_similarity = jnp.dot(row_block, columns, preferred_element_type=jnp.float32)
        allotment_share = jnp.sum(
            jnp.exp(centroid_similarity / ENTROPY_SMOOTHER) * column[None, :], axis=1
        )
        softmax_portion = jnp.sum(jnp.exp(centroid_similarity / SOFTMAX_TEMPER), axis=1)
        return (allotment_share, softmax_portion)

    code_parts, soft_parts = lax.map(batch_sums, batch_blocks)
    overall_mass_sum, softmax_total = lax.psum(
        (code_parts.reshape(total_batch), soft_parts.reshape(total_batch)), ("row", "proto")
    )
    member_blocks = member_all.astype(jnp.float32).reshape(
        span_count, per_span, image_local, batch_rows
    )

    def slopes(cumulative_accumulator, inputs_group):
        row_block, member_block, code_sum, soft_sum = inputs_group
        centroid_similarity = jnp.dot(row_block, columns, preferred_element_type=jnp.float32)
        cluster_allotment = (
            jnp.exp(centroid_similarity / ENTROPY_SMOOTHER) * column[None, :] / code_sum[:, None]
        )
        assigned_groups = cluster_allotment.reshape(per_span, batch_rows, -1)
        per_image = jnp.einsum(
            "gib,gbk->gik", member_block, assigned_groups, precision=lax.Precision.HIGHEST
        )
        grouped = jnp.einsum(
            "gib,gik->gbk", member_block, per_image, precision=lax.Precision.HIGHEST
        )
        target_codes = (grouped - assigned_groups).reshape(batch_span, -1) / (CROPS - 1)
        predicted_probs = jnp.exp(centroid_similarity / SOFTMAX_TEMPER) / soft_sum[:, None]
        logit_gradient = ((predicted_probs - target_codes) / SOFTMAX_TEMPER).astype(jnp.bfloat16)
        loss_portion = jnp.sum(
            target_codes * (jnp.log(soft_sum)[:, None] - centroid_similarity / SOFTMAX_TEMPER)
        )
        grad_cols = cumulative_accumulator[0] + lax.dot_general(
            row_block, logit_gradient, (((0,), (0,)), ((), ())), preferred_element_type=jnp.float32
        )
        normed_part = lax.dot_general(
            logit_gradient, columns, (((1,), (1,)), ((), ())), preferred_element_type=jnp.float32
        )
        return ((grad_cols, cumulative_accumulator[1] + loss_portion), normed_part)

    (grad_cols, loss_local), normed_parts = lax.scan(
        slopes,
        (jnp.zeros(columns.shape, jnp.float32), jnp.zeros((), jnp.float32)),
        (
            batch_blocks,
            member_blocks,
            overall_mass_sum.reshape(span_count, batch_span),
            softmax_total.reshape(span_count, batch_span),
        ),
    )
    owned = lax.psum_scatter(
        normed_parts.reshape(total_batch, feat_dim), "row", scatter_dimension=0, tiled=True
    )
    normed_grad = lax.psum(owned, "proto")
    grad_proto = lax.all_to_all(grad_cols, "row", split_axis=0, concat_axis=1, tiled=True)
    loss_total = lax.psum(loss_local, ("row", "proto"))
    loss = loss_total / total_batch
    grad_embed = inverse * (
        normed_grad - normed_exact * jnp.sum(normed_exact * normed_grad, axis=1, keepdims=True)
    )
    return (grad_embed, grad_proto, loss.reshape(1))


def solution(mesh):
    placed = (P("row", None), P("row", None), P("row", "proto"), P("row"), P())
    return jax.shard_map(
        body,
        mesh=mesh,
        in_specs=placed,
        out_specs=(P("row", None), P("row", "proto"), P()),
        check_vma=False,
    )
```

profile of v0, /device:TPU:0, one launch (start us, length us, event | category | flops | bytes accessed | tf_op | source)
XLA Modules:
  0.0 519.1 jit_solution(17987631648974948258)
XLA Ops:
  7.2 0.0 all-gather.3.cloned.1.call-start
  7.2 1.0 fusion.28
  8.3 0.5 copy-done.6
  8.8 1.7 fusion.24
  10.4 0.0 all-gather.3.cloned.1.call-update
  10.5 0.0 all-gather.5.cloned.1.call-start
  10.5 1.1 fusion.20
  11.6 1.8 fusion.21
  13.4 0.0 all-gather.5.cloned.1.call-update
  13.4 2.3 copy.13
  15.8 7.3 %all-to-all-start = ((bf16[32,8,2048]{2,0,1:T(8,128)(2,1)}), bf16[32,8,2048]{2,0,1:T(8,128)(2,1)}, u32[]{:S(2)}, u32[]{:S(2)}) async-start(bf16[32,8,2048]{2,0,1:T(8,128)(2,1)} %bitcast.59), calls=%async_computation | async-start | bytes 2097152 | tf_op jit(solution)/shard_map/all_to_all | solution.py:32
  23.0 0.0 reduce-scatter.2.cloned.1.call-start
  23.8 0.7 broadcast_subtract_fusion
  24.5 57.5 %all_gather.10 = bf16[256,256]{1,0:T(8,128)(2,1)} all-gather(bf16[32,256]{1,0:T(8,128)(2,1)S(1)} %fusion.29), channel_id=1, replica_groups=mesh['row'=8,'proto'=4] {'row'}, dimensions={0}, use_global_device_ids=true | all-gather | bytes 147456 | tf_op jit(solution)/shard_map/all_gather | solution.py:36
  82.0 30.6 %all-gather.5.cloned.1.call-done = bf16[4096,256]{1,0:T(8,128)(2,1)} async-done(((bf16[512,256]{1,0:T(8,128)(2,1)}), bf16[4096,256]{1,0:T(8,128)(2,1)}) %all-gather.5.cloned.1.call-update) | async-done | bytes 2097168 | tf_op jit(solution)/shard_map/all_gather | solution.py:35
  112.6 2.1 pad_maximum_fusion
  114.7 0.0 all-to-all-done
  114.7 14.3 %while.66 = (s32[]{:T(128)}, f32[2048]{0:T(1024)S(1)}, bf16[3,2048,256]{2,1,0:T(8,128)(2,1)S(1)}, bf16[256,2048]{1,0:T(8,128)(2,1)}, f32[3,2048]{1,0:T(4,128)S(1)}, /*index=5*/s32[]{:T(128)}, s32[]{:T(128)}) while((s32[]{:T(128)}, f32[2048]{0:T(1024)S(1)}, bf16[3,2048,256]{2,1,0:T(8,128)(2,1)S(1)}, bf16[256,2048]{1,0:T(8,128)(2,1)}, ...), condition=%wide.region_6.7_spmd.clone, body=%wide.region_4.6_spmd.clone.sunk | while | flops 2160068608 | bytes 2154591 | solution.py:61
  114.7 4.7 multiply_reduce_fusion.12
  119.5 4.7 multiply_reduce_fusion.12
  124.3 4.7 multiply_reduce_fusion.12
  129.0 14.9 %while.64 = (s32[]{:T(128)}, f32[3,2048]{1,0:T(4,128)S(1)}, bf16[3,2048,256]{2,1,0:T(8,128)(2,1)S(1)}, bf16[256,2048]{1,0:T(8,128)(2,1)}, f32[2048]{0:T(1024)S(1)}, /*index=5*/s32[]{:T(128)}, s32[]{:T(128)}) while((s32[]{:T(128)}, f32[3,2048]{1,0:T(4,128)S(1)}, bf16[3,2048,256]{2,1,0:T(8,128)(2,1)S(1)}, bf16[256,2048]{1,0:T(8,128)(2,1)}, ...), condition=%wide.region_9.10_spmd, body=%wide.region_7.9_spmd.sunk | while | flops 2160064512 | bytes 2130005 | solution.py:78
  129.0 4.8 multiply_reduce_fusion.10
  133.8 0.1 dynamic_update_slice.17
  134.0 4.8 multiply_reduce_fusion.10
  138.8 0.1 dynamic_update_slice.17
  139.0 4.8 multiply_reduce_fusion.10
  143.7 0.1 dynamic_update_slice.17
  143.9 39.4 %psum.43 = f32[6144]{0:T(1024)S(1)} all-reduce(f32[6144]{0:T(1024)S(1)} %reshape.88), channel_id=1, replica_groups=mesh['row'=8,'proto'=4] {'row','proto'}, use_global_device_ids=true, to_apply=%region_10.11 | all-reduce | flops 6144 | bytes 49152 | tf_op jit(solution)/shard_map/psum | solution.py:77
  183.4 14.3 %while.67 = (s32[]{:T(128)}, f32[2048]{0:T(1024)S(1)}, bf16[3,2048,256]{2,1,0:T(8,128)(2,1)S(1)}, bf16[256,2048]{1,0:T(8,128)(2,1)}, f32[3,2048]{1,0:T(4,128)S(1)}, /*index=5*/s32[]{:T(128)}, s32[]{:T(128)}) while((s32[]{:T(128)}, f32[2048]{0:T(1024)S(1)}, bf16[3,2048,256]{2,1,0:T(8,128)(2,1)S(1)}, ...), condition=%wide.region_13.14_spmd.clone, body=%wide.region_11.13_spmd.clone.sunk | while | flops 2160068608 | bytes 2154591 | solution.py:61
  183.4 4.7 multiply_reduce_fusion.13
  188.2 4.7 multiply_reduce_fusion.13
  193.0 4.7 multiply_reduce_fusion.13
  197.8 14.9 %while.65 = (s32[]{:T(128)}, f32[3,2048]{1,0:T(4,128)S(1)}, bf16[3,2048,256]{2,1,0:T(8,128)(2,1)S(1)}, bf16[256,2048]{1,0:T(8,128)(2,1)}, f32[2048]{0:T(1024)S(1)}, /*index=5*/s32[]{:T(128)}, s32[]{:T(128)}) while((s32[]{:T(128)}, f32[3,2048]{1,0:T(4,128)S(1)}, bf16[3,2048,256]{2,1,0:T(8,128)(2,1)S(1)}, bf16[256,2048]{1,0:T(8,128)(2,1)}, ...), condition=%wide.region_16.17_spmd, body=%wide.region_14.16_spmd.sunk | while | flops 2160064512 | bytes 2130005 | solution.py:78
  197.8 4.8 multiply_reduce_fusion.11
  202.6 0.1 dynamic_update_slice.18
  202.7 4.8 multiply_reduce_fusion.11
  207.5 0.1 dynamic_update_slice.18
  207.7 4.8 multiply_reduce_fusion.11
  212.5 0.1 dynamic_update_slice.18
  212.7 40.4 %psum.44 = f32[6144]{0:T(1024)S(1)} all-reduce(f32[6144]{0:T(1024)S(1)} %reshape.90), channel_id=1, replica_groups=mesh['row'=8,'proto'=4] {'row','proto'}, use_global_device_ids=true, to_apply=%region_17.18 | all-reduce | flops 6144 | bytes 49152 | tf_op jit(solution)/shard_map/psum | solution.py:77
  253.1 14.1 %while.68 = (s32[]{:T(128)}, f32[2048]{0:T(1024)S(1)}, bf16[3,2048,256]{2,1,0:T(8,128)(2,1)}, bf16[256,2048]{1,0:T(8,128)(2,1)}, f32[3,2048]{1,0:T(4,128)S(1)}, /*index=5*/s32[]{:T(128)}, s32[]{:T(128)}) while((s32[]{:T(128)}, f32[2048]{0:T(1024)S(1)}, bf16[3,2048,256]{2,1,0:T(8,128)(2,1)}, bf16[256,2048]{1,0:T(8,128)(2,1)}, ...), condition=%wide.region_20.21_spmd.clone, body=%wide.region_18.20_spmd.clone.sunk | while | flops 2160068608 | bytes 2155099 | solution.py:61
  253.2 4.7 multiply_reduce_fusion.14
  257.9 4.6 multiply_reduce_fusion.14
  262.6 4.6 multiply_reduce_fusion.14
  267.3 10.5 %exponential_reduce_fusion = (f32[2048]{0:T(1024)S(1)}, f32[2048]{0:T(1024)S(1)}, f32[2048,2048]{1,0:T(8,128)}) fusion(f32[2048]{0:T(1024)S(1)} %broadcast_divide_fusion, bf16[2048,256]{1,0:T(8,128)(2,1)S(1)} %copy-done.1, bf16[256,2048]{1,0:T(8,128)(2,1)} %bitcast.5), kind=kOutput, calls=%fused_computation.33 | convolution fusion | flops 2168451072 | bytes 18898944 | tf_op jit(solution)/shard_map/while/body/eval_jaxpr/dot_general | solution.py:103
  277.8 40.3 %all-reduce.1 = (f32[2048]{0:T(1024)S(1)}, f32[2048]{0:T(1024)S(1)}) all-reduce(f32[2048]{0:T(1024)S(1)} %get-tuple-element.246, f32[2048]{0:T(1024)S(1)} %get-tuple-element.245), channel_id=1, replica_groups=mesh['row'=8,'proto'=4] {'row','proto'}, use_global_device_ids=true, to_apply=%region_22.23 | all-reduce | flops 4096 | bytes 32768 | tf_op jit(solution)/shard_map/psum | solution.py:94
  318.1 7.7 %fusion.18 = f32[2048,2048]{1,0:T(8,128)S(1)} fusion(f32[2048,2048]{1,0:T(8,128)} %get-tuple-element.301, f32[2048]{0:T(1024)S(1)} %get-tuple-element.297, f32[2048]{0:T(1024)S(1)} %broadcast_divide_fusion), kind=kLoop, calls=%fused_computation.34 | loop fusion | flops 12582912 | bytes 33570816 | tf_op jit(solution)/shard_map/while/body/eval_jaxpr/div | solution.py:105
  325.8 6.4 %fusion.32 = f32[8,32,2048]{2,1,0:T(8,128)S(1)} fusion(bf16[8,32,256]{2,1,0:T(8,128)(2,1)S(1)} %bitcast.97, f32[8,256,2048]{2,1,0:T(8,128)S(1)} %bitcast.91), kind=kOutput, calls=%fused_computation.63 | convolution fusion | flops 1610612736 | bytes 19005440 | tf_op jit(solution)/shard_map/while/body/eval_jaxpr/gib,gbk->gik/dot_general | solution.py:108
  332.3 11.8 %subtract_multiply_fusion = f32[8,256,2048]{2,1,0:T(8,128)} fusion(f32[8,256,2048]{2,1,0:T(8,128)S(1)} %bitcast.92, bf16[8,32,256]{2,1,0:T(8,128)(2,1)S(1)} %bitcast.98, f32[8,32,2048]{2,1,0:T(8,128)S(1)} %fusion.32), kind=kOutput, calls=%fused_computation.31 | convolution fusion | flops 1619001344 | bytes 35782656 | tf_op jit(solution)/shard_map/while/body/eval_jaxpr/gib,gik->gbk/dot_general | solution.py:111
  344.0 15.1 %fusion.17 = (f32[]{:T(128)}, bf16[2048,2048]{1,0:T(8,128)(2,1)S(1)}) fusion(f32[8,256,2048]{2,1,0:T(8,128)} %subtract_multiply_fusion, f32[2048,2048]{1,0:T(8,128)} %get-tuple-element.301, f32[2048]{0:T(1024)S(1)} %log.4, f32[2048]{0:T(1024)S(1)} %get-tuple-element.298), kind=kLoop, calls=%fused_computation.30 | loop fusion | flops 33554432 | bytes 41959428 | tf_op jit(solution)/shard_map/while/body/eval_jaxpr/reduce_sum | solution.py:117
  359.2 3.2 copy-done
  362.4 5.1 fusion.33
  367.5 0.0 reduce-scatter.2.cloned.1.call-update
  367.5 7.2 %fusion.34 = f32[256,2048]{1,0:T(8,128)} fusion(bf16[2048,256]{1,0:T(8,128)(2,1)S(1)} %copy-done.2, bf16[2048,2048]{1,0:T(8,128)(2,1)} %copy-done), kind=kOutput, calls=%fused_computation.65 | convolution fusion | flops 2147483648 | bytes 11534336 | tf_op jit(solution)/shard_map/while/body/eval_jaxpr/dot_general | solution.py:120
  374.6 4.8 all-to-all-start.1
  379.5 0.0 all-reduce.4.cloned.1.call-start
  379.5 87.0 %reduce-scatter.2.cloned.1.call-done = f32[256,256]{1,0:T(8,128)} async-done(((f32[2048,256]{1,0:T(8,128)}), f32[256,256]{1,0:T(8,128)}) %reduce-scatter.2.cloned.1.call-update) | async-done | bytes 262160 | tf_op jit(solution)/shard_map/reduce_scatter | solution.py:138
  466.5 0.0 all-reduce.4.cloned.1.call-update
  466.6 39.8 %psum.47 = f32[]{:T(128)} all-reduce(f32[]{:T(128)} %get-tuple-element.299), channel_id=1, replica_groups=mesh['row'=8,'proto'=4] {'row','proto'}, use_global_device_ids=true, to_apply=%region_27.28 | all-reduce | flops 1 | bytes 8 | tf_op jit(solution)/shard_map/psum | solution.py:143
  507.0 0.0 all-to-all-done.1
  507.0 1.5 copy.11
  508.5 1.1 fusion.25
  509.6 1.8 fusion.27
  (55 shorter events, 0.4 us)
Async XLA Ops:
  7.2 74.8 %all-gather.3.cloned.1.call-start = ((), (), s32[]{:S(2)}) async-start(), calls=%async_computation.3 | async-start | bytes 1179648 | tf_op jit(solution)/shard_map/all_gather | solution.py:34
  8.2 0.5 copy-start.6
  10.5 102.1 %all-gather.5.cloned.1.call-start = ((), (), s32[]{:S(2)}) async-start(), calls=%async_computation.4 | async-start | bytes 2359296 | tf_op jit(solution)/shard_map/all_gather | solution.py:35
  15.8 98.9 %all-to-all-start = ((bf16[32,8,2048]{2,0,1:T(8,128)(2,1)}), bf16[32,8,2048]{2,0,1:T(8,128)(2,1)}, u32[]{:S(2)}, u32[]{:S(2)}) async-start(bf16[32,8,2048]{2,0,1:T(8,128)(2,1)} %bitcast.59), calls=%async_computation | async-start | bytes 2097152 | tf_op jit(solution)/shard_map/all_to_all | solution.py:32
  23.0 443.5 %reduce-scatter.2.cloned.1.call-start = ((), (), s32[]{:S(2)}) async-start(), calls=%async_computation.5 | async-start | bytes 2359296 | tf_op jit(solution)/shard_map/reduce_scatter | solution.py:138
  212.6 40.5 %copy-start.3 = (bf16[3,2048,256]{2,1,0:T(8,128)(2,1)}, bf16[3,2048,256]{2,1,0:T(8,128)(2,1)S(1)}, u32[]{:S(2)}) copy-start(bf16[3,2048,256]{2,1,0:T(8,128)(2,1)S(1)} %get-tuple-element.573) | copy-start | bytes 9437188
  253.1 14.2 %copy-start.1 = (bf16[2048,256]{1,0:T(8,128)(2,1)S(1)}, bf16[2048,256]{1,0:T(8,128)(2,1)}, u32[]{:S(2)}) copy-start(bf16[2048,256]{1,0:T(8,128)(2,1)} %all-gather.3.cloned.1.call-done) | copy-start | bytes 3145732
  318.1 7.7 %copy-start.5 = (bf16[256,256]{1,0:T(8,128)(2,1)S(1)}, bf16[256,256]{1,0:T(8,128)(2,1)}, u32[]{:S(2)}) copy-start(bf16[256,256]{1,0:T(8,128)(2,1)} %all_gather.10) | copy-start | bytes 393220
  359.2 3.2 copy-start
  359.2 8.3 %copy-start.2 = (bf16[2048,256]{1,0:T(8,128)(2,1)S(1)}, bf16[2048,256]{1,0:T(8,128)(2,1)}, u32[]{:S(2)}) copy-start(bf16[2048,256]{1,0:T(8,128)(2,1)} %all-gather.3.cloned.1.call-done) | copy-start | bytes 3145732
  367.5 141.1 %copy-start.4 = (bf16[256,256]{1,0:T(8,128)(2,1)S(1)}, bf16[256,256]{1,0:T(8,128)(2,1)}, u32[]{:S(2)}) copy-start(bf16[256,256]{1,0:T(8,128)(2,1)} %param.15) | copy-start | bytes 393220
  367.5 141.1 %copy-start.7 = (f32[256]{0:T(256)S(1)}, f32[256]{0:T(256)}, u32[]{:S(2)}) copy-start(f32[256]{0:T(256)} %copy-done.6) | copy-start | bytes 3076
  374.6 132.4 %all-to-all-start.1 = ((f32[8,32,2048]{2,1,0:T(8,128)}), f32[8,32,2048]{2,1,0:T(8,128)S(1)}, u32[]{:S(2)}, u32[]{:S(2)}) async-start(f32[8,32,2048]{2,1,0:T(8,128)} %bitcast.94), calls=%async_computation.2 | async-start | bytes 4194304 | tf_op jit(solution)/shard_map/all_to_all | solution.py:142
  379.5 129.0 %all-reduce.4.cloned.1.call-start = ((), (), s32[]{:S(2)}) async-start(), calls=%async_computation.6 | async-start | bytes 524288 | tf_op jit(solution)/shard_map/psum | solution.py:141
Sparse Core Ops, SparseCore 0:
  10.6 50.4 all-gather.2
  63.8 48.7 all-gather.4
  367.6 98.8 reduce-scatter.1
  468.7 31.1 all-reduce.3
where the time goes:
time: 520 us; the launch traced here: 519 us
  blocking collectives  217 us (42%)
  waiting for transfers between devices  118 us (23%)
  matrix products  112 us (22%)
  other arithmetic  34.2 us (7%)
  between operations  16.5 us (3%)
  starting transfers between devices  12.3 us (2%)
  local copies, waits for them, and re-layouts  8.53 us (2%)
    reduce_scatter x1, waiting for transfers between devices, body(): lax.psum_scatter(normed_parts.reshape(total_batch, feat_dim), 'row', scat...  87 us
    psum x2, blocking collectives, body(): lax.psum(lax.map(row_block_sums, row_blocks).reshape(total_rows), ('row',...  79.9 us
    all_gather x1, blocking collectives, body(): lax.all_gather(membership, 'row', axis=0, tiled=True)  57.5 us
    dot_general x9, matrix products, column_block(): jnp.dot(row_block, columns, preferred_element_type=jnp.float32)  42.2 us
    psum x1, blocking collectives, body(): lax.psum((code_parts.reshape(total_batch), soft_parts.reshape(total_batch...  40.3 us
    psum x1, blocking collectives, body(): loss_total = lax.psum(loss_local, ('row', 'proto'))  39.8 us
    all_gather x1, waiting for transfers between devices, body(): lax.all_gather(queue_normed, 'row', axis=0, tiled=True)  30.6 us
    dot_general x6, matrix products, row_block_sums(): jnp.dot(row_block, columns, preferred_element_type=jnp.float32)  28.7 us
  transfers between devices with their start and end apart: 6, of which 2 were waited for; matrix products, arithmetic and copies ran while one was open for 3% of the time, Pallas kernels for 0%

commit v1 on v0

v1 whole, which is shorter than its diff:
```python
import functools

import jax
import jax.numpy as jnp
from jax import lax
from jax.experimental import pallas as pl
from jax.experimental.pallas import tpu as pltpu
from jax.sharding import PartitionSpec as P

CROPS = 8
LOG2E = 1.4426950408889634
SOFT_SCALE = 10.0 * LOG2E
BLOCK = 1024
WIDE = 256

f32 = jnp.float32
bf16 = jnp.bfloat16
f16 = jnp.float16

VMEM = pl.BlockSpec(memory_space=pltpu.VMEM)
SMEM = pl.BlockSpec(memory_space=pltpu.SMEM)
ANY = pl.BlockSpec(memory_space=pl.ANY)


def limit(mib):
    return pltpu.CompilerParams(vmem_limit_bytes=mib << 20)


def bf16_terms(values):
    high = values.astype(bf16)
    rest = values - high.astype(f32)
    middle = rest.astype(bf16)
    return high, middle, (rest - middle.astype(f32)).astype(bf16)


def term_rows(values):
    high, middle, low = bf16_terms(values)
    return jnp.concatenate([high, middle, low] + [jnp.zeros_like(high)] * 5, axis=0)


def sum_terms(products):
    return products[0:1] + products[1:2] + products[2:3]


def dot_nt(left, right):
    return lax.dot_general(left, right, (((1,), (1,)), ((), ())), preferred_element_type=f32)


def dot_tn(left, right):
    return lax.dot_general(left, right, (((0,), (0,)), ((), ())), preferred_element_type=f32)


def unit_rows(raw):
    values = raw.astype(f32)
    inverse = lax.rsqrt(jnp.sum(values * values, axis=1, keepdims=True) + 1e-06)
    return values * inverse, inverse


def prep_kernel(place_ref, image_ref, embed_ref, queue_ref, unit_ref, order_ref, sorted_ref, queued_ref):
    row, core = place_ref[0], place_ref[1]
    rows = embed_ref.shape[0]
    half = rows // 2
    images = half // CROPS
    local = image_ref[...] - row * (rows // CROPS)
    across = jnp.broadcast_to(local, (rows, rows)).astype(f32)
    down = jnp.transpose(across, (1, 0))
    first = lax.broadcasted_iota(jnp.int32, (rows, rows), 0)
    second = lax.broadcasted_iota(jnp.int32, (rows, rows), 1)
    earlier = jnp.where((across == down) & (first < second), 1.0, 0.0)
    rank = jnp.sum(earlier, axis=0, keepdims=True).astype(jnp.int32)
    upper = jnp.where(local >= images, 1, 0)
    position = upper * half + rank * images + (local - upper * images)
    order = (first == position).astype(f32).astype(bf16)
    order_ref[...] = order
    normed = unit_rows(embed_ref[...])[0].astype(bf16)
    sorted_ref[...] = jnp.dot(order, normed, preferred_element_type=f32)
    queued_ref[...] = unit_rows(queue_ref[...])[0]
    queue_half = queue_ref.shape[0] // 2
    unit_ref[0:half, :] = sorted_ref[pl.ds(pl.multiple_of(core * half, half), half), :].astype(bf16)
    unit_ref[half : half + queue_half, :] = queued_ref[
        pl.ds(pl.multiple_of(core * queue_half, queue_half), queue_half), :
    ].astype(bf16)


def row_sums(column, total_batch, queue_blocks, mass_ref, out_ref):
    def one(index, carry):
        start = pl.multiple_of(index * BLOCK, BLOCK)
        out_ref[0:1, pl.ds(start, BLOCK)] = sum_terms(dot_nt(column, mass_ref[pl.ds(start, BLOCK), :]))
        return carry

    lax.fori_loop(0, total_batch // BLOCK + queue_blocks, one, 0)


def live_blocks(fill):
    return lax.div(fill + (BLOCK - 1), BLOCK)


def make_kernel(row_count, half, queue_half, total_batch, place_ref, fill_ref, columns_ref, *refs):
    units = refs[: row_count * 2]
    mass_ref, sums_ref, batch_ref, queue_ref, col_ref, sems = refs[row_count * 2 :]
    row, core = place_ref[0], place_ref[1]
    fill = fill_ref[0]
    copies = []
    for index, unit in enumerate(units):
        place = (row ^ (index // 2)) * 2 + (core ^ (index % 2))
        crops = pl.multiple_of(place * half, half)
        queued = pl.multiple_of(place * queue_half, queue_half)
        copies.append(
            pltpu.make_async_copy(
                unit.at[pl.ds(0, half), :], batch_ref.at[pl.ds(crops, half), :], sems.at[2 * index]
            )
        )
        copies.append(
            pltpu.make_async_copy(
                unit.at[pl.ds(half, queue_half), :],
                queue_ref.at[pl.ds(queued, queue_half), :],
                sems.at[2 * index + 1],
            )
        )
    for copy in copies:
        copy.start()
    total_queue = queue_ref.shape[0]
    total_rows = total_batch + total_queue
    width = columns_ref.shape[1]
    col_ref[...] = jnp.zeros_like(col_ref)
    sums_ref[...] = jnp.zeros_like(sums_ref)
    ones = jnp.ones((8, 128), bf16)
    bound = jnp.max(jnp.abs(columns_ref[...].astype(f32)))
    sums_ref[0:1, total_rows + total_batch : total_rows + total_batch + 128] = jnp.full((1, 128), bound, f32)
    for copy in copies:
        copy.wait()

    def add_columns(low, mass):
        col_ref[:, low : low + WIDE] += jnp.sum(mass.reshape(BLOCK // 8, 8, WIDE), axis=0)

    def crops_block(index, carry):
        start = pl.multiple_of(index * BLOCK, BLOCK)
        rows = batch_ref[pl.ds(start, BLOCK), :]
        lanes = None
        for low in range(0, width, WIDE):
            scores = jnp.dot(rows, columns_ref[:, low : low + WIDE], preferred_element_type=f32)
            soft = jnp.exp2(scores * SOFT_SCALE)
            mass = soft * soft
            mass_ref[pl.ds(start, BLOCK), low : low + WIDE] = mass.astype(bf16)
            add_columns(low, mass)
            for lane in range(0, WIDE, 128):
                part = soft[:, lane : lane + 128]
                lanes = part if lanes is None else lanes + part
        high, middle, small = bf16_terms(lanes)
        total = dot_nt(ones, high) + dot_nt(ones, middle) + dot_nt(ones, small)
        sums_ref[0:1, pl.ds(pl.multiple_of(total_rows + start, BLOCK), BLOCK)] = total[0:1]
        return carry

    lax.fori_loop(0, total_batch // BLOCK, crops_block, 0)

    def queue_block(index, carry):
        start = pl.multiple_of(index * BLOCK, BLOCK)
        rows = queue_ref[pl.ds(start, BLOCK), :]
        live = lax.broadcasted_iota(jnp.int32, (BLOCK, WIDE), 0) < fill - start
        place = pl.ds(pl.multiple_of(total_batch + start, BLOCK), BLOCK)
        for low in range(0, width, WIDE):
            scores = jnp.dot(rows, columns_ref[:, low : low + WIDE], preferred_element_type=f32)
            soft = jnp.exp2(scores * SOFT_SCALE)
            mass = jnp.where(live, soft * soft, 0.0)
            mass_ref[place, low : low + WIDE] = mass.astype(bf16)
            add_columns(low, mass)
        return carry

    lax.fori_loop(0, live_blocks(fill), queue_block, 0)
    column = term_rows(1.0 / jnp.sum(col_ref[...], axis=0, keepdims=True))
    row_sums(column, total_batch, live_blocks(fill), mass_ref, sums_ref)


def column_factor(fill, total_batch, parts, mass_ref, scale_ref, col_ref):
    total_rows = mass_ref.shape[0]
    total = parts[0][0:1, 0:total_rows]
    for part in parts[1:]:
        total = total + part[0:1, 0:total_rows]
    place = lax.broadcasted_iota(jnp.int32, (1, total_rows), 1)
    scale = jnp.where(place < total_batch + fill, 1.0 / total, 0.0)
    scale_ref[...] = term_rows(scale)
    col_ref[...] = jnp.zeros_like(col_ref)

    def one(index, carry):
        rows = pl.ds(pl.multiple_of(index * BLOCK, BLOCK), BLOCK)
        col_ref[...] += jnp.dot(scale_ref[:, rows], mass_ref[rows, :], preferred_element_type=f32)
        return carry

    lax.fori_loop(0, total_batch // BLOCK + live_blocks(fill), one, 0)
    return 1.0 / sum_terms(col_ref[...])


def sweep_kernel(total_batch, fill_ref, mass_ref, *refs):
    *parts, sums_ref, scale_ref, col_ref = refs
    fill = fill_ref[0]
    column = column_factor(fill, total_batch, parts, mass_ref, scale_ref, col_ref)
    sums_ref[...] = jnp.zeros_like(sums_ref)
    row_sums(term_rows(column), total_batch, live_blocks(fill), mass_ref, sums_ref)


def last_kernel(total_batch, fill_ref, mass_ref, *refs):
    *parts, sums_ref, column_ref, scale_ref, col_ref = refs
    fill = fill_ref[0]
    column = column_factor(fill, total_batch, parts, mass_ref, scale_ref, col_ref)
    column_ref[...] = column
    row_sums(term_rows(column), total_batch, 0, mass_ref, sums_ref)


def slope_kernel(crop_count, batch_ref, columns_ref, column_ref, *refs):
    *parts, soft_ref, normed_ref, grad_ref, loss_ref = refs
    total_batch, width = batch_ref.shape[0], columns_ref.shape[1]
    rows = 256
    wide = min(width, 512)
    grad_ref[...] = jnp.zeros_like(grad_ref)
    loss_ref[...] = jnp.zeros_like(loss_ref)

    def one(index, carry):
        start = pl.multiple_of(index * rows, rows)
        here = pl.ds(start, rows)

        def down(line, factor):
            return jnp.transpose(jnp.broadcast_to(factor(line), (128, rows)), (1, 0))[:, 0:1]

        code = parts[0][0:1, here]
        for part in parts[1:]:
            code = code + part[0:1, here]
        code_factor = down(code, lambda line: 1.0 / ((crop_count - 1) * line))
        soft_line = soft_ref[0:1, here]
        soft_factor = down(soft_line, lambda line: 10.0 / line)
        log_soft = down(soft_line, jnp.log)
        crops = batch_ref[here, :]
        crops_t = jnp.transpose(crops.astype(f32), (1, 0)).astype(bf16)
        normed = jnp.zeros((rows, crops.shape[1]), f32)
        loss = jnp.zeros((8, 128), f32)
        for low in range(0, width, wide):
            columns = columns_ref[:, low : low + wide]
            scores = jnp.dot(crops, columns, preferred_element_type=f32)
            soft = jnp.exp2(scores * SOFT_SCALE)
            assigned = (soft * soft) * column_ref[0:1, low : low + wide] * code_factor
            slabs = assigned.reshape(rows // 128, crop_count, 128 // crop_count, wide)
            grouped = jnp.sum(slabs, axis=1, keepdims=True)
            targets = (grouped - slabs).reshape(rows, wide)
            logits = (soft * soft_factor - targets * 10.0).astype(bf16)
            terms = targets * (log_soft - scores * 10.0)
            folded = jnp.sum(terms.reshape(rows // 8, 8, wide), axis=0)
            for lane in range(0, wide, 128):
                loss = loss + folded[:, lane : lane + 128]
            grad_ref[:, low : low + wide] += jnp.dot(crops_t, logits, preferred_element_type=f32)
            normed = normed + dot_nt(logits, columns)
        normed_ref[here, :] = normed
        loss_ref[...] += loss
        return carry

    lax.fori_loop(0, total_batch // rows, one, 0)


def finish_kernel(piece_count, proto_ref, embed_ref, order_ref, *refs):
    pieces, out_ref, sorted_ref = refs[:piece_count], refs[piece_count], refs[piece_count + 1]
    rows = embed_ref.shape[0]
    size = rows // piece_count
    proto = proto_ref[0]
    for index, piece in enumerate(pieces):
        other = proto ^ index
        place = (other % 2) * (piece_count // 2) + other // 2
        sorted_ref[pl.ds(pl.multiple_of(place * size, size), size), :] = piece[...]
    order = order_ref[...]
    high, middle, low = bf16_terms(sorted_ref[...])
    grad = dot_tn(order, high) + dot_tn(order, middle) + dot_tn(order, low)
    exact, inverse = unit_rows(embed_ref[...])
    out_ref[...] = inverse * (grad - exact * jnp.sum(exact * grad, axis=1, keepdims=True))


def solution(mesh):
    row_count, proto_count = mesh.shape["row"], mesh.shape["proto"]
    z_count = min(4, row_count)
    y_count = row_count // z_count
    x_count = proto_count // 2

    def shift_row(values, z, y):
        offset = z * y_count + y
        return lax.ppermute(values, "row", [(i, i ^ offset) for i in range(row_count)])

    def shift_proto(values, offset):
        return lax.ppermute(values, "proto", [(i, i ^ offset) for i in range(proto_count)])

    def shift_xy(values, x, y):
        pairs = []
        for i in range(row_count):
            for j in range(proto_count):
                pairs.append((i * proto_count + j, (i ^ y) * proto_count + (j ^ (2 * x))))
        return lax.ppermute(values, ("row", "proto"), pairs)

    def all_sum_parts(values):
        for offset in range(1, proto_count):
            pass
        moved = [shift_proto(values, offset) for offset in range(1, proto_count)]
        values = functools.reduce(jnp.add, moved, values)
        moved = [shift_row(values, 0, y) for y in range(1, y_count)]
        values = functools.reduce(jnp.add, moved, values)
        return [values] + [shift_row(values, z, 0) for z in range(1, z_count)]

    def body(embeddings, queue_feats, prototypes, crop_image, fill_count):
        batch_rows, feat = embeddings.shape
        queue_rows = queue_feats.shape[0]
        half, queue_half = batch_rows // 2, queue_rows // 2
        total_batch, total_queue = batch_rows * row_count, queue_rows * row_count
        total_rows = total_batch + total_queue
        row, proto = lax.axis_index("row"), lax.axis_index("proto")
        core, x, y, z = proto % 2, proto // 2, row % y_count, row // y_count
        place = jnp.stack([row, core]).astype(jnp.int32)
        unit_rows_count = half + queue_half

        unit, order = pl.pallas_call(
            prep_kernel,
            name="prep",
            out_shape=[
                jax.ShapeDtypeStruct((unit_rows_count, feat), bf16),
                jax.ShapeDtypeStruct((batch_rows, batch_rows), bf16),
            ],
            in_specs=[SMEM, VMEM, VMEM, VMEM],
            out_specs=[VMEM, VMEM],
            scratch_shapes=[pltpu.VMEM((batch_rows, feat), f32), pltpu.VMEM((queue_rows, feat), f32)],
            compiler_params=limit(12),
        )(place, crop_image.reshape(1, batch_rows), embeddings, queue_feats)

        columns = lax.all_to_all(prototypes, "row", split_axis=1, concat_axis=0, tiled=True)
        width = columns.shape[1]

        units = {(0, 0, 0): unit}
        for dz in range(1, z_count):
            units[dz, 0, 0] = shift_row(unit, dz, 0)
        for dy in range(1, y_count):
            for dz in range(z_count):
                units[dz, dy, 0] = shift_row(units[dz, 0, 0], 0, dy)
        for dz in range(z_count):
            for dy in range(y_count):
                units[dz, dy, 1] = shift_proto(units[dz, dy, 0], 1)
        unit_list = [units[i // y_count, i % y_count, c] for i in range(row_count) for c in range(2)]

        sums_size = total_rows + total_batch + 128
        mass, sums, batch = pl.pallas_call(
            functools.partial(make_kernel, row_count, half, queue_half, total_batch),
            name="make_mass",
            out_shape=[
                jax.ShapeDtypeStruct((total_rows, width), bf16),
                jax.ShapeDtypeStruct((1, sums_size), f32),
                jax.ShapeDtypeStruct((total_batch, feat), bf16),
            ],
            in_specs=[SMEM, SMEM, VMEM] + [ANY] * len(unit_list),
            out_specs=[VMEM, VMEM, VMEM],
            scratch_shapes=[
                pltpu.VMEM((total_queue, feat), bf16),
                pltpu.VMEM((8, width), f32),
                pltpu.SemaphoreType.DMA((2 * len(unit_list),)),
            ],
            compiler_params=limit(20),
        )(place, fill_count, columns, *unit_list)

        vectors = [pltpu.VMEM((8, total_rows), bf16), pltpu.VMEM((8, width), f32)]
        first_parts = all_sum_parts(sums)
        sums = pl.pallas_call(
            functools.partial(sweep_kernel, total_batch),
            name="sweep",
            out_shape=jax.ShapeDtypeStruct((1, total_rows), f32),
            in_specs=[SMEM] + [VMEM] * (1 + z_count),
            out_specs=VMEM,
            scratch_shapes=vectors,
            compiler_params=limit(8),
        )(fill_count, mass, *first_parts)
        side = functools.reduce(jnp.add, [part[:, total_rows:] for part in first_parts])
        soft_total, bound = side[:, :total_batch], side[0, total_batch]

        code_sums, column = pl.pallas_call(
            functools.partial(last_kernel, total_batch),
            name="last_sweep",
            out_shape=[
                jax.ShapeDtypeStruct((1, total_batch), f32),
                jax.ShapeDtypeStruct((1, width), f32),
            ],
            in_specs=[SMEM] + [VMEM] * (1 + z_count),
            out_specs=[VMEM, VMEM],
            scratch_shapes=vectors,
            compiler_params=limit(8),
        )(fill_count, mass, *all_sum_parts(sums))

        normed_part, grad_columns, loss = pl.pallas_call(
            functools.partial(slope_kernel, CROPS),
            name="slopes",
            out_shape=[
                jax.ShapeDtypeStruct((total_batch, feat), f32),
                jax.ShapeDtypeStruct((feat, width), f32),
                jax.ShapeDtypeStruct((8, 128), f32),
            ],
            in_specs=[VMEM] * (4 + z_count),
            out_specs=[VMEM] * 3,
            compiler_params=limit(24),
        )(batch, columns, column, *all_sum_parts(code_sums), soft_total)

        grad_parts = lax.all_to_all(grad_columns.astype(f16), "row", split_axis=0, concat_axis=1, tiled=True)
        grad_proto = grad_parts.astype(f32)

        scale = 32768.0 / (20.0 * bound + 1e-30)
        back = 1.0 / scale
        size = half // x_count
        pieces = normed_part.reshape(z_count, y_count, 2, x_count, size, feat)

        def pick(values, index, axis):
            return lax.dynamic_index_in_dim(values, index, axis, keepdims=False)

        away = shift_proto((pick(pieces, 1 - core, 2) * scale).astype(f16), 1)
        kept = pick(pieces, core, 2) + away.astype(f32) * back
        total = None
        for dy in range(y_count):
            for dx in range(x_count):
                part = pick(pick(kept, x ^ dx, 2), y ^ dy, 1)
                if dx or dy:
                    part = shift_xy((part * scale).astype(f16), dx, dy * 1).astype(f32) * back
                total = part if total is None else total + part
        piece = pick(total, z, 0)
        for dz in range(1, z_count):
            moved = shift_row((pick(total, z ^ dz, 0) * scale).astype(f16), dz, 0)
            piece = piece + moved.astype(f32) * back
        gathered = [piece] + [shift_proto(piece, k) for k in range(1, proto_count)]
        grad_embed = pl.pallas_call(
            functools.partial(finish_kernel, proto_count),
            name="finish",
            out_shape=jax.ShapeDtypeStruct((batch_rows, feat), f32),
            in_specs=[SMEM] + [VMEM] * (2 + proto_count),
            out_specs=VMEM,
            scratch_shapes=[pltpu.VMEM((batch_rows, feat), f32)],
            compiler_params=limit(8),
        )(proto.reshape(1).astype(jnp.int32), embeddings, order, *gathered)

        loss_parts = all_sum_parts(jnp.sum(loss).reshape(1))
        loss = functools.reduce(jnp.add, loss_parts) / total_batch
        return grad_embed, grad_proto, loss

    placed = (P("row", None), P("row", None), P("row", "proto"), P("row"), P())
    return jax.shard_map(
        body,
        mesh=mesh,
        in_specs=placed,
        out_specs=(P("row", None), P("row", "proto"), P()),
        check_vma=False,
    )
```

time: 520 us -> 255 us (0.49)
  blocking collectives: 217 us -> 0 us
  matrix products: 112 us -> 0 us
  Pallas kernels: 0 us -> 61.3 us
  starting transfers between devices: 12.3 us -> 71 us
  waiting for transfers between devices: 118 us -> 77.1 us
  other arithmetic: 34.2 us -> 3.89 us
  local copies, waits for them, and re-layouts: 8.53 us -> 32.8 us
  between operations: 16.5 us -> 8.62 us
    psum x4 -> x0, blocking collectives: 160 us -> none  [the longest x2 79.9 us: body(): lax.psum(lax.map(row_block_sums, row_blocks).reshape(total_rows), ('row',...]
    dot_general x20 -> x0, matrix products: 112 us -> none  [the longest x9 42.2 us: column_block(): jnp.dot(row_block, columns, preferred_element_type=jnp.float32)]
    reduce_scatter x1 -> x0, waiting for transfers between devices: 87 us -> none  [body(): lax.psum_scatter(normed_parts.reshape(total_batch, feat_dim), 'row', scat...]
    ppermute x0 -> x53, waiting for transfers between devices: none -> 77.1 us  [the longest x26 56.4 us: shift_row(): lax.ppermute(values, 'row', [(i, i ^ offset) for i in range(row_count)])]
    pallas_call x0 -> x6, Pallas kernels: none -> 61.3 us  [the longest x1 25.4 us: body(): pl.pallas_call(functools.partial(make_kernel, row_count, half, queue_half...]
    ppermute x0 -> x53, starting transfers between devices: none -> 59.4 us  [the longest x26 44.5 us: shift_row(): lax.ppermute(values, 'row', [(i, i ^ offset) for i in range(row_count)])]
    all_gather x1 -> x0, blocking collectives: 57.5 us -> none  [body(): lax.all_gather(membership, 'row', axis=0, tiled=True)]
    all_gather x2 -> x0, waiting for transfers between devices: 30.6 us -> none  [the longest x1 30.6 us: body(): lax.all_gather(queue_normed, 'row', axis=0, tiled=True)]
  transfers between devices with their start and end apart: 6 -> 55, of which waited for: 2 -> 27; matrix products, arithmetic and copies ran while one was open for 3% -> 1% of each run, Pallas kernels for 0% -> 1%
where the time goes in v1:
time: 255 us
  waiting for transfers between devices  77.1 us (30%)
  starting transfers between devices  71 us (28%)
  Pallas kernels  61.3 us (24%)
  local copies, waits for them, and re-layouts  32.8 us (13%)
  between operations  8.62 us (3%)
  other arithmetic  3.89 us (2%)
    ppermute x26, waiting for transfers between devices, shift_row(): lax.ppermute(values, 'row', [(i, i ^ offset) for i in range(row_count)])  56.4 us
    ppermute x26, starting transfers between devices, shift_row(): lax.ppermute(values, 'row', [(i, i ^ offset) for i in range(row_count)])  44.5 us
    unnamed x42, local copies, waits for them, and re-layouts  27.4 us
    pallas_call x1, Pallas kernels, body(): pl.pallas_call(functools.partial(make_kernel, row_count, half, queue_half...  25.4 us
    pallas_call x1, Pallas kernels, body(): pl.pallas_call(functools.partial(slope_kernel, CROPS), name='slopes', out...  15.9 us
    pallas_call x1, Pallas kernels, body(): pl.pallas_call(functools.partial(sweep_kernel, total_batch), name='sweep'...  11.4 us
    ppermute x24, starting transfers between devices, shift_proto(): lax.ppermute(values, 'proto', [(i, i ^ offset) for i in range(proto_count)])  11.4 us
    ppermute x3, waiting for transfers between devices, shift_xy(): return lax.ppermute(values, ('row', 'proto'), pairs)  11.2 us
  transfers between devices with their start and end apart: 55, of which 27 were waited for; matrix products, arithmetic and copies ran while one was open for 1% of the time, Pallas kernels for 1%

profile of v1, /device:TPU:0, one launch (start us, length us, event | category | flops | bytes accessed | tf_op | source)
XLA Modules:
  0.0 254.7 jit_solution(9050540725908249509)
XLA Ops:
  0.7 2.4 copy.24
  3.0 7.3 %all-to-all-start = ((bf16[32,8,2048]{2,0,1:T(8,128)(2,1)}), bf16[32,8,2048]{2,0,1:T(8,128)(2,1)S(1)}, u32[]{:S(2)}, u32[]{:S(2)}) async-start(bf16[32,8,2048]{2,0,1:T(8,128)(2,1)} %bitcast.47), calls=%async_computation | async-start | bytes 2097152 | tf_op jit(solution)/shard_map/all_to_all | solution.py:326
  11.9 2.0 collective-permute-start.1
  14.0 1.5 collective-permute-start.3
  15.4 2.4 collective-permute-start.7
  18.4 6.6 %collective-permute-done.1.refs_2_ = bf16[384,256]{1,0:T(8,128)(2,1)S(1)} collective-permute-done((bf16[384,256]{1,0:T(8,128)(2,1)S(1)}, bf16[384,256]{1,0:T(8,128)(2,1)S(1)}, u32[]{:S(2)}, u32[]{:S(2)}) %collective-permute-start.1) | collective-permute-done | bytes 196640 | tf_op jit(solution)/shard_map/ppermute | solution.py:281
  24.9 7.8 %collective-permute-done.3.refs_4_ = bf16[384,256]{1,0:T(8,128)(2,1)S(1)} collective-permute-done((bf16[384,256]{1,0:T(8,128)(2,1)S(1)}, bf16[384,256]{1,0:T(8,128)(2,1)S(1)}, u32[]{:S(2)}, u32[]{:S(2)}) %collective-permute-start.3) | collective-permute-done | bytes 196640 | tf_op jit(solution)/shard_map/ppermute | solution.py:281
  32.7 2.0 collective-permute-start.5
  34.8 15.3 %collective-permute-done.7.refs_8_ = bf16[384,256]{1,0:T(8,128)(2,1)S(1)} collective-permute-done((bf16[384,256]{1,0:T(8,128)(2,1)S(1)}, bf16[384,256]{1,0:T(8,128)(2,1)S(1)}, u32[]{:S(2)}, u32[]{:S(2)}) %collective-permute-start.7) | collective-permute-done | bytes 196640 | tf_op jit(solution)/shard_map/ppermute | solution.py:281
  50.1 1.1 collective-permute-start.9
  52.7 3.6 %collective-permute-done.9.refs_10_ = bf16[384,256]{1,0:T(8,128)(2,1)S(1)} collective-permute-done((bf16[384,256]{1,0:T(8,128)(2,1)S(1)}, bf16[384,256]{1,0:T(8,128)(2,1)S(1)}, u32[]{:S(2)}, u32[]{:S(2)}) %collective-permute-start.9) | collective-permute-done | bytes 196640 | tf_op jit(solution)/shard_map/ppermute | solution.py:281
  56.4 2.1 collective-permute-done.13.refs_14_
  67.2 25.4 %make_mass.1 = (bf16[6144,2048]{1,0:T(8,128)(2,1)S(1)}, f32[1,8320]{1,0:T(1,128)S(1)}, bf16[2048,256]{1,0:T(8,128)(2,1)S(1)}) custom-call(s32[2]{0:T(128)S(1)} %pad_add_fusion.place_ref, s32[1]{0:T(128)S(6)} %copy.25.fill_ref, bf16[256,2048]{1,0:T(8,128)(2,1)S(1)} %bitcast.48, bf16[384,256]{1,0:T(8,128)(2,1)S(1)} %get-tuple-element.14.refs_0_, ...), custom_call_target="tpu_custom_call" | custom-call | tf_op jit(solution)/shard_map/make_mass/pallas_call | solution.py:341
  92.5 8.3 %copy-done = bf16[6144,2048]{1,0:T(8,128)(2,1)} copy-done((bf16[6144,2048]{1,0:T(8,128)(2,1)}, bf16[6144,2048]{1,0:T(8,128)(2,1)S(1)}, u32[]{:S(2)}) %copy-start) | copy-done | bytes 25165848
  101.8 1.6 collective-permute-start.17
  104.0 1.2 collective-permute-done.17
  105.2 2.2 collective-permute-done.16
  107.4 1.8 collective-permute-start.18
  109.2 2.2 collective-permute-done.18
  112.2 2.3 collective-permute-start.20
  114.5 1.4 collective-permute-start.21
  115.9 1.2 collective-permute-done.20.refs_2_
  117.1 3.1 %collective-permute-done.21.refs_3_ = f32[1,8320]{1,0:T(1,128)S(1)} collective-permute-done((f32[1,8320]{1,0:T(1,128)S(1)}, f32[1,8320]{1,0:T(1,128)S(1)}, u32[]{:S(2)}, u32[]{:S(2)}) %collective-permute-start.21) | collective-permute-done | bytes 33312 | tf_op jit(solution)/shard_map/ppermute | solution.py:281
  120.2 8.2 %copy-done.1 = bf16[6144,2048]{1,0:T(8,128)(2,1)S(1)} copy-done((bf16[6144,2048]{1,0:T(8,128)(2,1)S(1)}, bf16[6144,2048]{1,0:T(8,128)(2,1)}, u32[]{:S(2)}) %copy-start.1) | copy-done | bytes 25165848
  128.4 11.4 %sweep.1 = f32[1,6144]{1,0:T(1,128)S(1)} custom-call(s32[1]{0:T(128)S(6)} %copy.25.fill_ref, bf16[6144,2048]{1,0:T(8,128)(2,1)S(1)} %copy-done.1, f32[1,8320]{1,0:T(1,128)S(1)} %add.163.refs_0_, f32[1,8320]{1,0:T(1,128)S(1)} %collective-permute-done.19.refs_1_, f32[1,8320]{1,0:T(1,128)S(1)} %collective-permute-done.20.refs_2_, ...), custom_call_target="tpu_custom_call" | custom-call | tf_op jit(solution)/shard_map/sweep/pallas_call | solution.py:361
  140.4 1.3 collective-permute-start.22
  141.7 1.4 collective-permute-done.24
  143.8 1.8 collective-permute-start.25
  145.6 2.1 collective-permute-done.25
  147.8 2.0 collective-permute-start.27
  149.7 2.4 collective-permute-start.28
  152.6 2.8 %collective-permute-done.28.refs_3_ = f32[1,6144]{1,0:T(1,128)S(1)} collective-permute-done((f32[1,6144]{1,0:T(1,128)S(1)}, f32[1,6144]{1,0:T(1,128)S(1)}, u32[]{:S(2)}, u32[]{:S(2)}) %collective-permute-start.28) | collective-permute-done | bytes 24608 | tf_op jit(solution)/shard_map/ppermute | solution.py:281
  155.4 6.7 %last_sweep.1 = (f32[1,2048]{1,0:T(1,128)S(1)}, f32[1,2048]{1,0:T(1,128)S(1)}) custom-call(s32[1]{0:T(128)S(6)} %copy.25.fill_ref, bf16[6144,2048]{1,0:T(8,128)(2,1)S(1)} %copy-done.2, f32[1,6144]{1,0:T(1,128)S(1)} %add.167.refs_0_, f32[1,6144]{1,0:T(1,128)S(1)} %collective-permute-done.26.refs_1_, f32[1,6144]{1,0:T(1,128)S(1)} %collective-permute-done.27.refs_2_, ...), custom_call_target="tpu_custom_call" | custom-call | tf_op jit(solution)/shard_map/last_sweep/pallas_call | solution.py:373
  162.7 1.2 collective-permute-start.29
  163.9 1.2 collective-permute-done.31
  165.8 1.8 collective-permute-start.32
  167.6 1.9 collective-permute-done.32
  169.6 3.0 %collective-permute-start.34 = (f32[1,2048]{1,0:T(1,128)S(1)}, f32[1,2048]{1,0:T(1,128)S(1)}, u32[]{:S(2)}, u32[]{:S(2)}) collective-permute-start(f32[1,2048]{1,0:T(1,128)S(1)} %add.171.refs_0_), channel_id=1, source_target_pairs={{0,16},{4,20},{8,24},{12,28},{16,0},{20,4},{24,8},{28,12},{1,17},{... | collective-permute-start | bytes 24584 | tf_op jit(solution)/shard_map/ppermute | solution.py:281
  172.6 1.4 collective-permute-start.35
  175.3 2.8 %collective-permute-done.35.refs_3_ = f32[1,2048]{1,0:T(1,128)S(1)} collective-permute-done((f32[1,2048]{1,0:T(1,128)S(1)}, f32[1,2048]{1,0:T(1,128)S(1)}, u32[]{:S(2)}, u32[]{:S(2)}) %collective-permute-start.35) | collective-permute-done | bytes 8224 | tf_op jit(solution)/shard_map/ppermute | solution.py:281
  178.1 1.2 copy-done.4
  179.3 15.9 %slopes.1 = (f32[2048,256]{1,0:T(8,128)S(1)}, f32[256,2048]{1,0:T(8,128)S(1)}, f32[8,128]{1,0:T(8,128)S(1)}) custom-call(bf16[2048,256]{1,0:T(8,128)(2,1)S(1)} %copy-done.4, bf16[256,2048]{1,0:T(8,128)(2,1)S(1)} %bitcast.49, f32[1,2048]{1,0:T(1,128)S(1)} %get-tuple-element.18.column_ref, f32[1,2048]{1,0:T(1,128)S(1)} %add.171.refs_0_, ...), custom_call_target="tpu_custom_call" | custom-call | tf_op jit(solution)/shard_map/slopes/pallas_call | solution.py:386
  195.1 1.1 convert_element_type.96
  196.3 4.3 %all-to-all-start.1 = ((f16[8,32,2048]{2,1,0:T(8,128)(2,1)}), f16[8,32,2048]{2,1,0:T(8,128)(2,1)}, u32[]{:S(2)}, u32[]{:S(2)}) async-start(f16[8,32,2048]{2,1,0:T(8,128)(2,1)} %bitcast.19), calls=%async_computation.1 | async-start | bytes 2097152 | tf_op jit(solution)/shard_map/all_to_all | solution.py:399
  200.5 1.1 constant_dynamic-slice_fusion
  201.9 1.8 collective-permute-done.36
  204.0 2.0 collective-permute-start.39
  206.1 1.5 collective-permute-start.37
  207.6 5.8 %collective-permute-done.39 = f16[4,64,256]{2,1,0:T(8,128)(2,1)S(1)} collective-permute-done((f16[4,64,256]{2,1,0:T(8,128)(2,1)S(1)}, f16[4,64,256]{2,1,0:T(8,128)(2,1)S(1)}, u32[]{:S(2)}, u32[]{:S(2)}) %collective-permute-start.39) | collective-permute-done | bytes 131104 | tf_op jit(solution)/shard_map/ppermute | solution.py:291
  213.4 5.4 %collective-permute-done.38 = f16[4,64,256]{2,1,0:T(8,128)(2,1)S(1)} collective-permute-done((f16[4,64,256]{2,1,0:T(8,128)(2,1)S(1)}, f16[4,64,256]{2,1,0:T(8,128)(2,1)S(1)}, u32[]{:S(2)}, u32[]{:S(2)}) %collective-permute-start.38) | collective-permute-done | bytes 131104 | tf_op jit(solution)/shard_map/ppermute | solution.py:291
  218.9 2.6 %collective-permute-start.42 = (f16[64,256]{1,0:T(8,128)(2,1)S(1)}, f16[64,256]{1,0:T(8,128)(2,1)S(1)}, u32[]{:S(2)}, u32[]{:S(2)}) collective-permute-start(f16[64,256]{1,0:T(8,128)(2,1)S(1)} %get-tuple-element.29), channel_id=1, source_target_pairs={{0,24},{4,28},{8,16},{12,20},{16,8},{20,12},{24,0},{28,4},{1,25},{... | collective-permute-start | bytes 98312 | tf_op jit(solution)/shard_map/ppermute | solution.py:281
  221.5 1.8 collective-permute-start.40
  223.4 1.4 collective-permute-done.42
  224.8 1.5 collective-permute-done.41
  226.4 1.8 collective-permute-start.44
  229.2 1.7 collective-permute-start.47
  234.7 2.5 collective-permute-start.49
  237.2 1.1 collective-permute-done.49
  238.9 1.9 collective-permute-start.50
  240.8 2.8 %collective-permute-start.51 = (f32[1]{0:T(128)}, f32[1]{0:T(128)}, u32[]{:S(2)}, u32[]{:S(2)}) collective-permute-start(f32[1]{0:T(128)} %add.197), channel_id=1, source_target_pairs={{0,16},{4,20},{8,24},{12,28},{16,0},{20,4},{24,8},{28,12},{1,17},{... | collective-permute-start | bytes 20 | tf_op jit(solution)/shard_map/ppermute | solution.py:281
  243.6 3.6 %collective-permute-start.52 = (f32[1]{0:T(128)}, f32[1]{0:T(128)}, u32[]{:S(2)}, u32[]{:S(2)}) collective-permute-start(f32[1]{0:T(128)} %add.197), channel_id=1, source_target_pairs={{0,24},{4,28},{8,16},{12,20},{16,8},{20,12},{24,0},{28,4},{1,25},{... | collective-permute-start | bytes 20 | tf_op jit(solution)/shard_map/ppermute | solution.py:281
  249.6 1.1 finish.1
  250.7 1.4 convert_bitcast_fusion
  252.1 1.5 copy.16
  (116 shorter events, 21.4 us)
Async XLA Ops:
  0.6 9.7 %copy-start.5 = (bf16[256,256]{1,0:T(8,128)(2,1)S(1)}, bf16[256,256]{1,0:T(8,128)(2,1)}, u32[]{:S(2)}) copy-start(bf16[256,256]{1,0:T(8,128)(2,1)} %embed_ref.3) | copy-start | bytes 393220
  0.6 9.7 %copy-start.6 = (bf16[512,256]{1,0:T(8,128)(2,1)S(1)}, bf16[512,256]{1,0:T(8,128)(2,1)}, u32[]{:S(2)}) copy-start(bf16[512,256]{1,0:T(8,128)(2,1)} %queue_ref.1) | copy-start | bytes 786436
  0.7 9.7 %copy-start.19 = (s32[256]{0:T(256)S(1)}, s32[256]{0:T(256)}, u32[]{:S(2)}) copy-start(s32[256]{0:T(256)} %param.8) | copy-start | bytes 3076
  3.0 59.5 %all-to-all-start = ((bf16[32,8,2048]{2,0,1:T(8,128)(2,1)}), bf16[32,8,2048]{2,0,1:T(8,128)(2,1)S(1)}, u32[]{:S(2)}, u32[]{:S(2)}) async-start(bf16[32,8,2048]{2,0,1:T(8,128)(2,1)} %bitcast.47), calls=%async_computation | async-start | bytes 2097152 | tf_op jit(solution)/shard_map/all_to_all | solution.py:326
  11.9 13.0 %collective-permute-start.1 = (bf16[384,256]{1,0:T(8,128)(2,1)S(1)}, bf16[384,256]{1,0:T(8,128)(2,1)S(1)}, u32[]{:S(2)}, u32[]{:S(2)}) collective-permute-start(bf16[384,256]{1,0:T(8,128)(2,1)S(1)} %get-tuple-element.14.refs_0_), channel_id=1, source_target_pairs={{0,4},{4,0},{8,12},{12,8},{16,20},{20,16},{24,28},{28,24},{1,5},{5... | collective-permute-start | bytes 589832 | tf_op jit(solution)/shard_map/ppermute | solution.py:281
  14.0 18.8 %collective-permute-start.3 = (bf16[384,256]{1,0:T(8,128)(2,1)S(1)}, bf16[384,256]{1,0:T(8,128)(2,1)S(1)}, u32[]{:S(2)}, u32[]{:S(2)}) collective-permute-start(bf16[384,256]{1,0:T(8,128)(2,1)S(1)} %get-tuple-element.14.refs_0_), channel_id=1, source_target_pairs={{0,8},{4,12},{8,0},{12,4},{16,24},{20,28},{24,16},{28,20},{1,9},{5... | collective-permute-start | bytes 589832 | tf_op jit(solution)/shard_map/ppermute | solution.py:281
  15.4 17.3 %collective-permute-start = (bf16[384,256]{1,0:T(8,128)(2,1)S(1)}, bf16[384,256]{1,0:T(8,128)(2,1)S(1)}, u32[]{:S(2)}, u32[]{:S(2)}) collective-permute-start(bf16[384,256]{1,0:T(8,128)(2,1)S(1)} %get-tuple-element.14.refs_0_), channel_id=1, source_target_pairs={{0,1},{1,0},{2,3},{3,2},{4,5},{5,4},{6,7},{7,6},{8,9},{9,8},{10,11... | collective-permute-start | bytes 589832 | tf_op jit(solution)/shard_map/ppermute | solution.py:284
  15.4 34.7 %collective-permute-start.7 = (bf16[384,256]{1,0:T(8,128)(2,1)S(1)}, bf16[384,256]{1,0:T(8,128)(2,1)S(1)}, u32[]{:S(2)}, u32[]{:S(2)}) collective-permute-start(bf16[384,256]{1,0:T(8,128)(2,1)S(1)} %get-tuple-element.14.refs_0_), channel_id=1, source_target_pairs={{0,16},{4,20},{8,24},{12,28},{16,0},{20,4},{24,8},{28,12},{1,17},{... | collective-permute-start | bytes 589832 | tf_op jit(solution)/shard_map/ppermute | solution.py:281
  17.8 33.4 %collective-permute-start.11 = (bf16[384,256]{1,0:T(8,128)(2,1)S(1)}, bf16[384,256]{1,0:T(8,128)(2,1)S(1)}, u32[]{:S(2)}, u32[]{:S(2)}) collective-permute-start(bf16[384,256]{1,0:T(8,128)(2,1)S(1)} %get-tuple-element.14.refs_0_), channel_id=1, source_target_pairs={{0,24},{4,28},{8,16},{12,20},{16,8},{20,12},{24,0},{28,4},{1,25},{... | collective-permute-start | bytes 589832 | tf_op jit(solution)/shard_map/ppermute | solution.py:281
  24.9 27.2 %collective-permute-start.2 = (bf16[384,256]{1,0:T(8,128)(2,1)S(1)}, bf16[384,256]{1,0:T(8,128)(2,1)S(1)}, u32[]{:S(2)}, u32[]{:S(2)}) collective-permute-start(bf16[384,256]{1,0:T(8,128)(2,1)S(1)} %collective-permute-done.1.refs_2_), channel_id=1, source_target_pairs={{0,1},{1,0},{2,3},{3,2},{4,5},{5,4},{6,7},{7,6},{8,9},{9,8},{10,11... | collective-permute-start | bytes 589832 | tf_op jit(solution)/shard_map/ppermute | solution.py:284
  32.7 19.4 %collective-permute-start.4 = (bf16[384,256]{1,0:T(8,128)(2,1)S(1)}, bf16[384,256]{1,0:T(8,128)(2,1)S(1)}, u32[]{:S(2)}, u32[]{:S(2)}) collective-permute-start(bf16[384,256]{1,0:T(8,128)(2,1)S(1)} %collective-permute-done.3.refs_4_), channel_id=1, source_target_pairs={{0,1},{1,0},{2,3},{3,2},{4,5},{5,4},{6,7},{7,6},{8,9},{9,8},{10,11... | collective-permute-start | bytes 589832 | tf_op jit(solution)/shard_map/ppermute | solution.py:284
  32.7 19.9 %collective-permute-start.5 = (bf16[384,256]{1,0:T(8,128)(2,1)S(1)}, bf16[384,256]{1,0:T(8,128)(2,1)S(1)}, u32[]{:S(2)}, u32[]{:S(2)}) collective-permute-start(bf16[384,256]{1,0:T(8,128)(2,1)S(1)} %collective-permute-done.3.refs_4_), channel_id=1, source_target_pairs={{0,4},{4,0},{8,12},{12,8},{16,20},{20,16},{24,28},{28,24},{1,5},{5... | collective-permute-start | bytes 589832 | tf_op jit(solution)/shard_map/ppermute | solution.py:281
  50.1 6.2 %collective-permute-start.9 = (bf16[384,256]{1,0:T(8,128)(2,1)S(1)}, bf16[384,256]{1,0:T(8,128)(2,1)S(1)}, u32[]{:S(2)}, u32[]{:S(2)}) collective-permute-start(bf16[384,256]{1,0:T(8,128)(2,1)S(1)} %collective-permute-done.7.refs_8_), channel_id=1, source_target_pairs={{0,4},{4,0},{8,12},{12,8},{16,20},{20,16},{24,28},{28,24},{1,5},{5... | collective-permute-start | bytes 589832 | tf_op jit(solution)/shard_map/ppermute | solution.py:281
  51.2 7.3 %collective-permute-start.13 = (bf16[384,256]{1,0:T(8,128)(2,1)S(1)}, bf16[384,256]{1,0:T(8,128)(2,1)S(1)}, u32[]{:S(2)}, u32[]{:S(2)}) collective-permute-start(bf16[384,256]{1,0:T(8,128)(2,1)S(1)} %collective-permute-done.11.refs_12_), channel_id=1, source_target_pairs={{0,4},{4,0},{8,12},{12,8},{16,20},{20,16},{24,28},{28,24},{1,5},{5... | collective-permute-start | bytes 589832 | tf_op jit(solution)/shard_map/ppermute | solution.py:281
  52.2 7.0 %collective-permute-start.8 = (bf16[384,256]{1,0:T(8,128)(2,1)S(1)}, bf16[384,256]{1,0:T(8,128)(2,1)S(1)}, u32[]{:S(2)}, u32[]{:S(2)}) collective-permute-start(bf16[384,256]{1,0:T(8,128)(2,1)S(1)} %collective-permute-done.7.refs_8_), channel_id=1, source_target_pairs={{0,1},{1,0},{2,3},{3,2},{4,5},{5,4},{6,7},{7,6},{8,9},{9,8},{10,11... | collective-permute-start | bytes 589832 | tf_op jit(solution)/shard_map/ppermute | solution.py:284
  52.2 7.6 %collective-permute-start.12 = (bf16[384,256]{1,0:T(8,128)(2,1)S(1)}, bf16[384,256]{1,0:T(8,128)(2,1)S(1)}, u32[]{:S(2)}, u32[]{:S(2)}) collective-permute-start(bf16[384,256]{1,0:T(8,128)(2,1)S(1)} %collective-permute-done.11.refs_12_), channel_id=1, source_target_pairs={{0,1},{1,0},{2,3},{3,2},{4,5},{5,4},{6,7},{7,6},{8,9},{9,8},{10,11... | collective-permute-start | bytes 589832 | tf_op jit(solution)/shard_map/ppermute | solution.py:284
  52.7 7.8 %collective-permute-start.6 = (bf16[384,256]{1,0:T(8,128)(2,1)S(1)}, bf16[384,256]{1,0:T(8,128)(2,1)S(1)}, u32[]{:S(2)}, u32[]{:S(2)}) collective-permute-start(bf16[384,256]{1,0:T(8,128)(2,1)S(1)} %collective-permute-done.5.refs_6_), channel_id=1, source_target_pairs={{0,1},{1,0},{2,3},{3,2},{4,5},{5,4},{6,7},{7,6},{8,9},{9,8},{10,11... | collective-permute-start | bytes 589832 | tf_op jit(solution)/shard_map/ppermute | solution.py:284
  56.3 4.8 %collective-permute-start.10 = (bf16[384,256]{1,0:T(8,128)(2,1)S(1)}, bf16[384,256]{1,0:T(8,128)(2,1)S(1)}, u32[]{:S(2)}, u32[]{:S(2)}) collective-permute-start(bf16[384,256]{1,0:T(8,128)(2,1)S(1)} %collective-permute-done.9.refs_10_), channel_id=1, source_target_pairs={{0,1},{1,0},{2,3},{3,2},{4,5},{5,4},{6,7},{7,6},{8,9},{9,8},{10,11... | collective-permute-start | bytes 589832 | tf_op jit(solution)/shard_map/ppermute | solution.py:284
  58.5 3.4 %collective-permute-start.14 = (bf16[384,256]{1,0:T(8,128)(2,1)S(1)}, bf16[384,256]{1,0:T(8,128)(2,1)S(1)}, u32[]{:S(2)}, u32[]{:S(2)}) collective-permute-start(bf16[384,256]{1,0:T(8,128)(2,1)S(1)} %collective-permute-done.13.refs_14_), channel_id=1, source_target_pairs={{0,1},{1,0},{2,3},{3,2},{4,5},{5,4},{6,7},{7,6},{8,9},{9,8},{10,11... | collective-permute-start | bytes 589832 | tf_op jit(solution)/shard_map/ppermute | solution.py:284
  92.5 8.3 %copy-start = (bf16[6144,2048]{1,0:T(8,128)(2,1)}, bf16[6144,2048]{1,0:T(8,128)(2,1)S(1)}, u32[]{:S(2)}) copy-start(bf16[6144,2048]{1,0:T(8,128)(2,1)S(1)} %get-tuple-element.16.mass_ref) | copy-start | bytes 75497472
  101.8 3.3 %collective-permute-start.17 = (f32[1,8320]{1,0:T(1,128)S(1)}, f32[1,8320]{1,0:T(1,128)S(1)}, u32[]{:S(2)}, u32[]{:S(2)}) collective-permute-start(f32[1,8320]{1,0:T(1,128)S(1)} %get-tuple-element.17), channel_id=1, source_target_pairs={{0,3},{1,2},{2,1},{3,0},{4,7},{5,6},{6,5},{7,4},{8,11},{9,10},{10,... | collective-permute-start | bytes 99848 | tf_op jit(solution)/shard_map/ppermute | solution.py:284
  103.5 3.9 %collective-permute-start.16 = (f32[1,8320]{1,0:T(1,128)S(1)}, f32[1,8320]{1,0:T(1,128)S(1)}, u32[]{:S(2)}, u32[]{:S(2)}) collective-permute-start(f32[1,8320]{1,0:T(1,128)S(1)} %get-tuple-element.17), channel_id=1, source_target_pairs={{0,2},{1,3},{2,0},{3,1},{4,6},{5,7},{6,4},{7,5},{8,10},{9,11},{10,... | collective-permute-start | bytes 99848 | tf_op jit(solution)/shard_map/ppermute | solution.py:284
  104.0 3.4 %collective-permute-start.15 = (f32[1,8320]{1,0:T(1,128)S(1)}, f32[1,8320]{1,0:T(1,128)S(1)}, u32[]{:S(2)}, u32[]{:S(2)}) collective-permute-start(f32[1,8320]{1,0:T(1,128)S(1)} %get-tuple-element.17), channel_id=1, source_target_pairs={{0,1},{1,0},{2,3},{3,2},{4,5},{5,4},{6,7},{7,6},{8,9},{9,8},{10,11... | collective-permute-start | bytes 99848 | tf_op jit(solution)/shard_map/ppermute | solution.py:284
  107.4 4.0 %collective-permute-start.18 = (f32[1,8320]{1,0:T(1,128)S(1)}, f32[1,8320]{1,0:T(1,128)S(1)}, u32[]{:S(2)}, u32[]{:S(2)}) collective-permute-start(f32[1,8320]{1,0:T(1,128)S(1)} %add_add_fusion), channel_id=1, source_target_pairs={{0,4},{4,0},{8,12},{12,8},{16,20},{20,16},{24,28},{28,24},{1,5},{5... | collective-permute-start | bytes 99848 | tf_op jit(solution)/shard_map/ppermute | solution.py:281
  111.5 4.5 %collective-permute-start.19 = (f32[1,8320]{1,0:T(1,128)S(1)}, f32[1,8320]{1,0:T(1,128)S(1)}, u32[]{:S(2)}, u32[]{:S(2)}) collective-permute-start(f32[1,8320]{1,0:T(1,128)S(1)} %add.163.refs_0_), channel_id=1, source_target_pairs={{0,8},{4,12},{8,0},{12,4},{16,24},{20,28},{24,16},{28,20},{1,9},{5... | collective-permute-start | bytes 99848 | tf_op jit(solution)/shard_map/ppermute | solution.py:281
  112.2 4.9 %collective-permute-start.20 = (f32[1,8320]{1,0:T(1,128)S(1)}, f32[1,8320]{1,0:T(1,128)S(1)}, u32[]{:S(2)}, u32[]{:S(2)}) collective-permute-start(f32[1,8320]{1,0:T(1,128)S(1)} %add.163.refs_0_), channel_id=1, source_target_pairs={{0,16},{4,20},{8,24},{12,28},{16,0},{20,4},{24,8},{28,12},{1,17},{... | collective-permute-start | bytes 99848 | tf_op jit(solution)/shard_map/ppermute | solution.py:281
  114.5 5.7 %collective-permute-start.21 = (f32[1,8320]{1,0:T(1,128)S(1)}, f32[1,8320]{1,0:T(1,128)S(1)}, u32[]{:S(2)}, u32[]{:S(2)}) collective-permute-start(f32[1,8320]{1,0:T(1,128)S(1)} %add.163.refs_0_), channel_id=1, source_target_pairs={{0,24},{4,28},{8,16},{12,20},{16,8},{20,12},{24,0},{28,4},{1,25},{... | collective-permute-start | bytes 99848 | tf_op jit(solution)/shard_map/ppermute | solution.py:281
  120.2 8.2 %copy-start.1 = (bf16[6144,2048]{1,0:T(8,128)(2,1)S(1)}, bf16[6144,2048]{1,0:T(8,128)(2,1)}, u32[]{:S(2)}) copy-start(bf16[6144,2048]{1,0:T(8,128)(2,1)} %copy-done) | copy-start | bytes 75497472
  128.4 27.0 %copy-start.2 = (bf16[6144,2048]{1,0:T(8,128)(2,1)S(1)}, bf16[6144,2048]{1,0:T(8,128)(2,1)}, u32[]{:S(2)}) copy-start(bf16[6144,2048]{1,0:T(8,128)(2,1)} %copy-done) | copy-start | bytes 75497472
  139.8 3.3 %collective-permute-start.24 = (f32[1,6144]{1,0:T(1,128)S(1)}, f32[1,6144]{1,0:T(1,128)S(1)}, u32[]{:S(2)}, u32[]{:S(2)}) collective-permute-start(f32[1,6144]{1,0:T(1,128)S(1)} %sweep.1), channel_id=1, source_target_pairs={{0,3},{1,2},{2,1},{3,0},{4,7},{5,6},{6,5},{7,4},{8,11},{9,10},{10,... | collective-permute-start | bytes 73736 | tf_op jit(solution)/shard_map/ppermute | solution.py:284
  139.8 3.9 %collective-permute-start.23 = (f32[1,6144]{1,0:T(1,128)S(1)}, f32[1,6144]{1,0:T(1,128)S(1)}, u32[]{:S(2)}, u32[]{:S(2)}) collective-permute-start(f32[1,6144]{1,0:T(1,128)S(1)} %sweep.1), channel_id=1, source_target_pairs={{0,2},{1,3},{2,0},{3,1},{4,6},{5,7},{6,4},{7,5},{8,10},{9,11},{10,... | collective-permute-start | bytes 73736 | tf_op jit(solution)/shard_map/ppermute | solution.py:284
  140.4 3.3 %collective-permute-start.22 = (f32[1,6144]{1,0:T(1,128)S(1)}, f32[1,6144]{1,0:T(1,128)S(1)}, u32[]{:S(2)}, u32[]{:S(2)}) collective-permute-start(f32[1,6144]{1,0:T(1,128)S(1)} %sweep.1), channel_id=1, source_target_pairs={{0,1},{1,0},{2,3},{3,2},{4,5},{5,4},{6,7},{7,6},{8,9},{9,8},{10,11... | collective-permute-start | bytes 73736 | tf_op jit(solution)/shard_map/ppermute | solution.py:284
  143.8 3.9 %collective-permute-start.25 = (f32[1,6144]{1,0:T(1,128)S(1)}, f32[1,6144]{1,0:T(1,128)S(1)}, u32[]{:S(2)}, u32[]{:S(2)}) collective-permute-start(f32[1,6144]{1,0:T(1,128)S(1)} %add_add_fusion.1), channel_id=1, source_target_pairs={{0,4},{4,0},{8,12},{12,8},{16,20},{20,16},{24,28},{28,24},{1,5},{5... | collective-permute-start | bytes 73736 | tf_op jit(solution)/shard_map/ppermute | solution.py:281
  147.7 4.5 %collective-permute-start.26 = (f32[1,6144]{1,0:T(1,128)S(1)}, f32[1,6144]{1,0:T(1,128)S(1)}, u32[]{:S(2)}, u32[]{:S(2)}) collective-permute-start(f32[1,6144]{1,0:T(1,128)S(1)} %add.167.refs_0_), channel_id=1, source_target_pairs={{0,8},{4,12},{8,0},{12,4},{16,24},{20,28},{24,16},{28,20},{1,9},{5... | collective-permute-start | bytes 73736 | tf_op jit(solution)/shard_map/ppermute | solution.py:281
  147.8 4.8 %collective-permute-start.27 = (f32[1,6144]{1,0:T(1,128)S(1)}, f32[1,6144]{1,0:T(1,128)S(1)}, u32[]{:S(2)}, u32[]{:S(2)}) collective-permute-start(f32[1,6144]{1,0:T(1,128)S(1)} %add.167.refs_0_), channel_id=1, source_target_pairs={{0,16},{4,20},{8,24},{12,28},{16,0},{20,4},{24,8},{28,12},{1,17},{... | collective-permute-start | bytes 73736 | tf_op jit(solution)/shard_map/ppermute | solution.py:281
  149.7 5.6 %collective-permute-start.28 = (f32[1,6144]{1,0:T(1,128)S(1)}, f32[1,6144]{1,0:T(1,128)S(1)}, u32[]{:S(2)}, u32[]{:S(2)}) collective-permute-start(f32[1,6144]{1,0:T(1,128)S(1)} %add.167.refs_0_), channel_id=1, source_target_pairs={{0,24},{4,28},{8,16},{12,20},{16,8},{20,12},{24,0},{28,4},{1,25},{... | collective-permute-start | bytes 73736 | tf_op jit(solution)/shard_map/ppermute | solution.py:281
  162.1 3.1 %collective-permute-start.31 = (f32[1,2048]{1,0:T(1,128)S(1)}, f32[1,2048]{1,0:T(1,128)S(1)}, u32[]{:S(2)}, u32[]{:S(2)}) collective-permute-start(f32[1,2048]{1,0:T(1,128)S(1)} %get-tuple-element.19), channel_id=1, source_target_pairs={{0,3},{1,2},{2,1},{3,0},{4,7},{5,6},{6,5},{7,4},{8,11},{9,10},{10,... | collective-permute-start | bytes 24584 | tf_op jit(solution)/shard_map/ppermute | solution.py:284
  162.1 3.7 %collective-permute-start.30 = (f32[1,2048]{1,0:T(1,128)S(1)}, f32[1,2048]{1,0:T(1,128)S(1)}, u32[]{:S(2)}, u32[]{:S(2)}) collective-permute-start(f32[1,2048]{1,0:T(1,128)S(1)} %get-tuple-element.19), channel_id=1, source_target_pairs={{0,2},{1,3},{2,0},{3,1},{4,6},{5,7},{6,4},{7,5},{8,10},{9,11},{10,... | collective-permute-start | bytes 24584 | tf_op jit(solution)/shard_map/ppermute | solution.py:284
  162.7 3.1 %collective-permute-start.29 = (f32[1,2048]{1,0:T(1,128)S(1)}, f32[1,2048]{1,0:T(1,128)S(1)}, u32[]{:S(2)}, u32[]{:S(2)}) collective-permute-start(f32[1,2048]{1,0:T(1,128)S(1)} %get-tuple-element.19), channel_id=1, source_target_pairs={{0,1},{1,0},{2,3},{3,2},{4,5},{5,4},{6,7},{7,6},{8,9},{9,8},{10,11... | collective-permute-start | bytes 24584 | tf_op jit(solution)/shard_map/ppermute | solution.py:284
  165.8 3.7 %collective-permute-start.32 = (f32[1,2048]{1,0:T(1,128)S(1)}, f32[1,2048]{1,0:T(1,128)S(1)}, u32[]{:S(2)}, u32[]{:S(2)}) collective-permute-start(f32[1,2048]{1,0:T(1,128)S(1)} %add_add_fusion.2), channel_id=1, source_target_pairs={{0,4},{4,0},{8,12},{12,8},{16,20},{20,16},{24,28},{28,24},{1,5},{5... | collective-permute-start | bytes 24584 | tf_op jit(solution)/shard_map/ppermute | solution.py:281
  169.6 5.7 %collective-permute-start.33 = (f32[1,2048]{1,0:T(1,128)S(1)}, f32[1,2048]{1,0:T(1,128)S(1)}, u32[]{:S(2)}, u32[]{:S(2)}) collective-permute-start(f32[1,2048]{1,0:T(1,128)S(1)} %add.171.refs_0_), channel_id=1, source_target_pairs={{0,8},{4,12},{8,0},{12,4},{16,24},{20,28},{24,16},{28,20},{1,9},{5... | collective-permute-start | bytes 24584 | tf_op jit(solution)/shard_map/ppermute | solution.py:281
  169.6 5.6 %collective-permute-start.34 = (f32[1,2048]{1,0:T(1,128)S(1)}, f32[1,2048]{1,0:T(1,128)S(1)}, u32[]{:S(2)}, u32[]{:S(2)}) collective-permute-start(f32[1,2048]{1,0:T(1,128)S(1)} %add.171.refs_0_), channel_id=1, source_target_pairs={{0,16},{4,20},{8,24},{12,28},{16,0},{20,4},{24,8},{28,12},{1,17},{... | collective-permute-start | bytes 24584 | tf_op jit(solution)/shard_map/ppermute | solution.py:281
  172.6 5.4 %collective-permute-start.35 = (f32[1,2048]{1,0:T(1,128)S(1)}, f32[1,2048]{1,0:T(1,128)S(1)}, u32[]{:S(2)}, u32[]{:S(2)}) collective-permute-start(f32[1,2048]{1,0:T(1,128)S(1)} %add.171.refs_0_), channel_id=1, source_target_pairs={{0,24},{4,28},{8,16},{12,20},{16,8},{20,12},{24,0},{28,4},{1,25},{... | collective-permute-start | bytes 24584 | tf_op jit(solution)/shard_map/ppermute | solution.py:281
  178.0 1.2 copy-start.4
  196.3 54.5 %all-to-all-start.1 = ((f16[8,32,2048]{2,1,0:T(8,128)(2,1)}), f16[8,32,2048]{2,1,0:T(8,128)(2,1)}, u32[]{:S(2)}, u32[]{:S(2)}) async-start(f16[8,32,2048]{2,1,0:T(8,128)(2,1)} %bitcast.19), calls=%async_computation.1 | async-start | bytes 2097152 | tf_op jit(solution)/shard_map/all_to_all | solution.py:399
  201.7 2.1 copy-start.20
  201.8 2.0 collective-permute-start.36
  203.8 45.8 %copy-start.18 = (bf16[256,256]{1,0:T(8,128)(2,1)S(1)}, bf16[256,256]{1,0:T(8,128)(2,1)}, u32[]{:S(2)}) copy-start(bf16[256,256]{1,0:T(8,128)(2,1)} %copy-done.17) | copy-start | bytes 393220
  204.0 9.4 %collective-permute-start.39 = (f16[4,64,256]{2,1,0:T(8,128)(2,1)S(1)}, f16[4,64,256]{2,1,0:T(8,128)(2,1)S(1)}, u32[]{:S(2)}, u32[]{:S(2)}) collective-permute-start(f16[4,64,256]{2,1,0:T(8,128)(2,1)S(1)} %get-tuple-element.26), channel_id=1, source_target_pairs={{0,6},{1,7},{2,4},{3,5},{4,2},{5,3},{6,0},{7,1},{8,14},{9,15},{10,... | collective-permute-start | bytes 393224 | tf_op jit(solution)/shard_map/ppermute | solution.py:291
  206.0 12.8 %collective-permute-start.38 = (f16[4,64,256]{2,1,0:T(8,128)(2,1)S(1)}, f16[4,64,256]{2,1,0:T(8,128)(2,1)S(1)}, u32[]{:S(2)}, u32[]{:S(2)}) collective-permute-start(f16[4,64,256]{2,1,0:T(8,128)(2,1)S(1)} %get-tuple-element.27), channel_id=1, source_target_pairs={{0,4},{1,5},{2,6},{3,7},{4,0},{5,1},{6,2},{7,3},{8,12},{9,13},{10,... | collective-permute-start | bytes 393224 | tf_op jit(solution)/shard_map/ppermute | solution.py:291
  206.1 12.6 %collective-permute-start.37 = (f16[4,64,256]{2,1,0:T(8,128)(2,1)S(1)}, f16[4,64,256]{2,1,0:T(8,128)(2,1)S(1)}, u32[]{:S(2)}, u32[]{:S(2)}) collective-permute-start(f16[4,64,256]{2,1,0:T(8,128)(2,1)S(1)} %get-tuple-element.25), channel_id=1, source_target_pairs={{0,2},{1,3},{2,0},{3,1},{4,6},{5,7},{6,4},{7,5},{8,10},{9,11},{10,... | collective-permute-start | bytes 393224 | tf_op jit(solution)/shard_map/ppermute | solution.py:291
  218.9 5.9 %collective-permute-start.42 = (f16[64,256]{1,0:T(8,128)(2,1)S(1)}, f16[64,256]{1,0:T(8,128)(2,1)S(1)}, u32[]{:S(2)}, u32[]{:S(2)}) collective-permute-start(f16[64,256]{1,0:T(8,128)(2,1)S(1)} %get-tuple-element.29), channel_id=1, source_target_pairs={{0,24},{4,28},{8,16},{12,20},{16,8},{20,12},{24,0},{28,4},{1,25},{... | collective-permute-start | bytes 98312 | tf_op jit(solution)/shard_map/ppermute | solution.py:281
  221.5 4.8 %collective-permute-start.41 = (f16[64,256]{1,0:T(8,128)(2,1)S(1)}, f16[64,256]{1,0:T(8,128)(2,1)S(1)}, u32[]{:S(2)}, u32[]{:S(2)}) collective-permute-start(f16[64,256]{1,0:T(8,128)(2,1)S(1)} %get-tuple-element.30), channel_id=1, source_target_pairs={{0,16},{4,20},{8,24},{12,28},{16,0},{20,4},{24,8},{28,12},{1,17},{... | collective-permute-start | bytes 98312 | tf_op jit(solution)/shard_map/ppermute | solution.py:281
  221.5 4.8 %collective-permute-start.40 = (f16[64,256]{1,0:T(8,128)(2,1)S(1)}, f16[64,256]{1,0:T(8,128)(2,1)S(1)}, u32[]{:S(2)}, u32[]{:S(2)}) collective-permute-start(f16[64,256]{1,0:T(8,128)(2,1)S(1)} %get-tuple-element.28), channel_id=1, source_target_pairs={{0,8},{4,12},{8,0},{12,4},{16,24},{20,28},{24,16},{28,20},{1,9},{5... | collective-permute-start | bytes 98312 | tf_op jit(solution)/shard_map/ppermute | solution.py:281
  226.3 23.2 %collective-permute-start.43 = (f32[64,256]{1,0:T(8,128)S(1)}, f32[64,256]{1,0:T(8,128)S(1)}, u32[]{:S(2)}, u32[]{:S(2)}) collective-permute-start(f32[64,256]{1,0:T(8,128)S(1)} %fusion.8.refs_0_), channel_id=1, source_target_pairs={{0,1},{1,0},{2,3},{3,2},{4,5},{5,4},{6,7},{7,6},{8,9},{9,8},{10,11... | collective-permute-start | bytes 196616 | tf_op jit(solution)/shard_map/ppermute | solution.py:284
  226.4 23.2 %collective-permute-start.44 = (f32[64,256]{1,0:T(8,128)S(1)}, f32[64,256]{1,0:T(8,128)S(1)}, u32[]{:S(2)}, u32[]{:S(2)}) collective-permute-start(f32[64,256]{1,0:T(8,128)S(1)} %fusion.8.refs_0_), channel_id=1, source_target_pairs={{0,2},{1,3},{2,0},{3,1},{4,6},{5,7},{6,4},{7,5},{8,10},{9,11},{10,... | collective-permute-start | bytes 196616 | tf_op jit(solution)/shard_map/ppermute | solution.py:284
  228.2 21.4 %collective-permute-start.45 = (f32[64,256]{1,0:T(8,128)S(1)}, f32[64,256]{1,0:T(8,128)S(1)}, u32[]{:S(2)}, u32[]{:S(2)}) collective-permute-start(f32[64,256]{1,0:T(8,128)S(1)} %fusion.8.refs_0_), channel_id=1, source_target_pairs={{0,3},{1,2},{2,1},{3,0},{4,7},{5,6},{6,5},{7,4},{8,11},{9,10},{10,... | collective-permute-start | bytes 196616 | tf_op jit(solution)/shard_map/ppermute | solution.py:284
  228.9 2.0 collective-permute-start.46
  229.2 3.9 %collective-permute-start.47 = (f32[1]{0:T(128)}, f32[1]{0:T(128)}, u32[]{:S(2)}, u32[]{:S(2)}) collective-permute-start(f32[1]{0:T(128)} %bitcast.21), channel_id=1, source_target_pairs={{0,2},{1,3},{2,0},{3,1},{4,6},{5,7},{6,4},{7,5},{8,10},{9,11},{10,... | collective-permute-start | bytes 20 | tf_op jit(solution)/shard_map/ppermute | solution.py:284
  230.9 3.1 %collective-permute-start.48 = (f32[1]{0:T(128)}, f32[1]{0:T(128)}, u32[]{:S(2)}, u32[]{:S(2)}) collective-permute-start(f32[1]{0:T(128)} %bitcast.21), channel_id=1, source_target_pairs={{0,3},{1,2},{2,1},{3,0},{4,7},{5,6},{6,5},{7,4},{8,11},{9,10},{10,... | collective-permute-start | bytes 20 | tf_op jit(solution)/shard_map/ppermute | solution.py:284
  234.7 3.6 %collective-permute-start.49 = (f32[1]{0:T(128)}, f32[1]{0:T(128)}, u32[]{:S(2)}, u32[]{:S(2)}) collective-permute-start(f32[1]{0:T(128)} %add.196), channel_id=1, source_target_pairs={{0,4},{4,0},{8,12},{12,8},{16,20},{20,16},{24,28},{28,24},{1,5},{5... | collective-permute-start | bytes 20 | tf_op jit(solution)/shard_map/ppermute | solution.py:281
  238.9 4.7 %collective-permute-start.50 = (f32[1]{0:T(128)}, f32[1]{0:T(128)}, u32[]{:S(2)}, u32[]{:S(2)}) collective-permute-start(f32[1]{0:T(128)} %add.197), channel_id=1, source_target_pairs={{0,8},{4,12},{8,0},{12,4},{16,24},{20,28},{24,16},{28,20},{1,9},{5... | collective-permute-start | bytes 20 | tf_op jit(solution)/shard_map/ppermute | solution.py:281
  240.8 7.1 %collective-permute-start.51 = (f32[1]{0:T(128)}, f32[1]{0:T(128)}, u32[]{:S(2)}, u32[]{:S(2)}) collective-permute-start(f32[1]{0:T(128)} %add.197), channel_id=1, source_target_pairs={{0,16},{4,20},{8,24},{12,28},{16,0},{20,4},{24,8},{28,12},{1,17},{... | collective-permute-start | bytes 20 | tf_op jit(solution)/shard_map/ppermute | solution.py:281
  243.6 5.3 %collective-permute-start.52 = (f32[1]{0:T(128)}, f32[1]{0:T(128)}, u32[]{:S(2)}, u32[]{:S(2)}) collective-permute-start(f32[1]{0:T(128)} %add.197), channel_id=1, source_target_pairs={{0,24},{4,28},{8,16},{12,20},{16,8},{20,12},{24,0},{28,4},{1,25},{... | collective-permute-start | bytes 20 | tf_op jit(solution)/shard_map/ppermute | solution.py:281
  (12 other events, 9.6 us)

commit v2 on v1

v2 whole, which is shorter than its diff:
```python
import functools

import jax
import jax.numpy as jnp
from jax import lax
from jax.experimental import pallas as pl
from jax.experimental.pallas import tpu as pltpu
from jax.sharding import PartitionSpec as P

CROPS = 8
LOG2E = 1.4426950408889634
SOFT_SCALE = 10.0 * LOG2E
BLOCK = 1024
WIDE = 256
ROWS = 1024

f32 = jnp.float32
bf16 = jnp.bfloat16
f16 = jnp.float16

VMEM = pl.BlockSpec(memory_space=pltpu.VMEM)
SMEM = pl.BlockSpec(memory_space=pltpu.SMEM)
ANY = pl.BlockSpec(memory_space=pl.ANY)


def limit(mib):
    return pltpu.CompilerParams(vmem_limit_bytes=mib << 20)


def bf16_terms(values):
    high = values.astype(bf16)
    rest = values - high.astype(f32)
    middle = rest.astype(bf16)
    return high, middle, (rest - middle.astype(f32)).astype(bf16)


def term_rows(values):
    high, middle, low = bf16_terms(values)
    return jnp.concatenate([high, middle, low] + [jnp.zeros_like(high)] * 5, axis=0)


def sum_terms(products):
    return products[0:1] + products[1:2] + products[2:3]


def dot_nt(left, right):
    return lax.dot_general(left, right, (((1,), (1,)), ((), ())), preferred_element_type=f32)


def dot_tn(left, right):
    return lax.dot_general(left, right, (((0,), (0,)), ((), ())), preferred_element_type=f32)


def unit_rows(raw):
    values = raw.astype(f32)
    inverse = lax.rsqrt(jnp.sum(values * values, axis=1, keepdims=True) + 1e-06)
    return values * inverse, inverse


def prep_kernel(
    place_ref, image_ref, embed_in, queue_in, unit_ref, order_ref, embed_ref, queue_ref, sorted_ref, queued_ref, sems
):
    fetch = [
        pltpu.make_async_copy(embed_in, embed_ref, sems.at[0]),
        pltpu.make_async_copy(queue_in, queue_ref, sems.at[1]),
    ]
    for copy in fetch:
        copy.start()
    row, proto = place_ref[0], place_ref[1]
    rows = embed_ref.shape[0]
    half = rows // 2
    images = half // CROPS
    local = image_ref[...] - row * (rows // CROPS)
    across = jnp.broadcast_to(local, (rows, rows)).astype(f32)
    down = jnp.transpose(across, (1, 0))
    first = lax.broadcasted_iota(jnp.int32, (rows, rows), 0)
    second = lax.broadcasted_iota(jnp.int32, (rows, rows), 1)
    earlier = jnp.where((across == down) & (first < second), 1.0, 0.0)
    rank = jnp.sum(earlier, axis=0, keepdims=True).astype(jnp.int32)
    upper = jnp.where(local >= images, 1, 0)
    position = upper * half + rank * images + (local - upper * images)
    order = (first == position).astype(f32).astype(bf16)
    order_ref[...] = order
    for copy in fetch:
        copy.wait()
    normed = unit_rows(embed_ref[...])[0].astype(bf16)
    sorted_ref[...] = jnp.dot(order, normed, preferred_element_type=f32)
    queued_ref[...] = unit_rows(queue_ref[...])[0]
    share = rows * unit_ref.shape[0] // (rows + queue_ref.shape[0])
    queue_share = unit_ref.shape[0] - share
    unit_ref[0:share, :] = sorted_ref[pl.ds(pl.multiple_of(proto * share, share), share), :].astype(bf16)
    unit_ref[share:, :] = queued_ref[
        pl.ds(pl.multiple_of(proto * queue_share, queue_share), queue_share), :
    ].astype(bf16)


def row_sums(column, total_batch, queue_blocks, mass_ref, out_ref):
    def one(index, carry):
        start = pl.multiple_of(index * BLOCK, BLOCK)
        out_ref[0:1, pl.ds(start, BLOCK)] = sum_terms(dot_nt(column, mass_ref[pl.ds(start, BLOCK), :]))
        return carry

    lax.fori_loop(0, total_batch // BLOCK + queue_blocks, one, 0)


def live_blocks(fill):
    return lax.div(fill + (BLOCK - 1), BLOCK)


def make_kernel(offsets, share, total_batch, place_ref, fill_ref, columns_ref, *refs):
    units = refs[: len(offsets)]
    mass_out, sums_ref, side_ref, batch_ref, mass_ref, queue_ref, col_ref, sems, out_sems = refs[len(offsets) :]
    row, proto = place_ref[0], place_ref[1]
    fill = fill_ref[0]
    z_count, unit_rows_count, _ = units[0].shape
    queue_share = unit_rows_count - share
    proto_count = 1 + max(other for _, other in offsets)
    y_count = 1 + max(y for y, _ in offsets)
    copies = []
    for index, (unit, (y, other)) in enumerate(zip(units, offsets)):
        for z in range(z_count):
            place = (row ^ (z * y_count + y)) * proto_count + (proto ^ other)
            crops = pl.multiple_of(place * share, share)
            queued = pl.multiple_of(place * queue_share, queue_share)
            copies.append(
                pltpu.make_async_copy(
                    unit.at[z, pl.ds(0, share), :],
                    batch_ref.at[pl.ds(crops, share), :],
                    sems.at[index, z, 0],
                )
            )
            copies.append(
                pltpu.make_async_copy(
                    unit.at[z, pl.ds(share, queue_share), :],
                    queue_ref.at[pl.ds(queued, queue_share), :],
                    sems.at[index, z, 1],
                )
            )
    for copy in copies[0::2] + copies[1::2]:
        copy.start()
    total_queue = queue_ref.shape[0]
    width = columns_ref.shape[1]
    col_ref[...] = jnp.zeros_like(col_ref)
    sums_ref[...] = jnp.zeros_like(sums_ref)
    ones = jnp.ones((8, 128), bf16)
    bound = jnp.max(jnp.abs(columns_ref[...].astype(f32)))
    side_ref[0:1, total_batch:] = jnp.full((1, 128), bound, f32)
    for copy in copies[0::2]:
        copy.wait()

    def add_columns(low, mass):
        col_ref[:, low : low + WIDE] += jnp.sum(mass.reshape(BLOCK // 8, 8, WIDE), axis=0)

    def keep(start):
        place = pl.ds(pl.multiple_of(start, BLOCK), BLOCK)
        return pltpu.make_async_copy(mass_ref.at[place, :], mass_out.at[place, :], out_sems)

    def crops_block(index, carry):
        start = pl.multiple_of(index * BLOCK, BLOCK)
        rows = batch_ref[pl.ds(start, BLOCK), :]
        lanes = None
        for low in range(0, width, WIDE):
            scores = jnp.dot(rows, columns_ref[:, low : low + WIDE], preferred_element_type=f32)
            soft = jnp.exp2(scores * SOFT_SCALE)
            mass = soft * soft
            mass_ref[pl.ds(start, BLOCK), low : low + WIDE] = mass.astype(bf16)
            add_columns(low, mass)
            for lane in range(0, WIDE, 128):
                part = soft[:, lane : lane + 128]
                lanes = part if lanes is None else lanes + part
        high, middle, small = bf16_terms(lanes)
        total = dot_nt(ones, high) + dot_nt(ones, middle) + dot_nt(ones, small)
        side_ref[0:1, pl.ds(start, BLOCK)] = total[0:1]
        keep(start).start()
        return carry

    lax.fori_loop(0, total_batch // BLOCK, crops_block, 0)

    for copy in copies[1::2]:
        copy.wait()

    def queue_block(index, carry):
        start = pl.multiple_of(index * BLOCK, BLOCK)
        rows = queue_ref[pl.ds(start, BLOCK), :]
        live = lax.broadcasted_iota(jnp.int32, (BLOCK, WIDE), 0) < fill - start
        place = pl.ds(pl.multiple_of(total_batch + start, BLOCK), BLOCK)
        for low in range(0, width, WIDE):
            scores = jnp.dot(rows, columns_ref[:, low : low + WIDE], preferred_element_type=f32)
            soft = jnp.exp2(scores * SOFT_SCALE)
            mass = jnp.where(live, soft * soft, 0.0)
            mass_ref[place, low : low + WIDE] = mass.astype(bf16)
            add_columns(low, mass)
        keep(total_batch + start).start()
        return carry

    lax.fori_loop(0, live_blocks(fill), queue_block, 0)
    column = term_rows(1.0 / jnp.sum(col_ref[...], axis=0, keepdims=True))
    row_sums(column, total_batch, live_blocks(fill), mass_ref, sums_ref)

    def finish(index, carry):
        keep(index * BLOCK).wait()
        return carry

    lax.fori_loop(0, total_batch // BLOCK + live_blocks(fill), finish, 0)


def column_factor(fill, total_batch, parts, mass_ref, scale_ref, col_ref, ready=None):
    total_rows = mass_ref.shape[0]
    total = parts[0][0:1, 0:total_rows]
    for part in parts[1:]:
        total = total + part[0:1, 0:total_rows]
    place = lax.broadcasted_iota(jnp.int32, (1, total_rows), 1)
    scale = jnp.where(place < total_batch + fill, 1.0 / total, 0.0)
    scale_ref[...] = term_rows(scale)
    col_ref[...] = jnp.zeros_like(col_ref)

    def one(index, carry):
        if ready is not None:
            ready(index)
        rows = pl.ds(pl.multiple_of(index * BLOCK, BLOCK), BLOCK)
        col_ref[...] += jnp.dot(scale_ref[:, rows], mass_ref[rows, :], preferred_element_type=f32)
        return carry

    lax.fori_loop(0, total_batch // BLOCK + live_blocks(fill), one, 0)
    return 1.0 / sum_terms(col_ref[...])


def sweep_kernel(total_batch, fill_ref, mass_in, *refs):
    *parts, sums_ref, mass_ref, scale_ref, col_ref, sems = refs
    fill = fill_ref[0]
    blocks = total_batch // BLOCK + live_blocks(fill)

    def fetch(index):
        rows = pl.ds(pl.multiple_of(index * BLOCK, BLOCK), BLOCK)
        return pltpu.make_async_copy(mass_in.at[rows, :], mass_ref.at[rows, :], sems.at[index])

    def start(index, carry):
        fetch(index).start()
        return carry

    lax.fori_loop(0, blocks, start, 0)
    column = column_factor(
        fill, total_batch, parts, mass_ref, scale_ref, col_ref, lambda index: fetch(index).wait()
    )
    sums_ref[...] = jnp.zeros_like(sums_ref)
    row_sums(term_rows(column), total_batch, live_blocks(fill), mass_ref, sums_ref)


def last_kernel(total_batch, fill_ref, side_ref, mass_ref, *refs):
    *parts, sums_ref, column_ref, scale_ref, col_ref = refs
    fill = fill_ref[0]
    column = column_factor(fill, total_batch, parts, mass_ref, scale_ref, col_ref)
    column_ref[...] = column
    sums_ref[0:1, total_batch:] = side_ref[...]
    row_sums(term_rows(column), total_batch, 0, mass_ref, sums_ref)


def slope_kernel(crop_count, first, last, batch_ref, columns_ref, column_ref, *refs):
    *parts, normed_out, grad_ref, loss_ref, back_ref, normed_ref, sems = refs
    total_batch, width = batch_ref.shape[0], last - first
    rows = ROWS
    wide = min(width, WIDE)
    grad_ref[...] = jnp.zeros_like(grad_ref)
    loss_ref[...] = jnp.zeros_like(loss_ref)

    bound = functools.reduce(jnp.add, [part[0:1, 2 * total_batch :] for part in parts])
    bound = 20.0 * bound + 1e-30
    back_ref[...] = jnp.broadcast_to(bound / 32768.0, (8, 128))
    scale = jnp.concatenate([32768.0 / bound] * (batch_ref.shape[1] // 128), axis=1)

    def keep(index):
        place = pl.ds(pl.multiple_of(index * rows, rows), rows)
        return pltpu.make_async_copy(normed_ref.at[place, :], normed_out.at[place, :], sems.at[index])

    def one(index, carry):
        start = pl.multiple_of(index * rows, rows)
        here = pl.ds(start, rows)

        later = pl.ds(pl.multiple_of(total_batch + start, rows), rows)
        code, soft_line = parts[0][0:1, here], parts[0][0:1, later]
        for part in parts[1:]:
            code, soft_line = code + part[0:1, here], soft_line + part[0:1, later]
        lines = [1.0 / ((crop_count - 1) * code), 10.0 / soft_line, jnp.log(soft_line)]
        factors = jnp.transpose(jnp.concatenate(lines + [jnp.zeros((125, rows), f32)], axis=0), (1, 0))
        code_factor, soft_factor, log_soft = (factors[:, i : i + 1] for i in range(3))
        crops = batch_ref[here, :]
        crops_t = jnp.transpose(crops.astype(f32), (1, 0)).astype(bf16)
        normed = jnp.zeros((rows, crops.shape[1]), f32)
        loss = jnp.zeros((8, 128), f32)
        for low in range(0, width, wide):
            place = slice(first + low, first + low + wide)
            columns = columns_ref[:, place]
            scores = jnp.dot(crops, columns, preferred_element_type=f32)
            soft = jnp.exp2(scores * SOFT_SCALE)
            assigned = (soft * soft) * column_ref[0:1, place] * code_factor
            slabs = assigned.reshape(rows // 128, crop_count, 128 // crop_count, wide)
            grouped = jnp.sum(slabs, axis=1, keepdims=True)
            targets = (grouped - slabs).reshape(rows, wide)
            logits = (soft * soft_factor - targets * 10.0).astype(bf16)
            terms = targets * (log_soft - scores * 10.0)
            folded = jnp.sum(terms.reshape(rows // 8, 8, wide), axis=0)
            for lane in range(0, wide, 128):
                loss = loss + folded[:, lane : lane + 128]
            grad_ref[:, low : low + wide] += jnp.dot(crops_t, logits, preferred_element_type=f32)
            normed = normed + dot_nt(logits, columns)
        normed_ref[here, :] = normed * scale
        keep(index).start()
        loss_ref[...] += loss
        return carry

    lax.fori_loop(0, total_batch // rows, one, 0)

    def kept(index, carry):
        keep(index).wait()
        return carry

    lax.fori_loop(0, total_batch // rows, kept, 0)


def finish_kernel(piece_count, total_batch, proto_ref, embed_ref, order_ref, back_ref, *refs):
    *parts, out_ref, loss_ref, sorted_ref = refs
    pieces, losses = parts[:piece_count], parts[piece_count:]
    rows = embed_ref.shape[0]
    size = rows // piece_count
    proto = proto_ref[0]
    for index, piece in enumerate(pieces):
        other = proto ^ index
        place = (other % 2) * (piece_count // 2) + other // 2
        sorted_ref[pl.ds(pl.multiple_of(place * size, size), size), :] = piece[...]
    loss_ref[0] = jnp.sum(functools.reduce(jnp.add, [loss[...] for loss in losses])) / total_batch
    order = order_ref[...]
    high, middle, low = bf16_terms(sorted_ref[...])
    grad = dot_tn(order, high) + dot_tn(order, middle) + dot_tn(order, low)
    grad = grad * back_ref[0:1, 0:1]
    exact, inverse = unit_rows(embed_ref[...])
    out_ref[...] = inverse * (grad - exact * jnp.sum(exact * grad, axis=1, keepdims=True))


def solution(mesh):
    row_count, proto_count = mesh.shape["row"], mesh.shape["proto"]
    z_count = min(4, row_count)
    y_count = row_count // z_count
    x_count = proto_count // 2

    def shift_row(values, z, y):
        offset = z * y_count + y
        return lax.ppermute(values, "row", [(i, i ^ offset) for i in range(row_count)])

    def shift_proto(values, offset):
        return lax.ppermute(values, "proto", [(i, i ^ offset) for i in range(proto_count)])

    def shift_xy(values, x, y):
        pairs = []
        for i in range(row_count):
            for j in range(proto_count):
                pairs.append((i * proto_count + j, (i ^ y) * proto_count + (j ^ (2 * x))))
        return lax.ppermute(values, ("row", "proto"), pairs)

    def all_sum_parts(values):
        values = values + shift_proto(values, 1)
        moved = [shift_xy(values, x, y) for y in range(y_count) for x in range(x_count) if x or y]
        values = functools.reduce(jnp.add, moved, values)
        return [values] + [shift_row(values, z, 0) for z in range(1, z_count)]

    def body(embeddings, queue_feats, prototypes, crop_image, fill_count):
        batch_rows, feat = embeddings.shape
        queue_rows = queue_feats.shape[0]
        share, queue_share = batch_rows // proto_count, queue_rows // proto_count
        half = batch_rows // 2
        total_batch, total_queue = batch_rows * row_count, queue_rows * row_count
        total_rows = total_batch + total_queue
        row, proto = lax.axis_index("row"), lax.axis_index("proto")
        core, x, y, z = proto % 2, proto // 2, row % y_count, row // y_count
        place = jnp.stack([row, proto]).astype(jnp.int32)
        unit_rows_count = share + queue_share

        unit, order = pl.pallas_call(
            prep_kernel,
            name="prep",
            out_shape=[
                jax.ShapeDtypeStruct((unit_rows_count, feat), bf16),
                jax.ShapeDtypeStruct((batch_rows, batch_rows), bf16),
            ],
            in_specs=[SMEM, VMEM, ANY, ANY],
            out_specs=[VMEM, VMEM],
            scratch_shapes=[
                pltpu.VMEM((batch_rows, feat), bf16),
                pltpu.VMEM((queue_rows, feat), bf16),
                pltpu.VMEM((batch_rows, feat), f32),
                pltpu.VMEM((queue_rows, feat), f32),
                pltpu.SemaphoreType.DMA((2,)),
            ],
            compiler_params=limit(56),
        )(place, crop_image.reshape(1, batch_rows), embeddings, queue_feats)

        lines = jnp.stack([unit] + [shift_row(unit, z, 0) for z in range(1, z_count)])
        width = prototypes.shape[1] // row_count
        blocks = prototypes.reshape(-1, row_count, width).transpose(1, 0, 2)
        lines, blocks = lax.optimization_barrier((lines, blocks))
        columns = lax.all_to_all(blocks, "row", split_axis=0, concat_axis=0, tiled=True).reshape(feat, width)

        offsets, units = [], []
        for dy in range(y_count):
            there = shift_row(lines, 0, dy) if dy else lines
            for dx in range(x_count):
                moved = shift_proto(there, 2 * dx) if dx else there
                offsets += [(dy, 2 * dx), (dy, 2 * dx + 1)]
                units += [moved, shift_proto(moved, 1)]

        mass, sums, side, batch = pl.pallas_call(
            functools.partial(make_kernel, offsets, share, total_batch),
            name="make_mass",
            out_shape=[
                jax.ShapeDtypeStruct((total_rows, width), bf16),
                jax.ShapeDtypeStruct((1, total_rows), f32),
                jax.ShapeDtypeStruct((1, total_batch + 128), f32),
                jax.ShapeDtypeStruct((total_batch, feat), bf16),
            ],
            in_specs=[SMEM, SMEM, VMEM] + [ANY] * len(units),
            out_specs=[ANY, VMEM, VMEM, VMEM],
            scratch_shapes=[
                pltpu.VMEM((total_rows, width), bf16),
                pltpu.VMEM((total_queue, feat), bf16),
                pltpu.VMEM((8, width), f32),
                pltpu.SemaphoreType.DMA((len(units), z_count, 2)),
                pltpu.SemaphoreType.DMA,
            ],
            compiler_params=limit(56),
        )(place, fill_count, columns, *units)

        vectors = [pltpu.VMEM((8, total_rows), bf16), pltpu.VMEM((8, width), f32)]
        sums = pl.pallas_call(
            functools.partial(sweep_kernel, total_batch),
            name="sweep",
            out_shape=jax.ShapeDtypeStruct((1, total_rows), f32),
            in_specs=[SMEM, ANY] + [VMEM] * z_count,
            out_specs=VMEM,
            scratch_shapes=[pltpu.VMEM((total_rows, width), bf16)]
            + vectors
            + [pltpu.SemaphoreType.DMA((total_rows // BLOCK,))],
            compiler_params=limit(30),
        )(fill_count, mass, *all_sum_parts(sums))

        code_sums, column = pl.pallas_call(
            functools.partial(last_kernel, total_batch),
            name="last_sweep",
            out_shape=[
                jax.ShapeDtypeStruct((1, 2 * total_batch + 128), f32),
                jax.ShapeDtypeStruct((1, width), f32),
            ],
            in_specs=[SMEM] + [VMEM] * (2 + z_count),
            out_specs=[VMEM, VMEM],
            scratch_shapes=vectors,
            compiler_params=limit(8),
        )(fill_count, side, mass, *all_sum_parts(sums))

        code_parts = all_sum_parts(code_sums)

        def slopes(first, last, batch):
            return pl.pallas_call(
                functools.partial(slope_kernel, CROPS, first, last),
                name="slopes",
                out_shape=[
                    jax.ShapeDtypeStruct((total_batch, feat), f32),
                    jax.ShapeDtypeStruct((feat, last - first), f32),
                    jax.ShapeDtypeStruct((8, 128), f32),
                    jax.ShapeDtypeStruct((8, 128), f32),
                ],
                in_specs=[VMEM] * (3 + z_count),
                out_specs=[ANY, VMEM, VMEM, VMEM],
                scratch_shapes=[
                    pltpu.VMEM((total_batch, feat), f32),
                    pltpu.SemaphoreType.DMA((total_batch // ROWS,)),
                ],
                compiler_params=limit(24),
            )(batch, columns, column, *code_parts)

        def as_blocks(grad_columns):
            return grad_columns.astype(f16).reshape(row_count, feat // row_count, -1)

        def exchange(blocks):
            return lax.all_to_all(blocks, "row", split_axis=0, concat_axis=0, tiled=True)

        normed_part, grad_columns, loss, back = slopes(0, width, batch)
        size = half // x_count

        def pick(values, index, axis):
            return lax.dynamic_index_in_dim(values, index, axis, keepdims=False)

        pieces = normed_part.reshape(z_count, y_count, 2, x_count, size, feat)

        away = shift_proto(pick(pieces, 1 - core, 2).astype(f16), 1)
        loss = loss + shift_proto(loss, 1)
        kept = pick(pieces, core, 2) + away.astype(f32)
        total, losses = None, None
        for dy in range(y_count):
            for dx in range(x_count):
                part, other = pick(pick(kept, x ^ dx, 2), y ^ dy, 1), loss
                if dx or dy:
                    part = shift_xy(part.astype(f16), dx, dy).astype(f32)
                    other = shift_xy(loss, dx, dy)
                total = part if total is None else total + part
                losses = other if losses is None else losses + other
        piece = pick(total, z, 0)
        loss_parts = [losses]
        for dz in range(1, z_count):
            piece = piece + shift_row(pick(total, z ^ dz, 0).astype(f16), dz, 0).astype(f32)
            loss_parts.append(shift_row(losses, dz, 0))
        piece, *loss_parts = lax.optimization_barrier((piece, *loss_parts))
        grad_proto = exchange(as_blocks(grad_columns)).astype(f32)
        grad_proto = grad_proto.transpose(1, 0, 2).reshape(feat // row_count, row_count * width)

        gathered = [piece] + [shift_proto(piece, k) for k in range(1, proto_count)]
        grad_embed, loss = pl.pallas_call(
            functools.partial(finish_kernel, proto_count, total_batch),
            name="finish",
            out_shape=[
                jax.ShapeDtypeStruct((batch_rows, feat), f32),
                jax.ShapeDtypeStruct((1,), f32),
            ],
            in_specs=[SMEM] + [VMEM] * (3 + proto_count + z_count),
            out_specs=[VMEM, SMEM],
            scratch_shapes=[pltpu.VMEM((batch_rows, feat), f32)],
            compiler_params=limit(8),
        )(proto.reshape(1).astype(jnp.int32), embeddings, order, back, *gathered, *loss_parts)
        return grad_embed, grad_proto, loss

    placed = (P("row", None), P("row", None), P("row", "proto"), P("row"), P())
    return jax.shard_map(
        body,
        mesh=mesh,
        in_specs=placed,
        out_specs=(P("row", None), P("row", "proto"), P()),
        check_vma=False,
    )
```

time: 255 us -> 209 us (0.82); the launches traced: 255 us -> 212 us
  local copies, waits for them, and re-layouts: 32.8 us -> 6.49 us
  between operations: 8.62 us -> 1.69 us
  starting transfers between devices: 71 us -> 64.1 us
  waiting for transfers between devices: 77.1 us -> 72.2 us
    unnamed x42 -> x32, local copies, waits for them, and re-layouts: 27.4 us -> 2.57 us
    ppermute x26 -> x19, waiting for transfers between devices: 56.4 us -> 40.5 us  [shift_row(): lax.ppermute(values, 'row', [(i, i ^ offset) for i in range(row_count)])]
    ppermute x3 -> x15, starting transfers between devices: 3.55 us -> 16.8 us  [shift_xy(): return lax.ppermute(values, ('row', 'proto'), pairs)]
    ppermute x26 -> x19, starting transfers between devices: 44.5 us -> 33.1 us  [shift_row(): lax.ppermute(values, 'row', [(i, i ^ offset) for i in range(row_count)])]
    ppermute x3 -> x15, waiting for transfers between devices: 11.2 us -> 17.2 us  [shift_xy(): return lax.ppermute(values, ('row', 'proto'), pairs)]
    ppermute x24 -> x14, starting transfers between devices: 11.4 us -> 5.92 us  [shift_proto(): lax.ppermute(values, 'proto', [(i, i ^ offset) for i in range(proto_count)])]
    pallas_call x3, Pallas kernels: 42.3 us -> 37.3 us  [the longest x1 23.4 us: body(): pl.pallas_call(functools.partial(make_kernel, offsets, share, total_batch...]
    pallas_call x1, Pallas kernels: 11.4 us -> 16.4 us  [body(): pl.pallas_call(functools.partial(sweep_kernel, total_batch), name='sweep'...]
  transfers between devices with their start and end apart: 55 -> 50, of which waited for: 27 -> 29; matrix products, arithmetic and copies ran while one was open for 1% -> 2% of each run, Pallas kernels for 1% -> 1%
where the time goes in v2:
time: 209 us; the launch traced here: 212 us
  waiting for transfers between devices  72.2 us (35%)
  starting transfers between devices  64.1 us (31%)
  Pallas kernels  63 us (30%)
  local copies, waits for them, and re-layouts  6.49 us (3%)
  other arithmetic  4.37 us (2%)
    ppermute x19, waiting for transfers between devices, shift_row(): lax.ppermute(values, 'row', [(i, i ^ offset) for i in range(row_count)])  40.5 us
    ppermute x19, starting transfers between devices, shift_row(): lax.ppermute(values, 'row', [(i, i ^ offset) for i in range(row_count)])  33.1 us
    pallas_call x1, Pallas kernels, body(): pl.pallas_call(functools.partial(make_kernel, offsets, share, total_batch...  23.4 us
    ppermute x15, waiting for transfers between devices, shift_xy(): return lax.ppermute(values, ('row', 'proto'), pairs)  17.2 us
    ppermute x15, starting transfers between devices, shift_xy(): return lax.ppermute(values, ('row', 'proto'), pairs)  16.8 us
    pallas_call x1, Pallas kernels, body(): pl.pallas_call(functools.partial(sweep_kernel, total_batch), name='sweep'...  16.4 us
    ppermute x14, waiting for transfers between devices, shift_proto(): lax.ppermute(values, 'proto', [(i, i ^ offset) for i in range(proto_count)])  14.4 us
    pallas_call x1, Pallas kernels, slopes(): pl.pallas_call(functools.partial(slope_kernel, CROPS, first, last), name=...  12.7 us
  transfers between devices with their start and end apart: 50, of which 29 were waited for; matrix products, arithmetic and copies ran while one was open for 2% of the time, Pallas kernels for 1%

profile of v2, /device:TPU:0, one launch (start us, length us, event | category | flops | bytes accessed | tf_op | source)
XLA Modules:
  0.0 211.8 jit_solution(6725746897918577041)
XLA Ops:
  1.2 2.6 %prep.1 = (bf16[192,256]{1,0:T(8,128)(2,1)}, bf16[256,256]{1,0:T(8,128)(2,1)}) custom-call(s32[2]{0:T(128)} %pad_add_fusion.place_ref, s32[1,256]{1,0:T(1,128)} %bitcast.58, bf16[256,256]{1,0:T(8,128)(2,1)} %embed_ref.1, bf16[512,256]{1,0:T(8,128)(2,1)} %queue_in.1), custom_call_target="tpu_custom_call" | custom-call | tf_op jit(solution)/shard_map/prep/pallas_call | solution.py:377
  3.9 5.1 %collective-permute-start.2 = (bf16[192,256]{1,0:T(8,128)(2,1)}, bf16[192,256]{1,0:T(8,128)(2,1)S(1)}, u32[]{:S(2)}, u32[]{:S(2)}) collective-permute-start(bf16[192,256]{1,0:T(8,128)(2,1)} %get-tuple-element.25), channel_id=1, source_target_pairs={{0,24},{4,28},{8,16},{12,20},{16,8},{20,12},{24,0},{28,4},{1,25},{... | collective-permute-start | bytes 294920 | tf_op jit(solution)/shard_map/ppermute | solution.py:347
  9.6 2.3 %copy.22 = bf16[4,8,8,2048]{3,2,0,1:T(8,128)(2,1)} copy(bf16[4,8,8,2048]{3,2,1,0:T(8,128)(2,1)} %bitcast.53) | data formatting | bytes 2097152 | tf_op jit(solution)/shard_map/reshape | solution.py:398
  11.9 1.0 collective-permute-done.2
  12.9 4.6 %collective-permute-done.1 = bf16[192,256]{1,0:T(8,128)(2,1)S(1)} collective-permute-done((bf16[192,256]{1,0:T(8,128)(2,1)}, bf16[192,256]{1,0:T(8,128)(2,1)S(1)}, u32[]{:S(2)}, u32[]{:S(2)}) %collective-permute-start.1) | collective-permute-done | bytes 98336 | tf_op jit(solution)/shard_map/ppermute | solution.py:347
  17.5 4.8 %all-to-all-start = ((bf16[8,32,2048]{2,1,0:T(8,128)(2,1)}), bf16[8,32,2048]{2,1,0:T(8,128)(2,1)S(1)}, u32[]{:S(2)}, u32[]{:S(2)}) async-start(bf16[8,32,2048]{2,1,0:T(8,128)(2,1)} %bitcast.48), calls=%async_computation | async-start | bytes 2097152 | tf_op jit(solution)/shard_map/all_to_all | solution.py:400
  22.3 2.0 collective-permute-start.6
  24.3 1.5 collective-permute-start.4
  25.8 17.4 %collective-permute-done.6.refs_4_ = bf16[4,192,256]{2,1,0:T(8,128)(2,1)S(1)} collective-permute-done((bf16[4,192,256]{2,1,0:T(8,128)(2,1)S(1)}, bf16[4,192,256]{2,1,0:T(8,128)(2,1)S(1)}, u32[]{:S(2)}, u32[]{:S(2)}) %collective-permute-start.6) | collective-permute-done | bytes 393248 | tf_op jit(solution)/shard_map/ppermute | solution.py:347
  43.2 1.5 collective-permute-start.8
  45.3 5.7 %collective-permute-done.8.refs_6_ = bf16[4,192,256]{2,1,0:T(8,128)(2,1)S(1)} collective-permute-done((bf16[4,192,256]{2,1,0:T(8,128)(2,1)S(1)}, bf16[4,192,256]{2,1,0:T(8,128)(2,1)S(1)}, u32[]{:S(2)}, u32[]{:S(2)}) %collective-permute-start.8) | collective-permute-done | bytes 393248 | tf_op jit(solution)/shard_map/ppermute | solution.py:350
  51.7 0.8 copy-done.14
  53.8 23.4 %make_mass.1 = (bf16[6144,2048]{1,0:T(8,128)(2,1)}, f32[1,6144]{1,0:T(1,128)}, f32[1,2176]{1,0:T(1,128)}, bf16[2048,256]{1,0:T(8,128)(2,1)}) custom-call(s32[2]{0:T(128)} %pad_add_fusion.place_ref, s32[1]{0:T(128)S(6)} %copy.23.fill_ref, bf16[256,2048]{1,0:T(8,128)(2,1)} %bitcast.49, bf16[4,192,256]{2,1,0:T(8,128)(2,1)} %copy-done.7, ...), custom_call_target="tpu_custom_call" | custom-call | tf_op jit(solution)/shard_map/make_mass/pallas_call | solution.py:410
  77.6 1.1 collective-permute-done.10
  78.7 0.8 add.137
  79.5 1.9 collective-permute-start.13
  81.4 1.1 collective-permute-start.12
  83.0 1.3 collective-permute-done.13
  84.4 0.8 collective-permute-done.12
  85.2 1.1 collective-permute-done.11
  86.4 2.4 %collective-permute-start.14 = (f32[1,6144]{1,0:T(1,128)S(1)}, f32[1,6144]{1,0:T(1,128)S(1)}, u32[]{:S(2)}, u32[]{:S(2)}) collective-permute-start(f32[1,6144]{1,0:T(1,128)S(1)} %add_add_fusion.1.refs_0_), channel_id=1, source_target_pairs={{0,8},{4,12},{8,0},{12,4},{16,24},{20,28},{24,16},{28,20},{1,9},{5... | collective-permute-start | bytes 73736 | tf_op jit(solution)/shard_map/ppermute | solution.py:347
  88.7 2.5 %collective-permute-start.15 = (f32[1,6144]{1,0:T(1,128)S(1)}, f32[1,6144]{1,0:T(1,128)S(1)}, u32[]{:S(2)}, u32[]{:S(2)}) collective-permute-start(f32[1,6144]{1,0:T(1,128)S(1)} %add_add_fusion.1.refs_0_), channel_id=1, source_target_pairs={{0,16},{4,20},{8,24},{12,28},{16,0},{20,4},{24,8},{28,12},{1,17},{... | collective-permute-start | bytes 73736 | tf_op jit(solution)/shard_map/ppermute | solution.py:347
  91.2 2.3 %collective-permute-done.15.refs_2_ = f32[1,6144]{1,0:T(1,128)S(1)} collective-permute-done((f32[1,6144]{1,0:T(1,128)S(1)}, f32[1,6144]{1,0:T(1,128)S(1)}, u32[]{:S(2)}, u32[]{:S(2)}) %collective-permute-start.15) | collective-permute-done | bytes 24608 | tf_op jit(solution)/shard_map/ppermute | solution.py:347
  93.5 3.3 %collective-permute-done.16.refs_3_ = f32[1,6144]{1,0:T(1,128)S(1)} collective-permute-done((f32[1,6144]{1,0:T(1,128)S(1)}, f32[1,6144]{1,0:T(1,128)S(1)}, u32[]{:S(2)}, u32[]{:S(2)}) %collective-permute-start.16) | collective-permute-done | bytes 24608 | tf_op jit(solution)/shard_map/ppermute | solution.py:347
  96.9 16.4 %sweep.1 = f32[1,6144]{1,0:T(1,128)S(1)} custom-call(s32[1]{0:T(128)S(6)} %copy.23.fill_ref, bf16[6144,2048]{1,0:T(8,128)(2,1)} %get-tuple-element.30.mass_in.mass_ref, f32[1,6144]{1,0:T(1,128)S(1)} %add_add_fusion.1.refs_0_, f32[1,6144]{1,0:T(1,128)S(1)} %collective-permute-done.14.refs_1_, f32[1,6144]{1,0:T(1,128)S(1)} %collective-permute-done.15.refs_2_, ...), custom_call_target="tpu_custom_call" | custom-call | tf_op jit(solution)/shard_map/sweep/pallas_call | solution.py:432
  113.3 1.2 collective-permute-done.17
  114.5 0.9 collective-permute-start.20
  115.5 1.1 collective-permute-start.19
  116.6 1.5 collective-permute-start.18
  118.1 1.4 collective-permute-done.20
  119.6 0.9 collective-permute-done.18
  120.6 0.8 collective-permute-start.22
  121.4 3.6 %collective-permute-start.23 = (f32[1,6144]{1,0:T(1,128)S(1)}, f32[1,6144]{1,0:T(1,128)S(1)}, u32[]{:S(2)}, u32[]{:S(2)}) collective-permute-start(f32[1,6144]{1,0:T(1,128)S(1)} %add_add_fusion.refs_0_), channel_id=1, source_target_pairs={{0,24},{4,28},{8,16},{12,20},{16,8},{20,12},{24,0},{28,4},{1,25},{... | collective-permute-start | bytes 73736 | tf_op jit(solution)/shard_map/ppermute | solution.py:347
  125.4 1.6 collective-permute-done.23.refs_3_
  127.0 6.7 %last_sweep.1 = (f32[1,4224]{1,0:T(1,128)S(1)}, f32[1,2048]{1,0:T(1,128)S(1)}) custom-call(s32[1]{0:T(128)S(6)} %copy.23.fill_ref, f32[1,2176]{1,0:T(1,128)S(1)} %copy-done.6, bf16[6144,2048]{1,0:T(8,128)(2,1)S(1)} %copy-done, f32[1,6144]{1,0:T(1,128)S(1)} %add_add_fusion.refs_0_, f32[1,6144]{1,0:T(1,128)S(1)} %collective-permute-done.21.refs_1_, ...), custom_call_target="tpu_custom_call" | custom-call | tf_op jit(solution)/shard_map/last_sweep/pallas_call | solution.py:444
  133.7 1.2 collective-permute-done.24
  134.9 2.7 %collective-permute-start.27 = (f32[1,4224]{1,0:T(1,128)S(1)}, f32[1,4224]{1,0:T(1,128)S(1)}, u32[]{:S(2)}, u32[]{:S(2)}) collective-permute-start(f32[1,4224]{1,0:T(1,128)S(1)} %add.145), channel_id=1, source_target_pairs={{0,6},{1,7},{2,4},{3,5},{4,2},{5,3},{6,0},{7,1},{8,14},{9,15},{10,... | collective-permute-start | bytes 50696 | tf_op jit(solution)/shard_map/ppermute | solution.py:357
  138.5 1.2 collective-permute-done.27
  139.7 1.8 collective-permute-done.26
  142.1 3.8 %collective-permute-start.29 = (f32[1,4224]{1,0:T(1,128)S(1)}, f32[1,4224]{1,0:T(1,128)S(1)}, u32[]{:S(2)}, u32[]{:S(2)}) collective-permute-start(f32[1,4224]{1,0:T(1,128)S(1)} %add_add_fusion.2.refs_0_), channel_id=1, source_target_pairs={{0,16},{4,20},{8,24},{12,28},{16,0},{20,4},{24,8},{28,12},{1,17},{... | collective-permute-start | bytes 50696 | tf_op jit(solution)/shard_map/ppermute | solution.py:347
  146.2 1.5 collective-permute-done.29.refs_2_
  147.7 3.8 %collective-permute-done.30.refs_3_ = f32[1,4224]{1,0:T(1,128)S(1)} collective-permute-done((f32[1,4224]{1,0:T(1,128)S(1)}, f32[1,4224]{1,0:T(1,128)S(1)}, u32[]{:S(2)}, u32[]{:S(2)}) %collective-permute-start.30) | collective-permute-done | bytes 16928 | tf_op jit(solution)/shard_map/ppermute | solution.py:347
  151.5 12.7 %slopes.1 = (f32[2048,256]{1,0:T(8,128)S(1)}, f32[256,2048]{1,0:T(8,128)S(1)}, f32[8,128]{1,0:T(8,128)S(1)}, f32[8,128]{1,0:T(8,128)S(1)}) custom-call(bf16[2048,256]{1,0:T(8,128)(2,1)S(1)} %copy-done.3, bf16[256,2048]{1,0:T(8,128)(2,1)S(1)} %bitcast.50, f32[1,2048]{1,0:T(1,128)S(1)} %get-tuple-element.32.column_ref, f32[1,4224]{1,0:T(1,128)S(1)} %add_add_fusion.2.refs_0_, ...), custom_call_target="tpu_custom_call" | custom-call | tf_op jit(solution)/shard_map/slopes/pallas_call | solution.py:460
  164.5 1.1 convert_element_type.88
  165.7 3.6 %all-to-all-start.1 = ((f16[8,32,2048]{2,1,0:T(8,128)(2,1)}), f16[8,32,2048]{2,1,0:T(8,128)(2,1)S(1)}, u32[]{:S(2)}, u32[]{:S(2)}) async-start(f16[8,32,2048]{2,1,0:T(8,128)(2,1)} %bitcast.20), calls=%async_computation.1 | async-start | bytes 2097152 | tf_op jit(solution)/shard_map/all_to_all | solution.py:482
  169.3 0.8 copy-done.8
  170.1 1.2 bitcast_add_fusion
  171.5 1.9 collective-permute-start.34
  173.5 1.5 collective-permute-start.32
  175.0 1.2 collective-permute-done.38
  176.2 1.8 collective-permute-start.41
  178.2 1.6 collective-permute-done.34
  180.3 6.8 %collective-permute-done.33 = f16[4,64,256]{2,1,0:T(8,128)(2,1)S(1)} collective-permute-done((f16[4,64,256]{2,1,0:T(8,128)(2,1)S(1)}, f16[4,64,256]{2,1,0:T(8,128)(2,1)S(1)}, u32[]{:S(2)}, u32[]{:S(2)}) %collective-permute-start.33) | collective-permute-done | bytes 131104 | tf_op jit(solution)/shard_map/ppermute | solution.py:357
  187.2 5.8 %collective-permute-start.37 = (f16[64,256]{1,0:T(8,128)(2,1)S(1)}, f16[64,256]{1,0:T(8,128)(2,1)S(1)}, u32[]{:S(2)}, u32[]{:S(2)}) collective-permute-start(f16[64,256]{1,0:T(8,128)(2,1)S(1)} %get-tuple-element.51), channel_id=1, source_target_pairs={{0,24},{4,28},{8,16},{12,20},{16,8},{20,12},{24,0},{28,4},{1,25},{... | collective-permute-start | bytes 98312 | tf_op jit(solution)/shard_map/ppermute | solution.py:347
  193.0 0.6 collective-permute-start.35
  193.7 1.5 collective-permute-start.42
  195.1 2.9 %collective-permute-start.43 = (f32[8,128]{1,0:T(8,128)S(1)}, f32[8,128]{1,0:T(8,128)S(1)}, u32[]{:S(2)}, u32[]{:S(2)}) collective-permute-start(f32[8,128]{1,0:T(8,128)S(1)} %add_add_fusion.3.refs_4_), channel_id=1, source_target_pairs={{0,16},{4,20},{8,24},{12,28},{16,0},{20,4},{24,8},{28,12},{1,17},{... | collective-permute-start | bytes 12296 | tf_op jit(solution)/shard_map/ppermute | solution.py:347
  198.1 0.7 collective-permute-start.44
  198.8 0.8 collective-permute-done.43.refs_6_
  199.6 3.8 %collective-permute-done.44.refs_7_ = f32[8,128]{1,0:T(8,128)S(1)} collective-permute-done((f32[8,128]{1,0:T(8,128)S(1)}, f32[8,128]{1,0:T(8,128)S(1)}, u32[]{:S(2)}, u32[]{:S(2)}) %collective-permute-start.44) | collective-permute-done | bytes 4128 | tf_op jit(solution)/shard_map/ppermute | solution.py:347
  204.0 1.3 collective-permute-start.47
  205.3 3.0 %collective-permute-done.46.refs_2_ = f32[64,256]{1,0:T(8,128)S(1)} collective-permute-done((f32[64,256]{1,0:T(8,128)S(1)}, f32[64,256]{1,0:T(8,128)S(1)}, u32[]{:S(2)}, u32[]{:S(2)}) %collective-permute-start.46) | collective-permute-done | bytes 65568 | tf_op jit(solution)/shard_map/ppermute | solution.py:350
  209.0 1.1 finish.1
  210.3 1.5 copy.16
  (95 shorter events, 9.4 us)
Async XLA Ops:
  3.8 13.6 %copy-start.15 = (bf16[192,256]{1,0:T(8,128)(2,1)S(1)}, bf16[192,256]{1,0:T(8,128)(2,1)}, u32[]{:S(2)}) copy-start(bf16[192,256]{1,0:T(8,128)(2,1)} %get-tuple-element.25) | copy-start | bytes 294916
  3.9 9.0 %collective-permute-start.2 = (bf16[192,256]{1,0:T(8,128)(2,1)}, bf16[192,256]{1,0:T(8,128)(2,1)S(1)}, u32[]{:S(2)}, u32[]{:S(2)}) collective-permute-start(bf16[192,256]{1,0:T(8,128)(2,1)} %get-tuple-element.25), channel_id=1, source_target_pairs={{0,24},{4,28},{8,16},{12,20},{16,8},{20,12},{24,0},{28,4},{1,25},{... | collective-permute-start | bytes 294920 | tf_op jit(solution)/shard_map/ppermute | solution.py:347
  9.0 8.5 %collective-permute-start.1 = (bf16[192,256]{1,0:T(8,128)(2,1)}, bf16[192,256]{1,0:T(8,128)(2,1)S(1)}, u32[]{:S(2)}, u32[]{:S(2)}) collective-permute-start(bf16[192,256]{1,0:T(8,128)(2,1)} %get-tuple-element.25), channel_id=1, source_target_pairs={{0,16},{4,20},{8,24},{12,28},{16,0},{20,4},{24,8},{28,12},{1,17},{... | collective-permute-start | bytes 294920 | tf_op jit(solution)/shard_map/ppermute | solution.py:347
  9.0 8.5 %collective-permute-start = (bf16[192,256]{1,0:T(8,128)(2,1)}, bf16[192,256]{1,0:T(8,128)(2,1)S(1)}, u32[]{:S(2)}, u32[]{:S(2)}) collective-permute-start(bf16[192,256]{1,0:T(8,128)(2,1)} %get-tuple-element.25), channel_id=1, source_target_pairs={{0,8},{4,12},{8,0},{12,4},{16,24},{20,28},{24,16},{28,20},{1,9},{5... | collective-permute-start | bytes 294920 | tf_op jit(solution)/shard_map/ppermute | solution.py:347
  17.5 35.3 %copy-start.7 = (bf16[4,192,256]{2,1,0:T(8,128)(2,1)}, bf16[4,192,256]{2,1,0:T(8,128)(2,1)S(1)}, u32[]{:S(2)}) copy-start(bf16[4,192,256]{2,1,0:T(8,128)(2,1)S(1)} %pad_maximum_fusion.refs_0_) | copy-start | bytes 1179652
  17.5 35.3 %all-to-all-start = ((bf16[8,32,2048]{2,1,0:T(8,128)(2,1)}), bf16[8,32,2048]{2,1,0:T(8,128)(2,1)S(1)}, u32[]{:S(2)}, u32[]{:S(2)}) async-start(bf16[8,32,2048]{2,1,0:T(8,128)(2,1)} %bitcast.48), calls=%async_computation | async-start | bytes 2097152 | tf_op jit(solution)/shard_map/all_to_all | solution.py:400
  22.3 20.9 %collective-permute-start.6 = (bf16[4,192,256]{2,1,0:T(8,128)(2,1)S(1)}, bf16[4,192,256]{2,1,0:T(8,128)(2,1)S(1)}, u32[]{:S(2)}, u32[]{:S(2)}) collective-permute-start(bf16[4,192,256]{2,1,0:T(8,128)(2,1)S(1)} %pad_maximum_fusion.refs_0_), channel_id=1, source_target_pairs={{0,4},{4,0},{8,12},{12,8},{16,20},{20,16},{24,28},{28,24},{1,5},{5... | collective-permute-start | bytes 1179656 | tf_op jit(solution)/shard_map/ppermute | solution.py:347
  24.3 20.9 %collective-permute-start.4 = (bf16[4,192,256]{2,1,0:T(8,128)(2,1)S(1)}, bf16[4,192,256]{2,1,0:T(8,128)(2,1)S(1)}, u32[]{:S(2)}, u32[]{:S(2)}) collective-permute-start(bf16[4,192,256]{2,1,0:T(8,128)(2,1)S(1)} %pad_maximum_fusion.refs_0_), channel_id=1, source_target_pairs={{0,2},{1,3},{2,0},{3,1},{4,6},{5,7},{6,4},{7,5},{8,10},{9,11},{10,... | collective-permute-start | bytes 1179656 | tf_op jit(solution)/shard_map/ppermute | solution.py:350
  43.2 9.6 %copy-start.9 = (bf16[4,192,256]{2,1,0:T(8,128)(2,1)}, bf16[4,192,256]{2,1,0:T(8,128)(2,1)S(1)}, u32[]{:S(2)}) copy-start(bf16[4,192,256]{2,1,0:T(8,128)(2,1)S(1)} %collective-permute-done.6.refs_4_) | copy-start | bytes 1179652
  43.2 7.8 %collective-permute-start.8 = (bf16[4,192,256]{2,1,0:T(8,128)(2,1)S(1)}, bf16[4,192,256]{2,1,0:T(8,128)(2,1)S(1)}, u32[]{:S(2)}, u32[]{:S(2)}) collective-permute-start(bf16[4,192,256]{2,1,0:T(8,128)(2,1)S(1)} %collective-permute-done.6.refs_4_), channel_id=1, source_target_pairs={{0,2},{1,3},{2,0},{3,1},{4,6},{5,7},{6,4},{7,5},{8,10},{9,11},{10,... | collective-permute-start | bytes 1179656 | tf_op jit(solution)/shard_map/ppermute | solution.py:350
  44.7 6.9 %collective-permute-start.3 = (bf16[4,192,256]{2,1,0:T(8,128)(2,1)S(1)}, bf16[4,192,256]{2,1,0:T(8,128)(2,1)S(1)}, u32[]{:S(2)}, u32[]{:S(2)}) collective-permute-start(bf16[4,192,256]{2,1,0:T(8,128)(2,1)S(1)} %pad_maximum_fusion.refs_0_), channel_id=1, source_target_pairs={{0,1},{1,0},{2,3},{3,2},{4,5},{5,4},{6,7},{7,6},{8,9},{9,8},{10,11... | collective-permute-start | bytes 1179656 | tf_op jit(solution)/shard_map/ppermute | solution.py:350
  44.7 7.0 %collective-permute-start.7 = (bf16[4,192,256]{2,1,0:T(8,128)(2,1)S(1)}, bf16[4,192,256]{2,1,0:T(8,128)(2,1)S(1)}, u32[]{:S(2)}, u32[]{:S(2)}) collective-permute-start(bf16[4,192,256]{2,1,0:T(8,128)(2,1)S(1)} %collective-permute-done.6.refs_4_), channel_id=1, source_target_pairs={{0,1},{1,0},{2,3},{3,2},{4,5},{5,4},{6,7},{7,6},{8,9},{9,8},{10,11... | collective-permute-start | bytes 1179656 | tf_op jit(solution)/shard_map/ppermute | solution.py:350
  45.2 7.7 %copy-start.10 = (bf16[4,192,256]{2,1,0:T(8,128)(2,1)}, bf16[4,192,256]{2,1,0:T(8,128)(2,1)S(1)}, u32[]{:S(2)}) copy-start(bf16[4,192,256]{2,1,0:T(8,128)(2,1)S(1)} %collective-permute-done.4.refs_2_) | copy-start | bytes 1179652
  45.2 6.4 %collective-permute-start.5 = (bf16[4,192,256]{2,1,0:T(8,128)(2,1)S(1)}, bf16[4,192,256]{2,1,0:T(8,128)(2,1)S(1)}, u32[]{:S(2)}, u32[]{:S(2)}) collective-permute-start(bf16[4,192,256]{2,1,0:T(8,128)(2,1)S(1)} %collective-permute-done.4.refs_2_), channel_id=1, source_target_pairs={{0,1},{1,0},{2,3},{3,2},{4,5},{5,4},{6,7},{7,6},{8,9},{9,8},{10,11... | collective-permute-start | bytes 1179656 | tf_op jit(solution)/shard_map/ppermute | solution.py:350
  51.0 1.9 copy-start.11
  51.0 1.9 collective-permute-start.9
  51.6 1.2 copy-start.12
  52.8 1.0 copy-start.1
  77.2 1.5 collective-permute-start.10
  79.5 4.9 %collective-permute-start.13 = (f32[1,6144]{1,0:T(1,128)S(1)}, f32[1,6144]{1,0:T(1,128)S(1)}, u32[]{:S(2)}, u32[]{:S(2)}) collective-permute-start(f32[1,6144]{1,0:T(1,128)S(1)} %add.137), channel_id=1, source_target_pairs={{0,6},{1,7},{2,4},{3,5},{4,2},{5,3},{6,0},{7,1},{8,14},{9,15},{10,... | collective-permute-start | bytes 73736 | tf_op jit(solution)/shard_map/ppermute | solution.py:357
  81.4 3.8 %collective-permute-start.12 = (f32[1,6144]{1,0:T(1,128)S(1)}, f32[1,6144]{1,0:T(1,128)S(1)}, u32[]{:S(2)}, u32[]{:S(2)}) collective-permute-start(f32[1,6144]{1,0:T(1,128)S(1)} %add.137), channel_id=1, source_target_pairs={{0,4},{1,5},{2,6},{3,7},{4,0},{5,1},{6,2},{7,3},{8,12},{9,13},{10,... | collective-permute-start | bytes 73736 | tf_op jit(solution)/shard_map/ppermute | solution.py:357
  82.5 3.8 %collective-permute-start.11 = (f32[1,6144]{1,0:T(1,128)S(1)}, f32[1,6144]{1,0:T(1,128)S(1)}, u32[]{:S(2)}, u32[]{:S(2)}) collective-permute-start(f32[1,6144]{1,0:T(1,128)S(1)} %add.137), channel_id=1, source_target_pairs={{0,2},{1,3},{2,0},{3,1},{4,6},{5,7},{6,4},{7,5},{8,10},{9,11},{10,... | collective-permute-start | bytes 73736 | tf_op jit(solution)/shard_map/ppermute | solution.py:357
  86.4 4.9 %collective-permute-start.14 = (f32[1,6144]{1,0:T(1,128)S(1)}, f32[1,6144]{1,0:T(1,128)S(1)}, u32[]{:S(2)}, u32[]{:S(2)}) collective-permute-start(f32[1,6144]{1,0:T(1,128)S(1)} %add_add_fusion.1.refs_0_), channel_id=1, source_target_pairs={{0,8},{4,12},{8,0},{12,4},{16,24},{20,28},{24,16},{28,20},{1,9},{5... | collective-permute-start | bytes 73736 | tf_op jit(solution)/shard_map/ppermute | solution.py:347
  88.7 4.8 %collective-permute-start.15 = (f32[1,6144]{1,0:T(1,128)S(1)}, f32[1,6144]{1,0:T(1,128)S(1)}, u32[]{:S(2)}, u32[]{:S(2)}) collective-permute-start(f32[1,6144]{1,0:T(1,128)S(1)} %add_add_fusion.1.refs_0_), channel_id=1, source_target_pairs={{0,16},{4,20},{8,24},{12,28},{16,0},{20,4},{24,8},{28,12},{1,17},{... | collective-permute-start | bytes 73736 | tf_op jit(solution)/shard_map/ppermute | solution.py:347
  91.2 5.6 %collective-permute-start.16 = (f32[1,6144]{1,0:T(1,128)S(1)}, f32[1,6144]{1,0:T(1,128)S(1)}, u32[]{:S(2)}, u32[]{:S(2)}) collective-permute-start(f32[1,6144]{1,0:T(1,128)S(1)} %add_add_fusion.1.refs_0_), channel_id=1, source_target_pairs={{0,24},{4,28},{8,16},{12,20},{16,8},{20,12},{24,0},{28,4},{1,25},{... | collective-permute-start | bytes 73736 | tf_op jit(solution)/shard_map/ppermute | solution.py:347
  96.9 30.1 %copy-start = (bf16[6144,2048]{1,0:T(8,128)(2,1)S(1)}, bf16[6144,2048]{1,0:T(8,128)(2,1)}, u32[]{:S(2)}) copy-start(bf16[6144,2048]{1,0:T(8,128)(2,1)} %get-tuple-element.30.mass_in.mass_ref) | copy-start | bytes 75497472
  96.9 30.1 %copy-start.6 = (f32[1,2176]{1,0:T(1,128)S(1)}, f32[1,2176]{1,0:T(1,128)}, u32[]{:S(2)}) copy-start(f32[1,2176]{1,0:T(1,128)} %get-tuple-element.29.side_ref) | copy-start | bytes 26116
  113.3 1.3 collective-permute-start.17
  114.5 5.0 %collective-permute-start.20 = (f32[1,6144]{1,0:T(1,128)S(1)}, f32[1,6144]{1,0:T(1,128)S(1)}, u32[]{:S(2)}, u32[]{:S(2)}) collective-permute-start(f32[1,6144]{1,0:T(1,128)S(1)} %add.141), channel_id=1, source_target_pairs={{0,6},{1,7},{2,4},{3,5},{4,2},{5,3},{6,0},{7,1},{8,14},{9,15},{10,... | collective-permute-start | bytes 73736 | tf_op jit(solution)/shard_map/ppermute | solution.py:357
  115.5 4.1 %collective-permute-start.19 = (f32[1,6144]{1,0:T(1,128)S(1)}, f32[1,6144]{1,0:T(1,128)S(1)}, u32[]{:S(2)}, u32[]{:S(2)}) collective-permute-start(f32[1,6144]{1,0:T(1,128)S(1)} %add.141), channel_id=1, source_target_pairs={{0,4},{1,5},{2,6},{3,7},{4,0},{5,1},{6,2},{7,3},{8,12},{9,13},{10,... | collective-permute-start | bytes 73736 | tf_op jit(solution)/shard_map/ppermute | solution.py:357
  116.6 3.8 %collective-permute-start.18 = (f32[1,6144]{1,0:T(1,128)S(1)}, f32[1,6144]{1,0:T(1,128)S(1)}, u32[]{:S(2)}, u32[]{:S(2)}) collective-permute-start(f32[1,6144]{1,0:T(1,128)S(1)} %add.141), channel_id=1, source_target_pairs={{0,2},{1,3},{2,0},{3,1},{4,6},{5,7},{6,4},{7,5},{8,10},{9,11},{10,... | collective-permute-start | bytes 73736 | tf_op jit(solution)/shard_map/ppermute | solution.py:357
  120.5 4.5 %collective-permute-start.21 = (f32[1,6144]{1,0:T(1,128)S(1)}, f32[1,6144]{1,0:T(1,128)S(1)}, u32[]{:S(2)}, u32[]{:S(2)}) collective-permute-start(f32[1,6144]{1,0:T(1,128)S(1)} %add_add_fusion.refs_0_), channel_id=1, source_target_pairs={{0,8},{4,12},{8,0},{12,4},{16,24},{20,28},{24,16},{28,20},{1,9},{5... | collective-permute-start | bytes 73736 | tf_op jit(solution)/shard_map/ppermute | solution.py:347
  120.6 4.8 %collective-permute-start.22 = (f32[1,6144]{1,0:T(1,128)S(1)}, f32[1,6144]{1,0:T(1,128)S(1)}, u32[]{:S(2)}, u32[]{:S(2)}) collective-permute-start(f32[1,6144]{1,0:T(1,128)S(1)} %add_add_fusion.refs_0_), channel_id=1, source_target_pairs={{0,16},{4,20},{8,24},{12,28},{16,0},{20,4},{24,8},{28,12},{1,17},{... | collective-permute-start | bytes 73736 | tf_op jit(solution)/shard_map/ppermute | solution.py:347
  121.4 5.6 %collective-permute-start.23 = (f32[1,6144]{1,0:T(1,128)S(1)}, f32[1,6144]{1,0:T(1,128)S(1)}, u32[]{:S(2)}, u32[]{:S(2)}) collective-permute-start(f32[1,6144]{1,0:T(1,128)S(1)} %add_add_fusion.refs_0_), channel_id=1, source_target_pairs={{0,24},{4,28},{8,16},{12,20},{16,8},{20,12},{24,0},{28,4},{1,25},{... | collective-permute-start | bytes 73736 | tf_op jit(solution)/shard_map/ppermute | solution.py:347
  127.0 24.5 %copy-start.2 = (bf16[8,32,2048]{2,1,0:T(8,128)(2,1)S(1)}, bf16[8,32,2048]{2,1,0:T(8,128)(2,1)}, u32[]{:S(2)}) copy-start(bf16[8,32,2048]{2,1,0:T(8,128)(2,1)} %copy-done.1) | copy-start | bytes 3145732
  127.0 24.5 %copy-start.3 = (bf16[2048,256]{1,0:T(8,128)(2,1)S(1)}, bf16[2048,256]{1,0:T(8,128)(2,1)}, u32[]{:S(2)}) copy-start(bf16[2048,256]{1,0:T(8,128)(2,1)} %get-tuple-element.28.batch_ref) | copy-start | bytes 3145732
  133.7 1.2 collective-permute-start.24
  134.9 4.7 %collective-permute-start.27 = (f32[1,4224]{1,0:T(1,128)S(1)}, f32[1,4224]{1,0:T(1,128)S(1)}, u32[]{:S(2)}, u32[]{:S(2)}) collective-permute-start(f32[1,4224]{1,0:T(1,128)S(1)} %add.145), channel_id=1, source_target_pairs={{0,6},{1,7},{2,4},{3,5},{4,2},{5,3},{6,0},{7,1},{8,14},{9,15},{10,... | collective-permute-start | bytes 50696 | tf_op jit(solution)/shard_map/ppermute | solution.py:357
  137.7 3.7 %collective-permute-start.26 = (f32[1,4224]{1,0:T(1,128)S(1)}, f32[1,4224]{1,0:T(1,128)S(1)}, u32[]{:S(2)}, u32[]{:S(2)}) collective-permute-start(f32[1,4224]{1,0:T(1,128)S(1)} %add.145), channel_id=1, source_target_pairs={{0,4},{1,5},{2,6},{3,7},{4,0},{5,1},{6,2},{7,3},{8,12},{9,13},{10,... | collective-permute-start | bytes 50696 | tf_op jit(solution)/shard_map/ppermute | solution.py:357
  138.0 3.7 %collective-permute-start.25 = (f32[1,4224]{1,0:T(1,128)S(1)}, f32[1,4224]{1,0:T(1,128)S(1)}, u32[]{:S(2)}, u32[]{:S(2)}) collective-permute-start(f32[1,4224]{1,0:T(1,128)S(1)} %add.145), channel_id=1, source_target_pairs={{0,2},{1,3},{2,0},{3,1},{4,6},{5,7},{6,4},{7,5},{8,10},{9,11},{10,... | collective-permute-start | bytes 50696 | tf_op jit(solution)/shard_map/ppermute | solution.py:357
  141.7 4.5 %collective-permute-start.28 = (f32[1,4224]{1,0:T(1,128)S(1)}, f32[1,4224]{1,0:T(1,128)S(1)}, u32[]{:S(2)}, u32[]{:S(2)}) collective-permute-start(f32[1,4224]{1,0:T(1,128)S(1)} %add_add_fusion.2.refs_0_), channel_id=1, source_target_pairs={{0,8},{4,12},{8,0},{12,4},{16,24},{20,28},{24,16},{28,20},{1,9},{5... | collective-permute-start | bytes 50696 | tf_op jit(solution)/shard_map/ppermute | solution.py:347
  142.1 5.5 %collective-permute-start.29 = (f32[1,4224]{1,0:T(1,128)S(1)}, f32[1,4224]{1,0:T(1,128)S(1)}, u32[]{:S(2)}, u32[]{:S(2)}) collective-permute-start(f32[1,4224]{1,0:T(1,128)S(1)} %add_add_fusion.2.refs_0_), channel_id=1, source_target_pairs={{0,16},{4,20},{8,24},{12,28},{16,0},{20,4},{24,8},{28,12},{1,17},{... | collective-permute-start | bytes 50696 | tf_op jit(solution)/shard_map/ppermute | solution.py:347
  145.9 5.5 %collective-permute-start.30 = (f32[1,4224]{1,0:T(1,128)S(1)}, f32[1,4224]{1,0:T(1,128)S(1)}, u32[]{:S(2)}, u32[]{:S(2)}) collective-permute-start(f32[1,4224]{1,0:T(1,128)S(1)} %add_add_fusion.2.refs_0_), channel_id=1, source_target_pairs={{0,24},{4,28},{8,16},{12,20},{16,8},{20,12},{24,0},{28,4},{1,25},{... | collective-permute-start | bytes 50696 | tf_op jit(solution)/shard_map/ppermute | solution.py:347
  164.5 4.8 %collective-permute-start.31 = (f16[4,2,2,64,256]{4,3,0,2,1:T(8,128)(2,1)S(1)}, f16[4,2,2,64,256]{4,3,0,2,1:T(8,128)(2,1)S(1)}, u32[]{:S(2)}, u32[]{:S(2)}) collective-permute-start(f16[4,2,2,64,256]{4,3,0,2,1:T(8,128)(2,1)S(1)} %fusion), channel_id=1, source_target_pairs={{0,1},{1,0},{2,3},{3,2},{4,5},{5,4},{6,7},{7,6},{8,9},{9,8},{10,11... | collective-permute-start | bytes 1572872 | tf_op jit(solution)/shard_map/ppermute | solution.py:350
  165.7 44.4 %all-to-all-start.1 = ((f16[8,32,2048]{2,1,0:T(8,128)(2,1)}), f16[8,32,2048]{2,1,0:T(8,128)(2,1)S(1)}, u32[]{:S(2)}, u32[]{:S(2)}) async-start(f16[8,32,2048]{2,1,0:T(8,128)(2,1)} %bitcast.20), calls=%async_computation.1 | async-start | bytes 2097152 | tf_op jit(solution)/shard_map/all_to_all | solution.py:482
  169.3 0.8 copy-start.8
  170.1 38.9 %copy-start.4 = (bf16[256,256]{1,0:T(8,128)(2,1)S(1)}, bf16[256,256]{1,0:T(8,128)(2,1)}, u32[]{:S(2)}) copy-start(bf16[256,256]{1,0:T(8,128)(2,1)} %embed_ref.1) | copy-start | bytes 393220
  170.1 38.9 %copy-start.5 = (bf16[256,256]{1,0:T(8,128)(2,1)S(1)}, bf16[256,256]{1,0:T(8,128)(2,1)}, u32[]{:S(2)}) copy-start(bf16[256,256]{1,0:T(8,128)(2,1)} %get-tuple-element.24.order_ref) | copy-start | bytes 393220
  171.5 8.3 %collective-permute-start.34 = (f16[4,64,256]{2,1,0:T(8,128)(2,1)S(1)}, f16[4,64,256]{2,1,0:T(8,128)(2,1)S(1)}, u32[]{:S(2)}, u32[]{:S(2)}) collective-permute-start(f16[4,64,256]{2,1,0:T(8,128)(2,1)S(1)} %get-tuple-element.48), channel_id=1, source_target_pairs={{0,6},{1,7},{2,4},{3,5},{4,2},{5,3},{6,0},{7,1},{8,14},{9,15},{10,... | collective-permute-start | bytes 393224 | tf_op jit(solution)/shard_map/ppermute | solution.py:357
  173.4 13.7 %collective-permute-start.33 = (f16[4,64,256]{2,1,0:T(8,128)(2,1)S(1)}, f16[4,64,256]{2,1,0:T(8,128)(2,1)S(1)}, u32[]{:S(2)}, u32[]{:S(2)}) collective-permute-start(f16[4,64,256]{2,1,0:T(8,128)(2,1)S(1)} %get-tuple-element.49), channel_id=1, source_target_pairs={{0,4},{1,5},{2,6},{3,7},{4,0},{5,1},{6,2},{7,3},{8,12},{9,13},{10,... | collective-permute-start | bytes 393224 | tf_op jit(solution)/shard_map/ppermute | solution.py:357
  173.5 13.6 %collective-permute-start.32 = (f16[4,64,256]{2,1,0:T(8,128)(2,1)S(1)}, f16[4,64,256]{2,1,0:T(8,128)(2,1)S(1)}, u32[]{:S(2)}, u32[]{:S(2)}) collective-permute-start(f16[4,64,256]{2,1,0:T(8,128)(2,1)S(1)} %get-tuple-element.47), channel_id=1, source_target_pairs={{0,2},{1,3},{2,0},{3,1},{4,6},{5,7},{6,4},{7,5},{8,10},{9,11},{10,... | collective-permute-start | bytes 393224 | tf_op jit(solution)/shard_map/ppermute | solution.py:357
  175.0 1.2 collective-permute-start.38
  176.2 16.8 %collective-permute-start.41 = (f32[8,128]{1,0:T(8,128)S(1)}, f32[8,128]{1,0:T(8,128)S(1)}, u32[]{:S(2)}, u32[]{:S(2)}) collective-permute-start(f32[8,128]{1,0:T(8,128)S(1)} %add.168), channel_id=1, source_target_pairs={{0,6},{1,7},{2,4},{3,5},{4,2},{5,3},{6,0},{7,1},{8,14},{9,15},{10,... | collective-permute-start | bytes 12296 | tf_op jit(solution)/shard_map/ppermute | solution.py:357
  178.0 15.6 %collective-permute-start.40 = (f32[8,128]{1,0:T(8,128)S(1)}, f32[8,128]{1,0:T(8,128)S(1)}, u32[]{:S(2)}, u32[]{:S(2)}) collective-permute-start(f32[8,128]{1,0:T(8,128)S(1)} %add.168), channel_id=1, source_target_pairs={{0,4},{1,5},{2,6},{3,7},{4,0},{5,1},{6,2},{7,3},{8,12},{9,13},{10,... | collective-permute-start | bytes 12296 | tf_op jit(solution)/shard_map/ppermute | solution.py:357
  179.8 13.9 %collective-permute-start.39 = (f32[8,128]{1,0:T(8,128)S(1)}, f32[8,128]{1,0:T(8,128)S(1)}, u32[]{:S(2)}, u32[]{:S(2)}) collective-permute-start(f32[8,128]{1,0:T(8,128)S(1)} %add.168), channel_id=1, source_target_pairs={{0,2},{1,3},{2,0},{3,1},{4,6},{5,7},{6,4},{7,5},{8,10},{9,11},{10,... | collective-permute-start | bytes 12296 | tf_op jit(solution)/shard_map/ppermute | solution.py:357
  187.2 10.9 %collective-permute-start.37 = (f16[64,256]{1,0:T(8,128)(2,1)S(1)}, f16[64,256]{1,0:T(8,128)(2,1)S(1)}, u32[]{:S(2)}, u32[]{:S(2)}) collective-permute-start(f16[64,256]{1,0:T(8,128)(2,1)S(1)} %get-tuple-element.51), channel_id=1, source_target_pairs={{0,24},{4,28},{8,16},{12,20},{16,8},{20,12},{24,0},{28,4},{1,25},{... | collective-permute-start | bytes 98312 | tf_op jit(solution)/shard_map/ppermute | solution.py:347
  193.0 5.8 %collective-permute-start.36 = (f16[64,256]{1,0:T(8,128)(2,1)S(1)}, f16[64,256]{1,0:T(8,128)(2,1)S(1)}, u32[]{:S(2)}, u32[]{:S(2)}) collective-permute-start(f16[64,256]{1,0:T(8,128)(2,1)S(1)} %get-tuple-element.52), channel_id=1, source_target_pairs={{0,16},{4,20},{8,24},{12,28},{16,0},{20,4},{24,8},{28,12},{1,17},{... | collective-permute-start | bytes 98312 | tf_op jit(solution)/shard_map/ppermute | solution.py:347
  193.0 5.8 %collective-permute-start.35 = (f16[64,256]{1,0:T(8,128)(2,1)S(1)}, f16[64,256]{1,0:T(8,128)(2,1)S(1)}, u32[]{:S(2)}, u32[]{:S(2)}) collective-permute-start(f16[64,256]{1,0:T(8,128)(2,1)S(1)} %get-tuple-element.50), channel_id=1, source_target_pairs={{0,8},{4,12},{8,0},{12,4},{16,24},{20,28},{24,16},{28,20},{1,9},{5... | collective-permute-start | bytes 98312 | tf_op jit(solution)/shard_map/ppermute | solution.py:347
  193.7 5.2 %collective-permute-start.42 = (f32[8,128]{1,0:T(8,128)S(1)}, f32[8,128]{1,0:T(8,128)S(1)}, u32[]{:S(2)}, u32[]{:S(2)}) collective-permute-start(f32[8,128]{1,0:T(8,128)S(1)} %add_add_fusion.3.refs_4_), channel_id=1, source_target_pairs={{0,8},{4,12},{8,0},{12,4},{16,24},{20,28},{24,16},{28,20},{1,9},{5... | collective-permute-start | bytes 12296 | tf_op jit(solution)/shard_map/ppermute | solution.py:347
  195.1 4.5 %collective-permute-start.43 = (f32[8,128]{1,0:T(8,128)S(1)}, f32[8,128]{1,0:T(8,128)S(1)}, u32[]{:S(2)}, u32[]{:S(2)}) collective-permute-start(f32[8,128]{1,0:T(8,128)S(1)} %add_add_fusion.3.refs_4_), channel_id=1, source_target_pairs={{0,16},{4,20},{8,24},{12,28},{16,0},{20,4},{24,8},{28,12},{1,17},{... | collective-permute-start | bytes 12296 | tf_op jit(solution)/shard_map/ppermute | solution.py:347
  198.1 5.4 %collective-permute-start.44 = (f32[8,128]{1,0:T(8,128)S(1)}, f32[8,128]{1,0:T(8,128)S(1)}, u32[]{:S(2)}, u32[]{:S(2)}) collective-permute-start(f32[8,128]{1,0:T(8,128)S(1)} %add_add_fusion.3.refs_4_), channel_id=1, source_target_pairs={{0,24},{4,28},{8,16},{12,20},{16,8},{20,12},{24,0},{28,4},{1,25},{... | collective-permute-start | bytes 12296 | tf_op jit(solution)/shard_map/ppermute | solution.py:347
  203.5 1.9 collective-permute-start.45
  203.5 4.9 %collective-permute-start.46 = (f32[64,256]{1,0:T(8,128)S(1)}, f32[64,256]{1,0:T(8,128)S(1)}, u32[]{:S(2)}, u32[]{:S(2)}) collective-permute-start(f32[64,256]{1,0:T(8,128)S(1)} %fusion.7.refs_0_), channel_id=1, source_target_pairs={{0,2},{1,3},{2,0},{3,1},{4,6},{5,7},{6,4},{7,5},{8,10},{9,11},{10,... | collective-permute-start | bytes 196616 | tf_op jit(solution)/shard_map/ppermute | solution.py:350
  204.0 5.0 %collective-permute-start.47 = (f32[64,256]{1,0:T(8,128)S(1)}, f32[64,256]{1,0:T(8,128)S(1)}, u32[]{:S(2)}, u32[]{:S(2)}) collective-permute-start(f32[64,256]{1,0:T(8,128)S(1)} %fusion.7.refs_0_), channel_id=1, source_target_pairs={{0,3},{1,2},{2,1},{3,0},{4,7},{5,6},{6,5},{7,4},{8,11},{9,10},{10,... | collective-permute-start | bytes 196616 | tf_op jit(solution)/shard_map/ppermute | solution.py:350
  (2 other events, 1.6 us)

commit v3 on v2

--- a/solution.py
+++ b/solution.py
@@ -94,10 +94,26 @@
     ].astype(bf16)
 
 
-def row_sums(column, total_batch, queue_blocks, mass_ref, out_ref):
+def row_sums(column, total_batch, queue_blocks, mass_ref, out_ref, wide=None):
+    head = wide or BLOCK // 4
+    width = mass_ref.shape[1]
+    step = 128
+    factor = column[0:1]
+    ones = jnp.ones((8, 128), bf16)
+
     def one(index, carry):
         start = pl.multiple_of(index * BLOCK, BLOCK)
-        out_ref[0:1, pl.ds(start, BLOCK)] = sum_terms(dot_nt(column, mass_ref[pl.ds(start, BLOCK), :]))
+        out_ref[0:1, pl.ds(start, head)] = sum_terms(dot_nt(column, mass_ref[pl.ds(start, head), :]))
+        for rows in range(head, BLOCK, step):
+            here = pl.ds(pl.multiple_of(start + rows, step), step)
+            total = None
+            for low in range(0, width, 256):
+                pair = mass_ref[here, low : low + 128] * factor[:, low : low + 128]
+                pair += mass_ref[here, low + 128 : low + 256] * factor[:, low + 128 : low + 256]
+                total = pair.astype(f32) if total is None else total + pair.astype(f32)
+            high = total.astype(bf16)
+            low = (total - high.astype(f32)).astype(bf16)
+            out_ref[0:1, here] = (dot_nt(ones, high) + dot_nt(ones, low))[0:1]
         return carry
 
     lax.fori_loop(0, total_batch // BLOCK + queue_blocks, one, 0)
@@ -204,7 +220,7 @@
     lax.fori_loop(0, total_batch // BLOCK + live_blocks(fill), finish, 0)
 
 
-def column_factor(fill, total_batch, parts, mass_ref, scale_ref, col_ref, ready=None):
+def column_factor(fill, total_batch, parts, mass_ref, scale_ref, col_ref, spare_ref, make=None, ready=None):
     total_rows = mass_ref.shape[0]
     total = parts[0][0:1, 0:total_rows]
     for part in parts[1:]:
@@ -213,46 +229,74 @@
     scale = jnp.where(place < total_batch + fill, 1.0 / total, 0.0)
     scale_ref[...] = term_rows(scale)
     col_ref[...] = jnp.zeros_like(col_ref)
-
-    def one(index, carry):
+    spare_ref[...] = jnp.zeros_like(spare_ref)
+
+    head = 3 * BLOCK // 4
+
+    def add(index):
+        start = pl.multiple_of(index * BLOCK, BLOCK)
+        rows, rest = pl.ds(start, head), pl.ds(pl.multiple_of(start + head, 128), BLOCK - head)
+        col_ref[...] += jnp.dot(scale_ref[:, rows], mass_ref[rows, :], preferred_element_type=f32)
+        high, middle, low = (scale_ref[i : i + 1, rest].astype(f32) for i in range(3))
+        factor = jnp.transpose(jnp.broadcast_to(high + middle + low, (128, BLOCK - head)), (1, 0))
+        for low in range(0, mass_ref.shape[1], 128):
+            part = mass_ref[rest, low : low + 128].astype(f32) * factor
+            spare_ref[:, low : low + 128] += jnp.sum(part.reshape((BLOCK - head) // 8, 8, 128), axis=0)
+
+    def crops(index, carry):
+        if make is not None:
+            make(index)
+        add(index)
+        return carry
+
+    def queue(index, carry):
         if ready is not None:
             ready(index)
-        rows = pl.ds(pl.multiple_of(index * BLOCK, BLOCK), BLOCK)
-        col_ref[...] += jnp.dot(scale_ref[:, rows], mass_ref[rows, :], preferred_element_type=f32)
-        return carry
-
-    lax.fori_loop(0, total_batch // BLOCK + live_blocks(fill), one, 0)
-    return 1.0 / sum_terms(col_ref[...])
-
-
-def sweep_kernel(total_batch, fill_ref, mass_in, *refs):
-    *parts, sums_ref, mass_ref, scale_ref, col_ref, sems = refs
+        add(total_batch // BLOCK + index)
+        return carry
+
+    lax.fori_loop(0, total_batch // BLOCK, crops, 0)
+    lax.fori_loop(0, live_blocks(fill), queue, 0)
+    return 1.0 / (sum_terms(col_ref[...]) + jnp.sum(spare_ref[...], axis=0, keepdims=True))
+
+
+def sweep_kernel(total_batch, fill_ref, mass_in, batch_ref, columns_ref, *refs):
+    *parts, sums_ref, mass_ref, scale_ref, col_ref, spare_ref, sems = refs
     fill = fill_ref[0]
-    blocks = total_batch // BLOCK + live_blocks(fill)
+    width = columns_ref.shape[1]
 
     def fetch(index):
-        rows = pl.ds(pl.multiple_of(index * BLOCK, BLOCK), BLOCK)
+        rows = pl.ds(pl.multiple_of(total_batch + index * BLOCK, BLOCK), BLOCK)
         return pltpu.make_async_copy(mass_in.at[rows, :], mass_ref.at[rows, :], sems.at[index])
 
     def start(index, carry):
         fetch(index).start()
         return carry
 
-    lax.fori_loop(0, blocks, start, 0)
+    lax.fori_loop(0, live_blocks(fill), start, 0)
+
+    def make(index):
+        rows = pl.ds(pl.multiple_of(index * BLOCK, BLOCK), BLOCK)
+        crops = batch_ref[rows, :]
+        for low in range(0, width, WIDE):
+            scores = jnp.dot(crops, columns_ref[:, low : low + WIDE], preferred_element_type=f32)
+            soft = jnp.exp2(scores * SOFT_SCALE)
+            mass_ref[rows, low : low + WIDE] = (soft * soft).astype(bf16)
+
     column = column_factor(
-        fill, total_batch, parts, mass_ref, scale_ref, col_ref, lambda index: fetch(index).wait()
+        fill, total_batch, parts, mass_ref, scale_ref, col_ref, spare_ref, make, lambda index: fetch(index).wait()
     )
     sums_ref[...] = jnp.zeros_like(sums_ref)
     row_sums(term_rows(column), total_batch, live_blocks(fill), mass_ref, sums_ref)
 
 
 def last_kernel(total_batch, fill_ref, side_ref, mass_ref, *refs):
-    *parts, sums_ref, column_ref, scale_ref, col_ref = refs
+    *parts, sums_ref, column_ref, scale_ref, col_ref, spare_ref = refs
     fill = fill_ref[0]
-    column = column_factor(fill, total_batch, parts, mass_ref, scale_ref, col_ref)
+    column = column_factor(fill, total_batch, parts, mass_ref, scale_ref, col_ref, spare_ref)
     column_ref[...] = column
     sums_ref[0:1, total_batch:] = side_ref[...]
-    row_sums(term_rows(column), total_batch, 0, mass_ref, sums_ref)
+    row_sums(term_rows(column), total_batch, 0, mass_ref, sums_ref, BLOCK)
 
 
 def slope_kernel(crop_count, first, last, batch_ref, columns_ref, column_ref, *refs):
@@ -310,6 +354,15 @@
 
     lax.fori_loop(0, total_batch // rows, one, 0)
 
+    loss = jnp.maximum(jnp.sum(loss_ref[...]), 1e-30)
+    exponent = jnp.floor(jnp.log2(jnp.full((1, 128), loss, f32)))
+    mantissa = loss / jnp.exp2(exponent)
+    high = jnp.floor(mantissa * 1024.0) / 1024.0
+    lane = lax.broadcasted_iota(jnp.int32, (1, 128), 1)
+    loss_ref[...] = jnp.broadcast_to(
+        jnp.where(lane == 0, exponent, jnp.where(lane == 1, high, (mantissa - high) * 2048.0)), (8, 128)
+    )
+
     def kept(index, carry):
         keep(index).wait()
         return carry
@@ -317,17 +370,16 @@
     lax.fori_loop(0, total_batch // rows, kept, 0)
 
 
-def finish_kernel(piece_count, total_batch, proto_ref, embed_ref, order_ref, back_ref, *refs):
-    *parts, out_ref, loss_ref, sorted_ref = refs
-    pieces, losses = parts[:piece_count], parts[piece_count:]
+def finish_kernel(piece_count, proto_ref, embed_ref, order_ref, back_ref, *refs):
+    *pieces, out_ref, loss_ref, sorted_ref = refs
     rows = embed_ref.shape[0]
     size = rows // piece_count
     proto = proto_ref[0]
     for index, piece in enumerate(pieces):
         other = proto ^ index
         place = (other % 2) * (piece_count // 2) + other // 2
-        sorted_ref[pl.ds(pl.multiple_of(place * size, size), size), :] = piece[...]
-    loss_ref[0] = jnp.sum(functools.reduce(jnp.add, [loss[...] for loss in losses])) / total_batch
+        sorted_ref[pl.ds(pl.multiple_of(place * size, size), size), :] = piece[0:size, :]
+    loss_ref[0] = jnp.max(functools.reduce(jnp.add, [piece[size:, 0:128] for piece in pieces]))
     order = order_ref[...]
     high, middle, low = bf16_terms(sorted_ref[...])
     grad = dot_tn(order, high) + dot_tn(order, middle) + dot_tn(order, low)
@@ -428,18 +480,18 @@
             compiler_params=limit(56),
         )(place, fill_count, columns, *units)
 
-        vectors = [pltpu.VMEM((8, total_rows), bf16), pltpu.VMEM((8, width), f32)]
+        vectors = [pltpu.VMEM((8, total_rows), bf16), pltpu.VMEM((8, width), f32), pltpu.VMEM((8, width), f32)]
         sums = pl.pallas_call(
             functools.partial(sweep_kernel, total_batch),
             name="sweep",
             out_shape=jax.ShapeDtypeStruct((1, total_rows), f32),
-            in_specs=[SMEM, ANY] + [VMEM] * z_count,
+            in_specs=[SMEM, ANY] + [VMEM] * (2 + z_count),
             out_specs=VMEM,
             scratch_shapes=[pltpu.VMEM((total_rows, width), bf16)]
             + vectors
-            + [pltpu.SemaphoreType.DMA((total_rows // BLOCK,))],
+            + [pltpu.SemaphoreType.DMA((total_queue // BLOCK,))],
             compiler_params=limit(30),
-        )(fill_count, mass, *all_sum_parts(sums))
+        )(fill_count, mass, batch, columns, *all_sum_parts(sums))
 
         code_sums, column = pl.pallas_call(
             functools.partial(last_kernel, total_batch),
@@ -490,39 +542,39 @@
         pieces = normed_part.reshape(z_count, y_count, 2, x_count, size, feat)
 
         away = shift_proto(pick(pieces, 1 - core, 2).astype(f16), 1)
-        loss = loss + shift_proto(loss, 1)
         kept = pick(pieces, core, 2) + away.astype(f32)
-        total, losses = None, None
+        total = None
         for dy in range(y_count):
             for dx in range(x_count):
-                part, other = pick(pick(kept, x ^ dx, 2), y ^ dy, 1), loss
+                part = pick(pick(kept, x ^ dx, 2), y ^ dy, 1)
                 if dx or dy:
                     part = shift_xy(part.astype(f16), dx, dy).astype(f32)
-                    other = shift_xy(loss, dx, dy)
                 total = part if total is None else total + part
-                losses = other if losses is None else losses + other
-        piece = pick(total, z, 0)
-        loss_parts = [losses]
-        for dz in range(1, z_count):
-            piece = piece + shift_row(pick(total, z ^ dz, 0).astype(f16), dz, 0).astype(f32)
-            loss_parts.append(shift_row(losses, dz, 0))
-        piece, *loss_parts = lax.optimization_barrier((piece, *loss_parts))
-        grad_proto = exchange(as_blocks(grad_columns)).astype(f32)
+        arriving = [shift_row(pick(total, z ^ dz, 0).astype(f16), dz, 0) for dz in range(1, z_count)]
+
+        sent = jnp.concatenate([as_blocks(grad_columns), jnp.broadcast_to(loss[0:1].astype(f16), (row_count, feat // row_count, 128))], axis=2)
+        got = exchange(sent)
+        grad_proto = got[:, :, :width].astype(f32)
         grad_proto = grad_proto.transpose(1, 0, 2).reshape(feat // row_count, row_count * width)
+        code = got[:, 0, width:].astype(f32)
+        losses = jnp.sum((code[:, 1] + code[:, 2] / 2048.0) * jnp.exp2(code[:, 0])) / total_batch
+        *arriving, losses = lax.optimization_barrier((*arriving, losses))
+        piece = functools.reduce(jnp.add, [part.astype(f32) for part in arriving], pick(total, z, 0))
+        piece = jnp.concatenate([piece, jnp.full((8, feat), losses, f32)], axis=0)
 
         gathered = [piece] + [shift_proto(piece, k) for k in range(1, proto_count)]
         grad_embed, loss = pl.pallas_call(
-            functools.partial(finish_kernel, proto_count, total_batch),
+            functools.partial(finish_kernel, proto_count),
             name="finish",
             out_shape=[
                 jax.ShapeDtypeStruct((batch_rows, feat), f32),
                 jax.ShapeDtypeStruct((1,), f32),
             ],
-            in_specs=[SMEM] + [VMEM] * (3 + proto_count + z_count),
+            in_specs=[SMEM] + [VMEM] * (3 + proto_count),
             out_specs=[VMEM, SMEM],
             scratch_shapes=[pltpu.VMEM((batch_rows, feat), f32)],
             compiler_params=limit(8),
-        )(proto.reshape(1).astype(jnp.int32), embeddings, order, back, *gathered, *loss_parts)
+        )(proto.reshape(1).astype(jnp.int32), embeddings, order, back, *gathered)
         return grad_embed, grad_proto, loss
 
     placed = (P("row", None), P("row", None), P("row", "proto"), P("row"), P())

time: 209 us -> 198 us (0.947); the launches traced: 212 us -> 195 us
  Pallas kernels: 63 us -> 50.3 us
  starting transfers between devices: 64.1 us -> 55.3 us
  local copies, waits for them, and re-layouts: 6.49 us -> 9.95 us
    pallas_call x1, Pallas kernels: 16.4 us -> 9.9 us  [body(): pl.pallas_call(functools.partial(sweep_kernel, total_batch), name='sweep'...]
    ppermute x19 -> x16, starting transfers between devices: 33.1 us -> 26.8 us  [shift_row(): lax.ppermute(values, 'row', [(i, i ^ offset) for i in range(row_count)])]
    pallas_call x1, Pallas kernels: 23.4 us -> 18.1 us  [body(): pl.pallas_call(functools.partial(make_kernel, offsets, share, total_batch...]
    ppermute x19 -> x16, waiting for transfers between devices: 40.5 us -> 37.9 us  [shift_row(): lax.ppermute(values, 'row', [(i, i ^ offset) for i in range(row_count)])]
    ppermute x15 -> x12, starting transfers between devices: 16.8 us -> 14.2 us  [shift_xy(): return lax.ppermute(values, ('row', 'proto'), pairs)]
    unnamed x32 -> x36, local copies, waits for them, and re-layouts: 2.57 us -> 4.99 us
    all_to_all x1, waiting for transfers between devices: 0.01 us -> 2.37 us  [exchange(): lax.all_to_all(blocks, 'row', split_axis=0, concat_axis=0, tiled=True)]
    ppermute x14 -> x13, waiting for transfers between devices: 14.4 us -> 13.7 us  [shift_proto(): lax.ppermute(values, 'proto', [(i, i ^ offset) for i in range(proto_count)])]
  transfers between devices with their start and end apart: 50 -> 43, of which waited for: 29 -> 30; matrix products, arithmetic and copies ran while one was open for 2% -> 4% of each run, Pallas kernels for 1% -> 0%
where the time goes in v3:
time: 198 us; the launch traced here: 195 us
  waiting for transfers between devices  71.8 us (36%)
  starting transfers between devices  55.3 us (28%)
  Pallas kernels  50.3 us (25%)
  local copies, waits for them, and re-layouts  9.95 us (5%)
  other arithmetic  5.39 us (3%)
  between operations  2.53 us (1%)
    ppermute x16, waiting for transfers between devices, shift_row(): lax.ppermute(values, 'row', [(i, i ^ offset) for i in range(row_count)])  37.9 us
    ppermute x16, starting transfers between devices, shift_row(): lax.ppermute(values, 'row', [(i, i ^ offset) for i in range(row_count)])  26.8 us
    pallas_call x1, Pallas kernels, body(): pl.pallas_call(functools.partial(make_kernel, offsets, share, total_batch...  18.1 us
    ppermute x12, waiting for transfers between devices, shift_xy(): return lax.ppermute(values, ('row', 'proto'), pairs)  17.8 us
    ppermute x12, starting transfers between devices, shift_xy(): return lax.ppermute(values, ('row', 'proto'), pairs)  14.2 us
    ppermute x13, waiting for transfers between devices, shift_proto(): lax.ppermute(values, 'proto', [(i, i ^ offset) for i in range(proto_count)])  13.7 us
    pallas_call x1, Pallas kernels, slopes(): pl.pallas_call(functools.partial(slope_kernel, CROPS, first, last), name=...  12.9 us
    pallas_call x1, Pallas kernels, body(): pl.pallas_call(functools.partial(sweep_kernel, total_batch), name='sweep'...  9.9 us
  transfers between devices with their start and end apart: 43, of which 30 were waited for; matrix products, arithmetic and copies ran while one was open for 4% of the time, Pallas kernels for 0%

profile of v3, /device:TPU:0, one launch (start us, length us, event | category | flops | bytes accessed | tf_op | source)
XLA Modules:
  0.0 195.2 jit_solution(11168344794877703115)
XLA Ops:
  1.2 2.6 %prep.1 = (bf16[192,256]{1,0:T(8,128)(2,1)}, bf16[256,256]{1,0:T(8,128)(2,1)}) custom-call(s32[2]{0:T(128)} %pad_add_fusion.place_ref, s32[1,256]{1,0:T(1,128)} %bitcast.64, bf16[256,256]{1,0:T(8,128)(2,1)} %embed_ref.1, bf16[512,256]{1,0:T(8,128)(2,1)} %queue_in.1), custom_call_target="tpu_custom_call" | custom-call | tf_op jit(solution)/shard_map/prep/pallas_call | solution.py:429
  3.9 5.1 %collective-permute-start.2 = (bf16[192,256]{1,0:T(8,128)(2,1)}, bf16[192,256]{1,0:T(8,128)(2,1)S(1)}, u32[]{:S(2)}, u32[]{:S(2)}) collective-permute-start(bf16[192,256]{1,0:T(8,128)(2,1)} %get-tuple-element.24), channel_id=1, source_target_pairs={{0,24},{4,28},{8,16},{12,20},{16,8},{20,12},{24,0},{28,4},{1,25},{... | collective-permute-start | bytes 294920 | tf_op jit(solution)/shard_map/ppermute | solution.py:399
  9.7 2.3 %copy.22 = bf16[4,8,8,2048]{3,2,0,1:T(8,128)(2,1)} copy(bf16[4,8,8,2048]{3,2,1,0:T(8,128)(2,1)} %bitcast.58) | data formatting | bytes 2097152 | tf_op jit(solution)/shard_map/reshape | solution.py:450
  12.0 1.0 collective-permute-done.2
  12.9 4.6 %collective-permute-done.1 = bf16[192,256]{1,0:T(8,128)(2,1)S(1)} collective-permute-done((bf16[192,256]{1,0:T(8,128)(2,1)}, bf16[192,256]{1,0:T(8,128)(2,1)S(1)}, u32[]{:S(2)}, u32[]{:S(2)}) %collective-permute-start.1) | collective-permute-done | bytes 98336 | tf_op jit(solution)/shard_map/ppermute | solution.py:399
  17.6 4.8 %all-to-all-start = ((bf16[8,32,2048]{2,1,0:T(8,128)(2,1)}), bf16[8,32,2048]{2,1,0:T(8,128)(2,1)S(1)}, u32[]{:S(2)}, u32[]{:S(2)}) async-start(bf16[8,32,2048]{2,1,0:T(8,128)(2,1)} %bitcast.51), calls=%async_computation | async-start | bytes 2097152 | tf_op jit(solution)/shard_map/all_to_all | solution.py:452
  22.3 2.0 %collective-permute-start.6 = (bf16[4,192,256]{2,1,0:T(8,128)(2,1)S(1)}, bf16[4,192,256]{2,1,0:T(8,128)(2,1)S(1)}, u32[]{:S(2)}, u32[]{:S(2)}) collective-permute-start(bf16[4,192,256]{2,1,0:T(8,128)(2,1)S(1)} %pad_maximum_fusion.1.refs_0_), channel_id=1, source_target_pairs={{0,4},{4,0},{8,12},{12,8},{16,20},{20,16},{24,28},{28,24},{1,5},{5... | collective-permute-start | bytes 1179656 | tf_op jit(solution)/shard_map/ppermute | solution.py:399
  24.4 1.5 collective-permute-start.4
  25.8 17.4 %collective-permute-done.6.refs_4_ = bf16[4,192,256]{2,1,0:T(8,128)(2,1)S(1)} collective-permute-done((bf16[4,192,256]{2,1,0:T(8,128)(2,1)S(1)}, bf16[4,192,256]{2,1,0:T(8,128)(2,1)S(1)}, u32[]{:S(2)}, u32[]{:S(2)}) %collective-permute-start.6) | collective-permute-done | bytes 393248 | tf_op jit(solution)/shard_map/ppermute | solution.py:399
  43.2 1.5 collective-permute-start.8
  45.3 5.7 %collective-permute-done.8.refs_6_ = bf16[4,192,256]{2,1,0:T(8,128)(2,1)S(1)} collective-permute-done((bf16[4,192,256]{2,1,0:T(8,128)(2,1)S(1)}, bf16[4,192,256]{2,1,0:T(8,128)(2,1)S(1)}, u32[]{:S(2)}, u32[]{:S(2)}) %collective-permute-start.8) | collective-permute-done | bytes 393248 | tf_op jit(solution)/shard_map/ppermute | solution.py:402
  51.7 0.8 copy-done.16
  53.8 18.1 %make_mass.1 = (bf16[6144,2048]{1,0:T(8,128)(2,1)}, f32[1,6144]{1,0:T(1,128)}, f32[1,2176]{1,0:T(1,128)}, bf16[2048,256]{1,0:T(8,128)(2,1)}) custom-call(s32[2]{0:T(128)} %pad_add_fusion.place_ref, s32[1]{0:T(128)S(6)} %copy.23.fill_ref, bf16[256,2048]{1,0:T(8,128)(2,1)} %bitcast.52, bf16[4,192,256]{2,1,0:T(8,128)(2,1)} %copy-done.9, ...), custom_call_target="tpu_custom_call" | custom-call | tf_op jit(solution)/shard_map/make_mass/pallas_call | solution.py:462
  72.3 1.2 collective-permute-done.10
  73.5 0.8 add.131
  74.2 1.8 collective-permute-start.13
  76.1 1.1 collective-permute-start.12
  77.8 1.3 collective-permute-done.13
  79.1 0.8 collective-permute-done.12
  79.9 1.1 collective-permute-done.11
  81.1 2.4 %collective-permute-start.14 = (f32[1,6144]{1,0:T(1,128)S(1)}, f32[1,6144]{1,0:T(1,128)S(1)}, u32[]{:S(2)}, u32[]{:S(2)}) collective-permute-start(f32[1,6144]{1,0:T(1,128)S(1)} %add_add_fusion.1.refs_0_), channel_id=1, source_target_pairs={{0,8},{4,12},{8,0},{12,4},{16,24},{20,28},{24,16},{28,20},{1,9},{5... | collective-permute-start | bytes 73736 | tf_op jit(solution)/shard_map/ppermute | solution.py:399
  83.5 2.5 %collective-permute-start.15 = (f32[1,6144]{1,0:T(1,128)S(1)}, f32[1,6144]{1,0:T(1,128)S(1)}, u32[]{:S(2)}, u32[]{:S(2)}) collective-permute-start(f32[1,6144]{1,0:T(1,128)S(1)} %add_add_fusion.1.refs_0_), channel_id=1, source_target_pairs={{0,16},{4,20},{8,24},{12,28},{16,0},{20,4},{24,8},{28,12},{1,17},{... | collective-permute-start | bytes 73736 | tf_op jit(solution)/shard_map/ppermute | solution.py:399
  85.9 2.3 %collective-permute-done.15.refs_2_ = f32[1,6144]{1,0:T(1,128)S(1)} collective-permute-done((f32[1,6144]{1,0:T(1,128)S(1)}, f32[1,6144]{1,0:T(1,128)S(1)}, u32[]{:S(2)}, u32[]{:S(2)}) %collective-permute-start.15) | collective-permute-done | bytes 24608 | tf_op jit(solution)/shard_map/ppermute | solution.py:399
  88.2 3.3 %collective-permute-done.16.refs_3_ = f32[1,6144]{1,0:T(1,128)S(1)} collective-permute-done((f32[1,6144]{1,0:T(1,128)S(1)}, f32[1,6144]{1,0:T(1,128)S(1)}, u32[]{:S(2)}, u32[]{:S(2)}) %collective-permute-start.16) | collective-permute-done | bytes 24608 | tf_op jit(solution)/shard_map/ppermute | solution.py:399
  91.6 1.2 copy-done.2
  92.8 1.2 copy-done.4
  94.0 9.9 %sweep.1 = f32[1,6144]{1,0:T(1,128)S(1)} custom-call(s32[1]{0:T(128)S(6)} %copy.23.fill_ref, bf16[6144,2048]{1,0:T(8,128)(2,1)} %get-tuple-element.29.mass_in.mass_ref, bf16[2048,256]{1,0:T(8,128)(2,1)S(1)} %copy-done.4, bf16[256,2048]{1,0:T(8,128)(2,1)S(1)} %bitcast.53, f32[1,6144]{1,0:T(1,128)S(1)} %add_add_fusion.1.refs_0_, ...), custom_call_target="tpu_custom_call" | custom-call | tf_op jit(solution)/shard_map/sweep/pallas_call | solution.py:484
  104.0 1.2 collective-permute-done.17
  105.2 0.9 collective-permute-start.20
  106.2 1.1 collective-permute-start.19
  107.3 1.5 collective-permute-start.18
  108.8 1.4 collective-permute-done.20
  110.3 0.9 collective-permute-done.18
  111.2 0.8 collective-permute-start.22
  112.1 3.6 %collective-permute-start.23 = (f32[1,6144]{1,0:T(1,128)S(1)}, f32[1,6144]{1,0:T(1,128)S(1)}, u32[]{:S(2)}, u32[]{:S(2)}) collective-permute-start(f32[1,6144]{1,0:T(1,128)S(1)} %add_add_fusion.refs_0_), channel_id=1, source_target_pairs={{0,24},{4,28},{8,16},{12,20},{16,8},{20,12},{24,0},{28,4},{1,25},{... | collective-permute-start | bytes 73736 | tf_op jit(solution)/shard_map/ppermute | solution.py:399
  116.0 1.7 collective-permute-done.23.refs_3_
  117.7 5.6 %last_sweep.1 = (f32[1,4224]{1,0:T(1,128)S(1)}, f32[1,2048]{1,0:T(1,128)S(1)}) custom-call(s32[1]{0:T(128)S(6)} %copy.23.fill_ref, f32[1,2176]{1,0:T(1,128)S(1)} %copy-done.7, bf16[6144,2048]{1,0:T(8,128)(2,1)S(1)} %copy-done, f32[1,6144]{1,0:T(1,128)S(1)} %add_add_fusion.refs_0_, f32[1,6144]{1,0:T(1,128)S(1)} %collective-permute-done.21.refs_1_, ...), custom_call_target="tpu_custom_call" | custom-call | tf_op jit(solution)/shard_map/last_sweep/pallas_call | solution.py:496
  123.4 1.2 collective-permute-done.24
  124.6 2.7 %collective-permute-start.27 = (f32[1,4224]{1,0:T(1,128)S(1)}, f32[1,4224]{1,0:T(1,128)S(1)}, u32[]{:S(2)}, u32[]{:S(2)}) collective-permute-start(f32[1,4224]{1,0:T(1,128)S(1)} %add.139), channel_id=1, source_target_pairs={{0,6},{1,7},{2,4},{3,5},{4,2},{5,3},{6,0},{7,1},{8,14},{9,15},{10,... | collective-permute-start | bytes 50696 | tf_op jit(solution)/shard_map/ppermute | solution.py:409
  128.1 1.2 collective-permute-done.27
  129.3 1.8 collective-permute-done.26
  131.7 3.8 %collective-permute-start.29 = (f32[1,4224]{1,0:T(1,128)S(1)}, f32[1,4224]{1,0:T(1,128)S(1)}, u32[]{:S(2)}, u32[]{:S(2)}) collective-permute-start(f32[1,4224]{1,0:T(1,128)S(1)} %add_add_fusion.2.refs_0_), channel_id=1, source_target_pairs={{0,16},{4,20},{8,24},{12,28},{16,0},{20,4},{24,8},{28,12},{1,17},{... | collective-permute-start | bytes 50696 | tf_op jit(solution)/shard_map/ppermute | solution.py:399
  135.8 1.4 collective-permute-done.29.refs_2_
  137.3 3.8 %collective-permute-done.30.refs_3_ = f32[1,4224]{1,0:T(1,128)S(1)} collective-permute-done((f32[1,4224]{1,0:T(1,128)S(1)}, f32[1,4224]{1,0:T(1,128)S(1)}, u32[]{:S(2)}, u32[]{:S(2)}) %collective-permute-start.30) | collective-permute-done | bytes 16928 | tf_op jit(solution)/shard_map/ppermute | solution.py:399
  141.1 12.9 %slopes.1 = (f32[2048,256]{1,0:T(8,128)S(1)}, f32[256,2048]{1,0:T(8,128)S(1)}, f32[8,128]{1,0:T(8,128)S(1)}, f32[8,128]{1,0:T(8,128)S(1)}) custom-call(bf16[2048,256]{1,0:T(8,128)(2,1)S(1)} %copy-done.4, bf16[256,2048]{1,0:T(8,128)(2,1)S(1)} %bitcast.54, f32[1,2048]{1,0:T(1,128)S(1)} %get-tuple-element.31.column_ref, f32[1,4224]{1,0:T(1,128)S(1)} %add_add_fusion.2.refs_0_, ...), custom_call_target="tpu_custom_call" | custom-call | tf_op jit(solution)/shard_map/slopes/pallas_call | solution.py:512
  154.2 1.3 pad_maximum_fusion
  155.4 3.6 %all-to-all-start.1 = ((f16[8,32,2176]{2,1,0:T(8,128)(2,1)}), f16[8,32,2176]{2,1,0:T(8,128)(2,1)S(1)}, u32[]{:S(2)}, u32[]{:S(2)}) async-start(f16[8,32,2176]{2,1,0:T(8,128)(2,1)} %pad_maximum_fusion), calls=%async_computation.1 | async-start | bytes 2228224 | tf_op jit(solution)/shard_map/all_to_all | solution.py:534
  159.0 1.2 constant_dynamic-slice_fusion
  160.4 1.8 collective-permute-done.31
  162.2 0.8 copy-done.10
  163.0 1.2 bitcast_add_fusion
  164.3 1.9 collective-permute-start.34
  166.4 1.5 collective-permute-start.32
  167.9 6.1 %collective-permute-done.34 = f16[4,64,256]{2,1,0:T(8,128)(2,1)S(1)} collective-permute-done((f16[4,64,256]{2,1,0:T(8,128)(2,1)S(1)}, f16[4,64,256]{2,1,0:T(8,128)(2,1)S(1)}, u32[]{:S(2)}, u32[]{:S(2)}) %collective-permute-start.34) | collective-permute-done | bytes 131104 | tf_op jit(solution)/shard_map/ppermute | solution.py:409
  173.9 3.0 %collective-permute-done.33 = f16[4,64,256]{2,1,0:T(8,128)(2,1)S(1)} collective-permute-done((f16[4,64,256]{2,1,0:T(8,128)(2,1)S(1)}, f16[4,64,256]{2,1,0:T(8,128)(2,1)S(1)}, u32[]{:S(2)}, u32[]{:S(2)}) %collective-permute-start.33) | collective-permute-done | bytes 131104 | tf_op jit(solution)/shard_map/ppermute | solution.py:409
  177.0 1.6 collective-permute-start.35
  178.6 3.7 %collective-permute-start.36 = (f16[64,256]{1,0:T(8,128)(2,1)S(1)}, f16[64,256]{1,0:T(8,128)(2,1)S(1)}, u32[]{:S(2)}, u32[]{:S(2)}) collective-permute-start(f16[64,256]{1,0:T(8,128)(2,1)S(1)} %get-tuple-element.49), channel_id=1, source_target_pairs={{0,16},{4,20},{8,24},{12,28},{16,0},{20,4},{24,8},{28,12},{1,17},{... | collective-permute-start | bytes 98312 | tf_op jit(solution)/shard_map/ppermute | solution.py:399
  182.3 2.4 %all-to-all-done.1 = f16[8,32,2176]{2,1,0:T(8,128)(2,1)S(1)} async-done(((f16[8,32,2176]{2,1,0:T(8,128)(2,1)}), f16[8,32,2176]{2,1,0:T(8,128)(2,1)S(1)}, u32[]{:S(2)}, u32[]{:S(2)}) %all-to-all-start.1) | async-done | bytes 1114144 | tf_op jit(solution)/shard_map/all_to_all | solution.py:534
  186.0 2.0 %collective-permute-done.37 = f16[64,256]{1,0:T(8,128)(2,1)S(1)} collective-permute-done((f16[64,256]{1,0:T(8,128)(2,1)S(1)}, f16[64,256]{1,0:T(8,128)(2,1)S(1)}, u32[]{:S(2)}, u32[]{:S(2)}) %collective-permute-start.37) | collective-permute-done | bytes 32800 | tf_op jit(solution)/shard_map/ppermute | solution.py:399
  188.1 0.7 collective-permute-start.39
  188.9 1.1 collective-permute-start.40
  190.2 1.5 copy.16
  191.7 1.5 collective-permute-done.39.refs_2_
  193.9 1.1 finish.1
  (90 shorter events, 9.0 us)
Async XLA Ops:
  3.9 13.6 %copy-start.17 = (bf16[192,256]{1,0:T(8,128)(2,1)S(1)}, bf16[192,256]{1,0:T(8,128)(2,1)}, u32[]{:S(2)}) copy-start(bf16[192,256]{1,0:T(8,128)(2,1)} %get-tuple-element.24) | copy-start | bytes 294916
  3.9 9.0 %collective-permute-start.2 = (bf16[192,256]{1,0:T(8,128)(2,1)}, bf16[192,256]{1,0:T(8,128)(2,1)S(1)}, u32[]{:S(2)}, u32[]{:S(2)}) collective-permute-start(bf16[192,256]{1,0:T(8,128)(2,1)} %get-tuple-element.24), channel_id=1, source_target_pairs={{0,24},{4,28},{8,16},{12,20},{16,8},{20,12},{24,0},{28,4},{1,25},{... | collective-permute-start | bytes 294920 | tf_op jit(solution)/shard_map/ppermute | solution.py:399
  9.0 8.5 %collective-permute-start.1 = (bf16[192,256]{1,0:T(8,128)(2,1)}, bf16[192,256]{1,0:T(8,128)(2,1)S(1)}, u32[]{:S(2)}, u32[]{:S(2)}) collective-permute-start(bf16[192,256]{1,0:T(8,128)(2,1)} %get-tuple-element.24), channel_id=1, source_target_pairs={{0,16},{4,20},{8,24},{12,28},{16,0},{20,4},{24,8},{28,12},{1,17},{... | collective-permute-start | bytes 294920 | tf_op jit(solution)/shard_map/ppermute | solution.py:399
  9.0 8.5 %collective-permute-start = (bf16[192,256]{1,0:T(8,128)(2,1)}, bf16[192,256]{1,0:T(8,128)(2,1)S(1)}, u32[]{:S(2)}, u32[]{:S(2)}) collective-permute-start(bf16[192,256]{1,0:T(8,128)(2,1)} %get-tuple-element.24), channel_id=1, source_target_pairs={{0,8},{4,12},{8,0},{12,4},{16,24},{20,28},{24,16},{28,20},{1,9},{5... | collective-permute-start | bytes 294920 | tf_op jit(solution)/shard_map/ppermute | solution.py:399
  17.6 35.3 %copy-start.9 = (bf16[4,192,256]{2,1,0:T(8,128)(2,1)}, bf16[4,192,256]{2,1,0:T(8,128)(2,1)S(1)}, u32[]{:S(2)}) copy-start(bf16[4,192,256]{2,1,0:T(8,128)(2,1)S(1)} %pad_maximum_fusion.1.refs_0_) | copy-start | bytes 1179652
  17.6 35.3 %all-to-all-start = ((bf16[8,32,2048]{2,1,0:T(8,128)(2,1)}), bf16[8,32,2048]{2,1,0:T(8,128)(2,1)S(1)}, u32[]{:S(2)}, u32[]{:S(2)}) async-start(bf16[8,32,2048]{2,1,0:T(8,128)(2,1)} %bitcast.51), calls=%async_computation | async-start | bytes 2097152 | tf_op jit(solution)/shard_map/all_to_all | solution.py:452
  22.3 20.9 %collective-permute-start.6 = (bf16[4,192,256]{2,1,0:T(8,128)(2,1)S(1)}, bf16[4,192,256]{2,1,0:T(8,128)(2,1)S(1)}, u32[]{:S(2)}, u32[]{:S(2)}) collective-permute-start(bf16[4,192,256]{2,1,0:T(8,128)(2,1)S(1)} %pad_maximum_fusion.1.refs_0_), channel_id=1, source_target_pairs={{0,4},{4,0},{8,12},{12,8},{16,20},{20,16},{24,28},{28,24},{1,5},{5... | collective-permute-start | bytes 1179656 | tf_op jit(solution)/shard_map/ppermute | solution.py:399
  24.4 20.9 %collective-permute-start.4 = (bf16[4,192,256]{2,1,0:T(8,128)(2,1)S(1)}, bf16[4,192,256]{2,1,0:T(8,128)(2,1)S(1)}, u32[]{:S(2)}, u32[]{:S(2)}) collective-permute-start(bf16[4,192,256]{2,1,0:T(8,128)(2,1)S(1)} %pad_maximum_fusion.1.refs_0_), channel_id=1, source_target_pairs={{0,2},{1,3},{2,0},{3,1},{4,6},{5,7},{6,4},{7,5},{8,10},{9,11},{10,... | collective-permute-start | bytes 1179656 | tf_op jit(solution)/shard_map/ppermute | solution.py:402
  43.2 9.6 %copy-start.11 = (bf16[4,192,256]{2,1,0:T(8,128)(2,1)}, bf16[4,192,256]{2,1,0:T(8,128)(2,1)S(1)}, u32[]{:S(2)}) copy-start(bf16[4,192,256]{2,1,0:T(8,128)(2,1)S(1)} %collective-permute-done.6.refs_4_) | copy-start | bytes 1179652
  43.2 7.8 %collective-permute-start.8 = (bf16[4,192,256]{2,1,0:T(8,128)(2,1)S(1)}, bf16[4,192,256]{2,1,0:T(8,128)(2,1)S(1)}, u32[]{:S(2)}, u32[]{:S(2)}) collective-permute-start(bf16[4,192,256]{2,1,0:T(8,128)(2,1)S(1)} %collective-permute-done.6.refs_4_), channel_id=1, source_target_pairs={{0,2},{1,3},{2,0},{3,1},{4,6},{5,7},{6,4},{7,5},{8,10},{9,11},{10,... | collective-permute-start | bytes 1179656 | tf_op jit(solution)/shard_map/ppermute | solution.py:402
  44.7 6.9 %collective-permute-start.3 = (bf16[4,192,256]{2,1,0:T(8,128)(2,1)S(1)}, bf16[4,192,256]{2,1,0:T(8,128)(2,1)S(1)}, u32[]{:S(2)}, u32[]{:S(2)}) collective-permute-start(bf16[4,192,256]{2,1,0:T(8,128)(2,1)S(1)} %pad_maximum_fusion.1.refs_0_), channel_id=1, source_target_pairs={{0,1},{1,0},{2,3},{3,2},{4,5},{5,4},{6,7},{7,6},{8,9},{9,8},{10,11... | collective-permute-start | bytes 1179656 | tf_op jit(solution)/shard_map/ppermute | solution.py:402
  44.7 7.0 %collective-permute-start.7 = (bf16[4,192,256]{2,1,0:T(8,128)(2,1)S(1)}, bf16[4,192,256]{2,1,0:T(8,128)(2,1)S(1)}, u32[]{:S(2)}, u32[]{:S(2)}) collective-permute-start(bf16[4,192,256]{2,1,0:T(8,128)(2,1)S(1)} %collective-permute-done.6.refs_4_), channel_id=1, source_target_pairs={{0,1},{1,0},{2,3},{3,2},{4,5},{5,4},{6,7},{7,6},{8,9},{9,8},{10,11... | collective-permute-start | bytes 1179656 | tf_op jit(solution)/shard_map/ppermute | solution.py:402
  45.2 7.7 %copy-start.12 = (bf16[4,192,256]{2,1,0:T(8,128)(2,1)}, bf16[4,192,256]{2,1,0:T(8,128)(2,1)S(1)}, u32[]{:S(2)}) copy-start(bf16[4,192,256]{2,1,0:T(8,128)(2,1)S(1)} %collective-permute-done.4.refs_2_) | copy-start | bytes 1179652
  45.2 6.5 %collective-permute-start.5 = (bf16[4,192,256]{2,1,0:T(8,128)(2,1)S(1)}, bf16[4,192,256]{2,1,0:T(8,128)(2,1)S(1)}, u32[]{:S(2)}, u32[]{:S(2)}) collective-permute-start(bf16[4,192,256]{2,1,0:T(8,128)(2,1)S(1)} %collective-permute-done.4.refs_2_), channel_id=1, source_target_pairs={{0,1},{1,0},{2,3},{3,2},{4,5},{5,4},{6,7},{7,6},{8,9},{9,8},{10,11... | collective-permute-start | bytes 1179656 | tf_op jit(solution)/shard_map/ppermute | solution.py:402
  51.0 1.9 copy-start.13
  51.0 1.9 collective-permute-start.9
  51.7 1.2 copy-start.14
  51.7 0.8 copy-start.16
  52.5 0.8 copy-start.15
  52.9 1.0 copy-start.1
  72.0 1.5 collective-permute-start.10
  74.2 4.9 %collective-permute-start.13 = (f32[1,6144]{1,0:T(1,128)S(1)}, f32[1,6144]{1,0:T(1,128)S(1)}, u32[]{:S(2)}, u32[]{:S(2)}) collective-permute-start(f32[1,6144]{1,0:T(1,128)S(1)} %add.131), channel_id=1, source_target_pairs={{0,6},{1,7},{2,4},{3,5},{4,2},{5,3},{6,0},{7,1},{8,14},{9,15},{10,... | collective-permute-start | bytes 73736 | tf_op jit(solution)/shard_map/ppermute | solution.py:409
  76.1 3.8 %collective-permute-start.12 = (f32[1,6144]{1,0:T(1,128)S(1)}, f32[1,6144]{1,0:T(1,128)S(1)}, u32[]{:S(2)}, u32[]{:S(2)}) collective-permute-start(f32[1,6144]{1,0:T(1,128)S(1)} %add.131), channel_id=1, source_target_pairs={{0,4},{1,5},{2,6},{3,7},{4,0},{5,1},{6,2},{7,3},{8,12},{9,13},{10,... | collective-permute-start | bytes 73736 | tf_op jit(solution)/shard_map/ppermute | solution.py:409
  77.2 3.8 %collective-permute-start.11 = (f32[1,6144]{1,0:T(1,128)S(1)}, f32[1,6144]{1,0:T(1,128)S(1)}, u32[]{:S(2)}, u32[]{:S(2)}) collective-permute-start(f32[1,6144]{1,0:T(1,128)S(1)} %add.131), channel_id=1, source_target_pairs={{0,2},{1,3},{2,0},{3,1},{4,6},{5,7},{6,4},{7,5},{8,10},{9,11},{10,... | collective-permute-start | bytes 73736 | tf_op jit(solution)/shard_map/ppermute | solution.py:409
  81.1 4.9 %collective-permute-start.14 = (f32[1,6144]{1,0:T(1,128)S(1)}, f32[1,6144]{1,0:T(1,128)S(1)}, u32[]{:S(2)}, u32[]{:S(2)}) collective-permute-start(f32[1,6144]{1,0:T(1,128)S(1)} %add_add_fusion.1.refs_0_), channel_id=1, source_target_pairs={{0,8},{4,12},{8,0},{12,4},{16,24},{20,28},{24,16},{28,20},{1,9},{5... | collective-permute-start | bytes 73736 | tf_op jit(solution)/shard_map/ppermute | solution.py:399
  83.5 4.7 %collective-permute-start.15 = (f32[1,6144]{1,0:T(1,128)S(1)}, f32[1,6144]{1,0:T(1,128)S(1)}, u32[]{:S(2)}, u32[]{:S(2)}) collective-permute-start(f32[1,6144]{1,0:T(1,128)S(1)} %add_add_fusion.1.refs_0_), channel_id=1, source_target_pairs={{0,16},{4,20},{8,24},{12,28},{16,0},{20,4},{24,8},{28,12},{1,17},{... | collective-permute-start | bytes 73736 | tf_op jit(solution)/shard_map/ppermute | solution.py:399
  85.9 5.6 %collective-permute-start.16 = (f32[1,6144]{1,0:T(1,128)S(1)}, f32[1,6144]{1,0:T(1,128)S(1)}, u32[]{:S(2)}, u32[]{:S(2)}) collective-permute-start(f32[1,6144]{1,0:T(1,128)S(1)} %add_add_fusion.1.refs_0_), channel_id=1, source_target_pairs={{0,24},{4,28},{8,16},{12,20},{16,8},{20,12},{24,0},{28,4},{1,25},{... | collective-permute-start | bytes 73736 | tf_op jit(solution)/shard_map/ppermute | solution.py:399
  91.6 1.2 copy-start.2
  92.8 1.2 copy-start.4
  94.0 23.7 %copy-start = (bf16[6144,2048]{1,0:T(8,128)(2,1)S(1)}, bf16[6144,2048]{1,0:T(8,128)(2,1)}, u32[]{:S(2)}) copy-start(bf16[6144,2048]{1,0:T(8,128)(2,1)} %get-tuple-element.29.mass_in.mass_ref) | copy-start | bytes 75497472
  94.0 23.7 %copy-start.7 = (f32[1,2176]{1,0:T(1,128)S(1)}, f32[1,2176]{1,0:T(1,128)}, u32[]{:S(2)}) copy-start(f32[1,2176]{1,0:T(1,128)} %get-tuple-element.28.side_ref) | copy-start | bytes 26116
  103.9 1.3 collective-permute-start.17
  105.2 5.0 %collective-permute-start.20 = (f32[1,6144]{1,0:T(1,128)S(1)}, f32[1,6144]{1,0:T(1,128)S(1)}, u32[]{:S(2)}, u32[]{:S(2)}) collective-permute-start(f32[1,6144]{1,0:T(1,128)S(1)} %add.135), channel_id=1, source_target_pairs={{0,6},{1,7},{2,4},{3,5},{4,2},{5,3},{6,0},{7,1},{8,14},{9,15},{10,... | collective-permute-start | bytes 73736 | tf_op jit(solution)/shard_map/ppermute | solution.py:409
  106.2 4.1 %collective-permute-start.19 = (f32[1,6144]{1,0:T(1,128)S(1)}, f32[1,6144]{1,0:T(1,128)S(1)}, u32[]{:S(2)}, u32[]{:S(2)}) collective-permute-start(f32[1,6144]{1,0:T(1,128)S(1)} %add.135), channel_id=1, source_target_pairs={{0,4},{1,5},{2,6},{3,7},{4,0},{5,1},{6,2},{7,3},{8,12},{9,13},{10,... | collective-permute-start | bytes 73736 | tf_op jit(solution)/shard_map/ppermute | solution.py:409
  107.3 3.8 %collective-permute-start.18 = (f32[1,6144]{1,0:T(1,128)S(1)}, f32[1,6144]{1,0:T(1,128)S(1)}, u32[]{:S(2)}, u32[]{:S(2)}) collective-permute-start(f32[1,6144]{1,0:T(1,128)S(1)} %add.135), channel_id=1, source_target_pairs={{0,2},{1,3},{2,0},{3,1},{4,6},{5,7},{6,4},{7,5},{8,10},{9,11},{10,... | collective-permute-start | bytes 73736 | tf_op jit(solution)/shard_map/ppermute | solution.py:409
  111.2 4.5 %collective-permute-start.21 = (f32[1,6144]{1,0:T(1,128)S(1)}, f32[1,6144]{1,0:T(1,128)S(1)}, u32[]{:S(2)}, u32[]{:S(2)}) collective-permute-start(f32[1,6144]{1,0:T(1,128)S(1)} %add_add_fusion.refs_0_), channel_id=1, source_target_pairs={{0,8},{4,12},{8,0},{12,4},{16,24},{20,28},{24,16},{28,20},{1,9},{5... | collective-permute-start | bytes 73736 | tf_op jit(solution)/shard_map/ppermute | solution.py:399
  111.2 4.8 %collective-permute-start.22 = (f32[1,6144]{1,0:T(1,128)S(1)}, f32[1,6144]{1,0:T(1,128)S(1)}, u32[]{:S(2)}, u32[]{:S(2)}) collective-permute-start(f32[1,6144]{1,0:T(1,128)S(1)} %add_add_fusion.refs_0_), channel_id=1, source_target_pairs={{0,16},{4,20},{8,24},{12,28},{16,0},{20,4},{24,8},{28,12},{1,17},{... | collective-permute-start | bytes 73736 | tf_op jit(solution)/shard_map/ppermute | solution.py:399
  112.1 5.6 %collective-permute-start.23 = (f32[1,6144]{1,0:T(1,128)S(1)}, f32[1,6144]{1,0:T(1,128)S(1)}, u32[]{:S(2)}, u32[]{:S(2)}) collective-permute-start(f32[1,6144]{1,0:T(1,128)S(1)} %add_add_fusion.refs_0_), channel_id=1, source_target_pairs={{0,24},{4,28},{8,16},{12,20},{16,8},{20,12},{24,0},{28,4},{1,25},{... | collective-permute-start | bytes 73736 | tf_op jit(solution)/shard_map/ppermute | solution.py:399
  117.7 23.4 %copy-start.3 = (bf16[8,32,2048]{2,1,0:T(8,128)(2,1)S(1)}, bf16[8,32,2048]{2,1,0:T(8,128)(2,1)}, u32[]{:S(2)}) copy-start(bf16[8,32,2048]{2,1,0:T(8,128)(2,1)} %copy-done.1) | copy-start | bytes 3145732
  123.3 1.2 collective-permute-start.24
  124.6 4.7 %collective-permute-start.27 = (f32[1,4224]{1,0:T(1,128)S(1)}, f32[1,4224]{1,0:T(1,128)S(1)}, u32[]{:S(2)}, u32[]{:S(2)}) collective-permute-start(f32[1,4224]{1,0:T(1,128)S(1)} %add.139), channel_id=1, source_target_pairs={{0,6},{1,7},{2,4},{3,5},{4,2},{5,3},{6,0},{7,1},{8,14},{9,15},{10,... | collective-permute-start | bytes 50696 | tf_op jit(solution)/shard_map/ppermute | solution.py:409
  127.3 3.7 %collective-permute-start.26 = (f32[1,4224]{1,0:T(1,128)S(1)}, f32[1,4224]{1,0:T(1,128)S(1)}, u32[]{:S(2)}, u32[]{:S(2)}) collective-permute-start(f32[1,4224]{1,0:T(1,128)S(1)} %add.139), channel_id=1, source_target_pairs={{0,4},{1,5},{2,6},{3,7},{4,0},{5,1},{6,2},{7,3},{8,12},{9,13},{10,... | collective-permute-start | bytes 50696 | tf_op jit(solution)/shard_map/ppermute | solution.py:409
  127.6 3.7 %collective-permute-start.25 = (f32[1,4224]{1,0:T(1,128)S(1)}, f32[1,4224]{1,0:T(1,128)S(1)}, u32[]{:S(2)}, u32[]{:S(2)}) collective-permute-start(f32[1,4224]{1,0:T(1,128)S(1)} %add.139), channel_id=1, source_target_pairs={{0,2},{1,3},{2,0},{3,1},{4,6},{5,7},{6,4},{7,5},{8,10},{9,11},{10,... | collective-permute-start | bytes 50696 | tf_op jit(solution)/shard_map/ppermute | solution.py:409
  131.4 4.5 %collective-permute-start.28 = (f32[1,4224]{1,0:T(1,128)S(1)}, f32[1,4224]{1,0:T(1,128)S(1)}, u32[]{:S(2)}, u32[]{:S(2)}) collective-permute-start(f32[1,4224]{1,0:T(1,128)S(1)} %add_add_fusion.2.refs_0_), channel_id=1, source_target_pairs={{0,8},{4,12},{8,0},{12,4},{16,24},{20,28},{24,16},{28,20},{1,9},{5... | collective-permute-start | bytes 50696 | tf_op jit(solution)/shard_map/ppermute | solution.py:399
  131.7 5.5 %collective-permute-start.29 = (f32[1,4224]{1,0:T(1,128)S(1)}, f32[1,4224]{1,0:T(1,128)S(1)}, u32[]{:S(2)}, u32[]{:S(2)}) collective-permute-start(f32[1,4224]{1,0:T(1,128)S(1)} %add_add_fusion.2.refs_0_), channel_id=1, source_target_pairs={{0,16},{4,20},{8,24},{12,28},{16,0},{20,4},{24,8},{28,12},{1,17},{... | collective-permute-start | bytes 50696 | tf_op jit(solution)/shard_map/ppermute | solution.py:399
  135.6 5.5 %collective-permute-start.30 = (f32[1,4224]{1,0:T(1,128)S(1)}, f32[1,4224]{1,0:T(1,128)S(1)}, u32[]{:S(2)}, u32[]{:S(2)}) collective-permute-start(f32[1,4224]{1,0:T(1,128)S(1)} %add_add_fusion.2.refs_0_), channel_id=1, source_target_pairs={{0,24},{4,28},{8,16},{12,20},{16,8},{20,12},{24,0},{28,4},{1,25},{... | collective-permute-start | bytes 50696 | tf_op jit(solution)/shard_map/ppermute | solution.py:399
  155.4 29.2 %all-to-all-start.1 = ((f16[8,32,2176]{2,1,0:T(8,128)(2,1)}), f16[8,32,2176]{2,1,0:T(8,128)(2,1)S(1)}, u32[]{:S(2)}, u32[]{:S(2)}) async-start(f16[8,32,2176]{2,1,0:T(8,128)(2,1)} %pad_maximum_fusion), calls=%async_computation.1 | async-start | bytes 2228224 | tf_op jit(solution)/shard_map/all_to_all | solution.py:534
  160.2 2.9 %copy-start.8 = (f32[4,2,1,2,64,256]{5,4,3,2,1,0:T(8,128)S(1)}, f32[4,2,1,2,64,256]{5,4,3,2,1,0:T(8,128)}, u32[]{:S(2)}) copy-start(f32[4,2,1,2,64,256]{5,4,3,2,1,0:T(8,128)} %get-tuple-element.44) | copy-start | bytes 3145732
  160.3 2.0 %collective-permute-start.31 = (f16[4,2,2,64,256]{4,3,0,2,1:T(8,128)(2,1)S(1)}, f16[4,2,2,64,256]{4,3,0,2,1:T(8,128)(2,1)S(1)}, u32[]{:S(2)}, u32[]{:S(2)}) collective-permute-start(f16[4,2,2,64,256]{4,3,0,2,1:T(8,128)(2,1)S(1)} %fusion), channel_id=1, source_target_pairs={{0,1},{1,0},{2,3},{3,2},{4,5},{5,4},{6,7},{7,6},{8,9},{9,8},{10,11... | collective-permute-start | bytes 1572872 | tf_op jit(solution)/shard_map/ppermute | solution.py:402
  162.2 0.8 copy-start.10
  164.3 9.6 %collective-permute-start.34 = (f16[4,64,256]{2,1,0:T(8,128)(2,1)S(1)}, f16[4,64,256]{2,1,0:T(8,128)(2,1)S(1)}, u32[]{:S(2)}, u32[]{:S(2)}) collective-permute-start(f16[4,64,256]{2,1,0:T(8,128)(2,1)S(1)} %get-tuple-element.46), channel_id=1, source_target_pairs={{0,6},{1,7},{2,4},{3,5},{4,2},{5,3},{6,0},{7,1},{8,14},{9,15},{10,... | collective-permute-start | bytes 393224 | tf_op jit(solution)/shard_map/ppermute | solution.py:409
  166.2 10.7 %collective-permute-start.33 = (f16[4,64,256]{2,1,0:T(8,128)(2,1)S(1)}, f16[4,64,256]{2,1,0:T(8,128)(2,1)S(1)}, u32[]{:S(2)}, u32[]{:S(2)}) collective-permute-start(f16[4,64,256]{2,1,0:T(8,128)(2,1)S(1)} %get-tuple-element.47), channel_id=1, source_target_pairs={{0,4},{1,5},{2,6},{3,7},{4,0},{5,1},{6,2},{7,3},{8,12},{9,13},{10,... | collective-permute-start | bytes 393224 | tf_op jit(solution)/shard_map/ppermute | solution.py:409
  166.4 10.5 %collective-permute-start.32 = (f16[4,64,256]{2,1,0:T(8,128)(2,1)S(1)}, f16[4,64,256]{2,1,0:T(8,128)(2,1)S(1)}, u32[]{:S(2)}, u32[]{:S(2)}) collective-permute-start(f16[4,64,256]{2,1,0:T(8,128)(2,1)S(1)} %get-tuple-element.45), channel_id=1, source_target_pairs={{0,2},{1,3},{2,0},{3,1},{4,6},{5,7},{6,4},{7,5},{8,10},{9,11},{10,... | collective-permute-start | bytes 393224 | tf_op jit(solution)/shard_map/ppermute | solution.py:409
  177.0 9.0 %collective-permute-start.35 = (f16[64,256]{1,0:T(8,128)(2,1)S(1)}, f16[64,256]{1,0:T(8,128)(2,1)S(1)}, u32[]{:S(2)}, u32[]{:S(2)}) collective-permute-start(f16[64,256]{1,0:T(8,128)(2,1)S(1)} %get-tuple-element.50), channel_id=1, source_target_pairs={{0,8},{4,12},{8,0},{12,4},{16,24},{20,28},{24,16},{28,20},{1,9},{5... | collective-permute-start | bytes 98312 | tf_op jit(solution)/shard_map/ppermute | solution.py:399
  178.6 7.4 %collective-permute-start.36 = (f16[64,256]{1,0:T(8,128)(2,1)S(1)}, f16[64,256]{1,0:T(8,128)(2,1)S(1)}, u32[]{:S(2)}, u32[]{:S(2)}) collective-permute-start(f16[64,256]{1,0:T(8,128)(2,1)S(1)} %get-tuple-element.49), channel_id=1, source_target_pairs={{0,16},{4,20},{8,24},{12,28},{16,0},{20,4},{24,8},{28,12},{1,17},{... | collective-permute-start | bytes 98312 | tf_op jit(solution)/shard_map/ppermute | solution.py:399
  182.3 5.7 %collective-permute-start.37 = (f16[64,256]{1,0:T(8,128)(2,1)S(1)}, f16[64,256]{1,0:T(8,128)(2,1)S(1)}, u32[]{:S(2)}, u32[]{:S(2)}) collective-permute-start(f16[64,256]{1,0:T(8,128)(2,1)S(1)} %get-tuple-element.48), channel_id=1, source_target_pairs={{0,24},{4,28},{8,16},{12,20},{16,8},{20,12},{24,0},{28,4},{1,25},{... | collective-permute-start | bytes 98312 | tf_op jit(solution)/shard_map/ppermute | solution.py:399
  188.0 3.7 %collective-permute-start.38 = (f32[72,256]{1,0:T(8,128)S(1)}, f32[72,256]{1,0:T(8,128)S(1)}, u32[]{:S(2)}, u32[]{:S(2)}) collective-permute-start(f32[72,256]{1,0:T(8,128)S(1)} %concatenate.7.refs_0_), channel_id=1, source_target_pairs={{0,1},{1,0},{2,3},{3,2},{4,5},{5,4},{6,7},{7,6},{8,9},{9,8},{10,11... | collective-permute-start | bytes 221192 | tf_op jit(solution)/shard_map/ppermute | solution.py:402
  188.1 5.1 %collective-permute-start.39 = (f32[72,256]{1,0:T(8,128)S(1)}, f32[72,256]{1,0:T(8,128)S(1)}, u32[]{:S(2)}, u32[]{:S(2)}) collective-permute-start(f32[72,256]{1,0:T(8,128)S(1)} %concatenate.7.refs_0_), channel_id=1, source_target_pairs={{0,2},{1,3},{2,0},{3,1},{4,6},{5,7},{6,4},{7,5},{8,10},{9,11},{10,... | collective-permute-start | bytes 221192 | tf_op jit(solution)/shard_map/ppermute | solution.py:402
  188.9 5.1 %collective-permute-start.40 = (f32[72,256]{1,0:T(8,128)S(1)}, f32[72,256]{1,0:T(8,128)S(1)}, u32[]{:S(2)}, u32[]{:S(2)}) collective-permute-start(f32[72,256]{1,0:T(8,128)S(1)} %concatenate.7.refs_0_), channel_id=1, source_target_pairs={{0,3},{1,2},{2,1},{3,0},{4,7},{5,6},{6,5},{7,4},{8,11},{9,10},{10,... | collective-permute-start | bytes 221192 | tf_op jit(solution)/shard_map/ppermute | solution.py:402
  190.2 3.7 %copy-start.5 = (bf16[256,256]{1,0:T(8,128)(2,1)S(1)}, bf16[256,256]{1,0:T(8,128)(2,1)}, u32[]{:S(2)}) copy-start(bf16[256,256]{1,0:T(8,128)(2,1)} %embed_ref.1) | copy-start | bytes 393220
  190.2 3.7 %copy-start.6 = (bf16[256,256]{1,0:T(8,128)(2,1)S(1)}, bf16[256,256]{1,0:T(8,128)(2,1)}, u32[]{:S(2)}) copy-start(bf16[256,256]{1,0:T(8,128)(2,1)} %get-tuple-element.23.order_ref) | copy-start | bytes 393220

commit v4 on v3

--- a/solution.py
+++ b/solution.py
@@ -119,19 +119,40 @@
     lax.fori_loop(0, total_batch // BLOCK + queue_blocks, one, 0)
 
 
+def kept_places(total_rows, total_batch, feat, width):
+    across = width // feat
+    pieces = [
+        (total_rows + feat * (1 + index // across), feat * (index % across), feat * index)
+        for index in range(total_batch // feat)
+    ]
+    return total_rows, pieces
+
+
 def live_blocks(fill):
     return lax.div(fill + (BLOCK - 1), BLOCK)
 
 
-def make_kernel(offsets, share, total_batch, place_ref, fill_ref, columns_ref, *refs):
-    units = refs[: len(offsets)]
-    mass_out, sums_ref, side_ref, batch_ref, mass_ref, queue_ref, col_ref, sems, out_sems = refs[len(offsets) :]
+def make_kernel(offsets, share, total_batch, place_ref, fill_ref, *refs):
+    *inputs, mass_out, sums_ref, side_ref, batch_ref, columns_ref, mass_ref, queue_ref, col_ref, sems, strip_sems, kept_sems, out_sems = refs
+    *units, strips_ref = inputs
     row, proto = place_ref[0], place_ref[1]
     fill = fill_ref[0]
     z_count, unit_rows_count, _ = units[0].shape
     queue_share = unit_rows_count - share
     proto_count = 1 + max(other for _, other in offsets)
     y_count = 1 + max(y for y, _ in offsets)
+    strip_copies = []
+    z_count, y_count, features, _ = strips_ref.shape
+    for z in range(z_count):
+        for y in range(y_count):
+            first = pl.multiple_of((z * y_count + (lax.rem(row, y_count) ^ y)) * features, features)
+            strip_copies.append(
+                pltpu.make_async_copy(
+                    strips_ref.at[z, y], columns_ref.at[pl.ds(first, features), :], strip_sems.at[z, y]
+                )
+            )
+    for copy in strip_copies:
+        copy.start()
     copies = []
     for index, (unit, (y, other)) in enumerate(zip(units, offsets)):
         for z in range(z_count):
@@ -155,10 +176,13 @@
     for copy in copies[0::2] + copies[1::2]:
         copy.start()
     total_queue = queue_ref.shape[0]
+    total_rows = total_batch + total_queue
     width = columns_ref.shape[1]
     col_ref[...] = jnp.zeros_like(col_ref)
     sums_ref[...] = jnp.zeros_like(sums_ref)
     ones = jnp.ones((8, 128), bf16)
+    for copy in strip_copies:
+        copy.wait()
     bound = jnp.max(jnp.abs(columns_ref[...].astype(f32)))
     side_ref[0:1, total_batch:] = jnp.full((1, 128), bound, f32)
     for copy in copies[0::2]:
@@ -166,6 +190,20 @@
 
     def add_columns(low, mass):
         col_ref[:, low : low + WIDE] += jnp.sum(mass.reshape(BLOCK // 8, 8, WIDE), axis=0)
+
+    feat = columns_ref.shape[0]
+    first, pieces = kept_places(total_rows, total_batch, feat, width)
+    kept = [pltpu.make_async_copy(columns_ref, mass_out.at[pl.ds(first, feat), :], kept_sems.at[0])]
+    for index, (place, lane, crop) in enumerate(pieces):
+        kept.append(
+            pltpu.make_async_copy(
+                batch_ref.at[pl.ds(crop, feat), :],
+                mass_out.at[pl.ds(place, feat), pl.ds(lane, feat)],
+                kept_sems.at[1 + index],
+            )
+        )
+    for copy in kept:
+        copy.start()
 
     def keep(start):
         place = pl.ds(pl.multiple_of(start, BLOCK), BLOCK)
@@ -195,21 +233,32 @@
     for copy in copies[1::2]:
         copy.wait()
 
-    def queue_block(index, carry):
+    def queue_block(index, masked):
         start = pl.multiple_of(index * BLOCK, BLOCK)
         rows = queue_ref[pl.ds(start, BLOCK), :]
-        live = lax.broadcasted_iota(jnp.int32, (BLOCK, WIDE), 0) < fill - start
         place = pl.ds(pl.multiple_of(total_batch + start, BLOCK), BLOCK)
         for low in range(0, width, WIDE):
             scores = jnp.dot(rows, columns_ref[:, low : low + WIDE], preferred_element_type=f32)
             soft = jnp.exp2(scores * SOFT_SCALE)
-            mass = jnp.where(live, soft * soft, 0.0)
+            mass = soft * soft
+            if masked:
+                live = lax.broadcasted_iota(jnp.int32, (BLOCK, WIDE), 0) < fill - start
+                mass = jnp.where(live, mass, 0.0)
             mass_ref[place, low : low + WIDE] = mass.astype(bf16)
             add_columns(low, mass)
         keep(total_batch + start).start()
-        return carry
-
-    lax.fori_loop(0, live_blocks(fill), queue_block, 0)
+
+    def whole_block(index, carry):
+        queue_block(index, False)
+        return carry
+
+    whole = lax.div(fill, BLOCK)
+    lax.fori_loop(0, whole, whole_block, 0)
+
+    @pl.when(live_blocks(fill) > whole)
+    def _():
+        queue_block(whole, True)
+
     column = term_rows(1.0 / jnp.sum(col_ref[...], axis=0, keepdims=True))
     row_sums(column, total_batch, live_blocks(fill), mass_ref, sums_ref)
 
@@ -218,10 +267,12 @@
         return carry
 
     lax.fori_loop(0, total_batch // BLOCK + live_blocks(fill), finish, 0)
+    for copy in kept:
+        copy.wait()
 
 
 def column_factor(fill, total_batch, parts, mass_ref, scale_ref, col_ref, spare_ref, make=None, ready=None):
-    total_rows = mass_ref.shape[0]
+    total_rows = scale_ref.shape[1]
     total = parts[0][0:1, 0:total_rows]
     for part in parts[1:]:
         total = total + part[0:1, 0:total_rows]
@@ -260,10 +311,22 @@
     return 1.0 / (sum_terms(col_ref[...]) + jnp.sum(spare_ref[...], axis=0, keepdims=True))
 
 
-def sweep_kernel(total_batch, fill_ref, mass_in, batch_ref, columns_ref, *refs):
-    *parts, sums_ref, mass_ref, scale_ref, col_ref, spare_ref, sems = refs
+def sweep_kernel(total_batch, fill_ref, mass_in, *refs):
+    *parts, sums_ref, mass_ref, scale_ref, col_ref, spare_ref, batch_ref, columns_ref, sems, kept_sems = refs
     fill = fill_ref[0]
-    width = columns_ref.shape[1]
+    feat, width = columns_ref.shape
+    first, pieces = kept_places(mass_ref.shape[0], total_batch, feat, width)
+    kept = [pltpu.make_async_copy(mass_in.at[pl.ds(first, feat), :], columns_ref, kept_sems.at[0])]
+    for index, (place, lane, crop) in enumerate(pieces):
+        kept.append(
+            pltpu.make_async_copy(
+                mass_in.at[pl.ds(place, feat), pl.ds(lane, feat)],
+                batch_ref.at[pl.ds(crop, feat), :],
+                kept_sems.at[1 + index],
+            )
+        )
+    for copy in kept:
+        copy.start()
 
     def fetch(index):
         rows = pl.ds(pl.multiple_of(total_batch + index * BLOCK, BLOCK), BLOCK)
@@ -274,6 +337,9 @@
         return carry
 
     lax.fori_loop(0, live_blocks(fill), start, 0)
+
+    for copy in kept:
+        copy.wait()
 
     def make(index):
         rows = pl.ds(pl.multiple_of(index * BLOCK, BLOCK), BLOCK)
@@ -426,6 +492,9 @@
         place = jnp.stack([row, proto]).astype(jnp.int32)
         unit_rows_count = share + queue_share
 
+        def pick(values, index, axis):
+            return lax.dynamic_index_in_dim(values, index, axis, keepdims=False)
+
         unit, order = pl.pallas_call(
             prep_kernel,
             name="prep",
@@ -447,9 +516,18 @@
 
         lines = jnp.stack([unit] + [shift_row(unit, z, 0) for z in range(1, z_count)])
         width = prototypes.shape[1] // row_count
-        blocks = prototypes.reshape(-1, row_count, width).transpose(1, 0, 2)
-        lines, blocks = lax.optimization_barrier((lines, blocks))
-        columns = lax.all_to_all(blocks, "row", split_axis=0, concat_axis=0, tiled=True).reshape(feat, width)
+        features = prototypes.shape[0]
+
+        def strip(dy):
+            places = [((other * y_count) + (y ^ dy)) * width for other in range(z_count)]
+            return jnp.stack([lax.dynamic_slice(prototypes, (0, place), (features, width)) for place in places])
+
+        strips = [shift_row(strip(dy), 0, dy) if dy else strip(dy) for dy in range(y_count)]
+        lanes = [[other * y_count + own for other in range(z_count)] for own in range(y_count)]
+        lines, strips = lax.optimization_barrier((lines, jnp.stack(strips, axis=1)))
+        strips = lax.all_to_all(
+            strips, "row", split_axis=0, concat_axis=0, axis_index_groups=lanes, tiled=True
+        )
 
         offsets, units = [], []
         for dy in range(y_count):
@@ -459,39 +537,47 @@
                 offsets += [(dy, 2 * dx), (dy, 2 * dx + 1)]
                 units += [moved, shift_proto(moved, 1)]
 
-        mass, sums, side, batch = pl.pallas_call(
+        mass, sums, side, batch, columns = pl.pallas_call(
             functools.partial(make_kernel, offsets, share, total_batch),
             name="make_mass",
             out_shape=[
-                jax.ShapeDtypeStruct((total_rows, width), bf16),
+                jax.ShapeDtypeStruct((total_rows + feat * (1 + total_batch // width), width), bf16),
                 jax.ShapeDtypeStruct((1, total_rows), f32),
                 jax.ShapeDtypeStruct((1, total_batch + 128), f32),
                 jax.ShapeDtypeStruct((total_batch, feat), bf16),
+                jax.ShapeDtypeStruct((feat, width), bf16),
             ],
-            in_specs=[SMEM, SMEM, VMEM] + [ANY] * len(units),
-            out_specs=[ANY, VMEM, VMEM, VMEM],
+            in_specs=[SMEM, SMEM] + [ANY] * (len(units) + 1),
+            out_specs=[ANY, VMEM, VMEM, VMEM, VMEM],
             scratch_shapes=[
                 pltpu.VMEM((total_rows, width), bf16),
                 pltpu.VMEM((total_queue, feat), bf16),
                 pltpu.VMEM((8, width), f32),
                 pltpu.SemaphoreType.DMA((len(units), z_count, 2)),
+                pltpu.SemaphoreType.DMA((z_count, y_count)),
+                pltpu.SemaphoreType.DMA((1 + total_batch // feat,)),
                 pltpu.SemaphoreType.DMA,
             ],
-            compiler_params=limit(56),
-        )(place, fill_count, columns, *units)
+            compiler_params=limit(53),
+        )(place, fill_count, *units, strips)
 
         vectors = [pltpu.VMEM((8, total_rows), bf16), pltpu.VMEM((8, width), f32), pltpu.VMEM((8, width), f32)]
         sums = pl.pallas_call(
             functools.partial(sweep_kernel, total_batch),
             name="sweep",
             out_shape=jax.ShapeDtypeStruct((1, total_rows), f32),
-            in_specs=[SMEM, ANY] + [VMEM] * (2 + z_count),
+            in_specs=[SMEM, ANY] + [VMEM] * z_count,
             out_specs=VMEM,
             scratch_shapes=[pltpu.VMEM((total_rows, width), bf16)]
             + vectors
-            + [pltpu.SemaphoreType.DMA((total_queue // BLOCK,))],
-            compiler_params=limit(30),
-        )(fill_count, mass, batch, columns, *all_sum_parts(sums))
+            + [
+                pltpu.VMEM((total_batch, feat), bf16),
+                pltpu.VMEM((feat, width), bf16),
+                pltpu.SemaphoreType.DMA((total_queue // BLOCK,)),
+                pltpu.SemaphoreType.DMA((1 + total_batch // feat,)),
+            ],
+            compiler_params=limit(33),
+        )(fill_count, mass, *all_sum_parts(sums))
 
         code_sums, column = pl.pallas_call(
             functools.partial(last_kernel, total_batch),
@@ -536,9 +622,6 @@
         normed_part, grad_columns, loss, back = slopes(0, width, batch)
         size = half // x_count
 
-        def pick(values, index, axis):
-            return lax.dynamic_index_in_dim(values, index, axis, keepdims=False)
-
         pieces = normed_part.reshape(z_count, y_count, 2, x_count, size, feat)
 
         away = shift_proto(pick(pieces, 1 - core, 2).astype(f16), 1)

time: 198 us -> 188 us (0.949); the launches traced: 195 us -> 188 us
  local copies, waits for them, and re-layouts: 9.95 us -> 5.79 us
  waiting for transfers between devices: 71.8 us -> 68.2 us
    ppermute x16 -> x17, waiting for transfers between devices: 37.9 us -> 27.3 us  [shift_row(): lax.ppermute(values, 'row', [(i, i ^ offset) for i in range(row_count)])]
    all_to_all x1, waiting for transfers between devices: 0.01 us -> 4.08 us  [body(): lax.all_to_all(strips, 'row', split_axis=0, concat_axis=0, axis_index_gro...]
    unnamed x36 -> x26, local copies, waits for them, and re-layouts: 4.99 us -> 1.76 us
    reshape x1 -> x0, local copies, waits for them, and re-layouts: 2.3 us -> none  [body(): blocks = prototypes.reshape(-1, row_count, width).transpose(1, 0, 2)]
    ppermute x16 -> x17, starting transfers between devices: 26.8 us -> 26.2 us  [shift_row(): lax.ppermute(values, 'row', [(i, i ^ offset) for i in range(row_count)])]
  transfers between devices with their start and end apart: 43 -> 44, of which waited for: 30 -> 30; matrix products, arithmetic and copies ran while one was open for 4% -> 4% of each run, Pallas kernels for 0% -> 1%
where the time goes in v4:
time: 188 us
  waiting for transfers between devices  68.2 us (36%)
  starting transfers between devices  53.6 us (29%)
  Pallas kernels  51.2 us (27%)
  other arithmetic  6.73 us (4%)
  local copies, waits for them, and re-layouts  5.79 us (3%)
  between operations  2.55 us (1%)
    ppermute x17, waiting for transfers between devices, shift_row(): lax.ppermute(values, 'row', [(i, i ^ offset) for i in range(row_count)])  27.3 us
    ppermute x17, starting transfers between devices, shift_row(): lax.ppermute(values, 'row', [(i, i ^ offset) for i in range(row_count)])  26.2 us
    ppermute x12, waiting for transfers between devices, shift_xy(): return lax.ppermute(values, ('row', 'proto'), pairs)  18.6 us
    pallas_call x1, Pallas kernels, body(): pl.pallas_call(functools.partial(make_kernel, offsets, share, total_batch...  17.4 us
    ppermute x13, waiting for transfers between devices, shift_proto(): lax.ppermute(values, 'proto', [(i, i ^ offset) for i in range(proto_count)])  15.2 us
    ppermute x12, starting transfers between devices, shift_xy(): return lax.ppermute(values, ('row', 'proto'), pairs)  14.2 us
    pallas_call x1, Pallas kernels, slopes(): pl.pallas_call(functools.partial(slope_kernel, CROPS, first, last), name=...  12.9 us
    pallas_call x1, Pallas kernels, body(): pl.pallas_call(functools.partial(sweep_kernel, total_batch), name='sweep'...  11.5 us
  transfers between devices with their start and end apart: 44, of which 30 were waited for; matrix products, arithmetic and copies ran while one was open for 4% of the time, Pallas kernels for 1%

profile of v4, /device:TPU:0, one launch (start us, length us, event | category | flops | bytes accessed | tf_op | source)
XLA Modules:
  0.0 188.0 jit_solution(6250244940481623351)
XLA Ops:
  0.7 1.4 dynamic-slice_bitcast_fusion.7
  2.1 3.0 %collective-permute-start.3 = (bf16[4,32,2048]{2,1,0:T(8,128)(2,1)S(1)}, bf16[4,32,2048]{2,1,0:T(8,128)(2,1)S(1)}, u32[]{:S(2)}, u32[]{:S(2)}) collective-permute-start(bf16[4,32,2048]{2,1,0:T(8,128)(2,1)S(1)} %pad_maximum_fusion.2), channel_id=1, source_target_pairs={{0,4},{4,0},{8,12},{12,8},{16,20},{20,16},{24,28},{28,24},{1,5},{5... | collective-permute-start | bytes 1572872 | tf_op jit(solution)/shard_map/ppermute | solution.py:465
  5.8 2.7 %prep.1 = (bf16[192,256]{1,0:T(8,128)(2,1)}, bf16[256,256]{1,0:T(8,128)(2,1)}) custom-call(s32[2]{0:T(128)} %pad_add_fusion.place_ref, s32[1,256]{1,0:T(1,128)} %bitcast.72, bf16[256,256]{1,0:T(8,128)(2,1)} %embed_ref.1, bf16[512,256]{1,0:T(8,128)(2,1)} %queue_in.1), custom_call_target="tpu_custom_call" | custom-call | tf_op jit(solution)/shard_map/prep/pallas_call | solution.py:498
  8.4 3.7 %collective-permute-start.2 = (bf16[192,256]{1,0:T(8,128)(2,1)}, bf16[192,256]{1,0:T(8,128)(2,1)S(1)}, u32[]{:S(2)}, u32[]{:S(2)}) collective-permute-start(bf16[192,256]{1,0:T(8,128)(2,1)} %get-tuple-element.25), channel_id=1, source_target_pairs={{0,24},{4,28},{8,16},{12,20},{16,8},{20,12},{24,0},{28,4},{1,25},{... | collective-permute-start | bytes 294920 | tf_op jit(solution)/shard_map/ppermute | solution.py:465
  12.1 0.8 collective-permute-start
  13.0 3.3 %collective-permute-done.2 = bf16[192,256]{1,0:T(8,128)(2,1)S(1)} collective-permute-done((bf16[192,256]{1,0:T(8,128)(2,1)}, bf16[192,256]{1,0:T(8,128)(2,1)S(1)}, u32[]{:S(2)}, u32[]{:S(2)}) %collective-permute-start.2) | collective-permute-done | bytes 98336 | tf_op jit(solution)/shard_map/ppermute | solution.py:465
  16.2 4.1 %collective-permute-done.1 = bf16[192,256]{1,0:T(8,128)(2,1)S(1)} collective-permute-done((bf16[192,256]{1,0:T(8,128)(2,1)}, bf16[192,256]{1,0:T(8,128)(2,1)S(1)}, u32[]{:S(2)}, u32[]{:S(2)}) %collective-permute-start.1) | collective-permute-done | bytes 98336 | tf_op jit(solution)/shard_map/ppermute | solution.py:465
  20.3 0.9 pad_maximum_fusion.3.refs_0_
  21.3 1.1 pad_maximum_fusion.1
  22.3 3.8 %all-to-all-start = ((bf16[4,2,32,2048]{3,2,1,0:T(8,128)(2,1)}), bf16[4,2,32,2048]{3,2,1,0:T(8,128)(2,1)S(1)}, u32[]{:S(2)}, u32[]{:S(2)}) async-start(bf16[4,2,32,2048]{3,2,1,0:T(8,128)(2,1)} %pad_maximum_fusion.1), calls=%async_computation | async-start | bytes 2097152 | tf_op jit(solution)/shard_map/all_to_all | solution.py:528
  26.6 1.5 collective-permute-start.5
  28.1 8.0 %collective-permute-done.7.refs_4_ = bf16[4,192,256]{2,1,0:T(8,128)(2,1)S(1)} collective-permute-done((bf16[4,192,256]{2,1,0:T(8,128)(2,1)S(1)}, bf16[4,192,256]{2,1,0:T(8,128)(2,1)S(1)}, u32[]{:S(2)}, u32[]{:S(2)}) %collective-permute-start.7) | collective-permute-done | bytes 393248 | tf_op jit(solution)/shard_map/ppermute | solution.py:465
  36.1 1.5 collective-permute-start.9
  38.2 7.0 %collective-permute-done.9.refs_6_ = bf16[4,192,256]{2,1,0:T(8,128)(2,1)S(1)} collective-permute-done((bf16[4,192,256]{2,1,0:T(8,128)(2,1)S(1)}, bf16[4,192,256]{2,1,0:T(8,128)(2,1)S(1)}, u32[]{:S(2)}, u32[]{:S(2)}) %collective-permute-start.9) | collective-permute-done | bytes 393248 | tf_op jit(solution)/shard_map/ppermute | solution.py:468
  45.9 0.7 copy-done.12
  47.1 4.1 %all-to-all-done.refs_8_ = bf16[4,2,32,2048]{3,2,1,0:T(8,128)(2,1)S(1)} async-done(((bf16[4,2,32,2048]{3,2,1,0:T(8,128)(2,1)}), bf16[4,2,32,2048]{3,2,1,0:T(8,128)(2,1)S(1)}, u32[]{:S(2)}, u32[]{:S(2)}) %all-to-all-start) | async-done | bytes 1048608 | tf_op jit(solution)/shard_map/all_to_all | solution.py:528
  51.2 1.0 copy-done.6
  52.2 17.4 %make_mass.1 = (bf16[6656,2048]{1,0:T(8,128)(2,1)}, f32[1,6144]{1,0:T(1,128)S(1)}, f32[1,2176]{1,0:T(1,128)S(1)}, bf16[2048,256]{1,0:T(8,128)(2,1)}, bf16[256,2048]{1,0:T(8,128)(2,1)}) custom-call(s32[2]{0:T(128)S(1)} %copy-done.5, s32[1]{0:T(128)S(6)} %copy.18.fill_ref, bf16[4,192,256]{2,1,0:T(8,128)(2,1)S(1)} %pad_maximum_fusion.3.refs_0_, ...), custom_call_target="tpu_custom_call" | custom-call | tf_op jit(solution)/shard_map/make_mass/pallas_call | solution.py:540
  69.7 1.2 collective-permute-done.11
  70.9 1.5 collective-permute-start.14
  72.4 1.5 collective-permute-start.13
  74.5 1.2 collective-permute-done.14
  76.2 1.5 collective-permute-done.12
  77.9 2.0 %collective-permute-start.16 = (f32[1,6144]{1,0:T(1,128)S(1)}, f32[1,6144]{1,0:T(1,128)S(1)}, u32[]{:S(2)}, u32[]{:S(2)}) collective-permute-start(f32[1,6144]{1,0:T(1,128)S(1)} %add_add_fusion.1.refs_0_), channel_id=1, source_target_pairs={{0,16},{4,20},{8,24},{12,28},{16,0},{20,4},{24,8},{28,12},{1,17},{... | collective-permute-start | bytes 73736 | tf_op jit(solution)/shard_map/ppermute | solution.py:465
  79.9 2.4 %collective-permute-start.17 = (f32[1,6144]{1,0:T(1,128)S(1)}, f32[1,6144]{1,0:T(1,128)S(1)}, u32[]{:S(2)}, u32[]{:S(2)}) collective-permute-start(f32[1,6144]{1,0:T(1,128)S(1)} %add_add_fusion.1.refs_0_), channel_id=1, source_target_pairs={{0,24},{4,28},{8,16},{12,20},{16,8},{20,12},{24,0},{28,4},{1,25},{... | collective-permute-start | bytes 73736 | tf_op jit(solution)/shard_map/ppermute | solution.py:465
  82.8 2.7 %collective-permute-done.17.refs_3_ = f32[1,6144]{1,0:T(1,128)S(1)} collective-permute-done((f32[1,6144]{1,0:T(1,128)S(1)}, f32[1,6144]{1,0:T(1,128)S(1)}, u32[]{:S(2)}, u32[]{:S(2)}) %collective-permute-start.17) | collective-permute-done | bytes 24608 | tf_op jit(solution)/shard_map/ppermute | solution.py:465
  85.5 11.5 %sweep.1 = f32[1,6144]{1,0:T(1,128)S(1)} custom-call(s32[1]{0:T(128)S(6)} %copy.18.fill_ref, bf16[6656,2048]{1,0:T(8,128)(2,1)} %get-tuple-element.31.mass_in.mass_ref, f32[1,6144]{1,0:T(1,128)S(1)} %add_add_fusion.1.refs_0_, f32[1,6144]{1,0:T(1,128)S(1)} %collective-permute-done.15.refs_1_, f32[1,6144]{1,0:T(1,128)S(1)} %collective-permute-done.16.refs_2_, ...), custom_call_target="tpu_custom_call" | custom-call | tf_op jit(solution)/shard_map/sweep/pallas_call | solution.py:565
  97.1 1.2 collective-permute-done.18
  98.8 1.6 collective-permute-start.20
  100.4 1.5 collective-permute-start.19
  101.9 1.2 collective-permute-done.21
  103.1 1.1 collective-permute-done.19
  104.3 2.9 %collective-permute-start.23 = (f32[1,6144]{1,0:T(1,128)S(1)}, f32[1,6144]{1,0:T(1,128)S(1)}, u32[]{:S(2)}, u32[]{:S(2)}) collective-permute-start(f32[1,6144]{1,0:T(1,128)S(1)} %add_add_fusion.refs_0_), channel_id=1, source_target_pairs={{0,16},{4,20},{8,24},{12,28},{16,0},{20,4},{24,8},{28,12},{1,17},{... | collective-permute-start | bytes 73736 | tf_op jit(solution)/shard_map/ppermute | solution.py:465
  107.2 1.5 collective-permute-start.24
  109.1 3.8 %collective-permute-done.24.refs_3_ = f32[1,6144]{1,0:T(1,128)S(1)} collective-permute-done((f32[1,6144]{1,0:T(1,128)S(1)}, f32[1,6144]{1,0:T(1,128)S(1)}, u32[]{:S(2)}, u32[]{:S(2)}) %collective-permute-start.24) | collective-permute-done | bytes 24608 | tf_op jit(solution)/shard_map/ppermute | solution.py:465
  112.9 5.7 %last_sweep.1 = (f32[1,4224]{1,0:T(1,128)S(1)}, f32[1,2048]{1,0:T(1,128)S(1)}) custom-call(s32[1]{0:T(128)S(6)} %copy.18.fill_ref, f32[1,2176]{1,0:T(1,128)S(1)} %get-tuple-element.30.side_ref, bf16[6656,2048]{1,0:T(8,128)(2,1)S(1)} %copy-done, f32[1,6144]{1,0:T(1,128)S(1)} %add_add_fusion.refs_0_, f32[1,6144]{1,0:T(1,128)S(1)} %collective-permute-done.22.refs_1_, ...), custom_call_target="tpu_custom_call" | custom-call | tf_op jit(solution)/shard_map/last_sweep/pallas_call | solution.py:582
  118.5 1.2 collective-permute-done.25
  119.8 1.5 collective-permute-start.28
  121.2 1.5 collective-permute-start.27
  123.3 1.2 collective-permute-done.28
  125.0 1.5 collective-permute-done.26
  126.6 2.0 %collective-permute-start.30 = (f32[1,4224]{1,0:T(1,128)S(1)}, f32[1,4224]{1,0:T(1,128)S(1)}, u32[]{:S(2)}, u32[]{:S(2)}) collective-permute-start(f32[1,4224]{1,0:T(1,128)S(1)} %add_add_fusion.2.refs_0_), channel_id=1, source_target_pairs={{0,16},{4,20},{8,24},{12,28},{16,0},{20,4},{24,8},{28,12},{1,17},{... | collective-permute-start | bytes 50696 | tf_op jit(solution)/shard_map/ppermute | solution.py:465
  128.6 2.4 %collective-permute-start.31 = (f32[1,4224]{1,0:T(1,128)S(1)}, f32[1,4224]{1,0:T(1,128)S(1)}, u32[]{:S(2)}, u32[]{:S(2)}) collective-permute-start(f32[1,4224]{1,0:T(1,128)S(1)} %add_add_fusion.2.refs_0_), channel_id=1, source_target_pairs={{0,24},{4,28},{8,16},{12,20},{16,8},{20,12},{24,0},{28,4},{1,25},{... | collective-permute-start | bytes 50696 | tf_op jit(solution)/shard_map/ppermute | solution.py:465
  131.4 2.8 %collective-permute-done.31.refs_3_ = f32[1,4224]{1,0:T(1,128)S(1)} collective-permute-done((f32[1,4224]{1,0:T(1,128)S(1)}, f32[1,4224]{1,0:T(1,128)S(1)}, u32[]{:S(2)}, u32[]{:S(2)}) %collective-permute-start.31) | collective-permute-done | bytes 16928 | tf_op jit(solution)/shard_map/ppermute | solution.py:465
  134.2 12.9 %slopes.1 = (f32[2048,256]{1,0:T(8,128)S(1)}, f32[256,2048]{1,0:T(8,128)S(1)}, f32[8,128]{1,0:T(8,128)S(1)}, f32[8,128]{1,0:T(8,128)S(1)}) custom-call(bf16[2048,256]{1,0:T(8,128)(2,1)S(1)} %copy-done.1, bf16[256,2048]{1,0:T(8,128)(2,1)S(1)} %copy-done.2, f32[1,2048]{1,0:T(1,128)S(1)} %get-tuple-element.33.column_ref, f32[1,4224]{1,0:T(1,128)S(1)} %add_add_fusion.2.refs_0_, ...), custom_call_target="tpu_custom_call" | custom-call | tf_op jit(solution)/shard_map/slopes/pallas_call | solution.py:598
  147.3 1.3 pad_maximum_fusion
  148.5 3.6 %all-to-all-start.1 = ((f16[8,32,2176]{2,1,0:T(8,128)(2,1)}), f16[8,32,2176]{2,1,0:T(8,128)(2,1)S(1)}, u32[]{:S(2)}, u32[]{:S(2)}) async-start(f16[8,32,2176]{2,1,0:T(8,128)(2,1)} %pad_maximum_fusion), calls=%async_computation.1 | async-start | bytes 2228224 | tf_op jit(solution)/shard_map/all_to_all | solution.py:620
  152.2 1.2 constant_dynamic-slice_fusion
  153.6 2.0 %collective-permute-done.32 = f16[4,2,2,64,256]{4,3,0,2,1:T(8,128)(2,1)} collective-permute-done((f16[4,2,2,64,256]{4,3,0,2,1:T(8,128)(2,1)S(1)}, f16[4,2,2,64,256]{4,3,0,2,1:T(8,128)(2,1)}, u32[]{:S(2)}, u32[]{:S(2)}) %collective-permute-start.32) | collective-permute-done | bytes 524320 | tf_op jit(solution)/shard_map/ppermute | solution.py:468
  155.6 1.2 bitcast_add_fusion
  156.8 2.1 %collective-permute-start.35 = (f16[4,64,256]{2,1,0:T(8,128)(2,1)S(1)}, f16[4,64,256]{2,1,0:T(8,128)(2,1)S(1)}, u32[]{:S(2)}, u32[]{:S(2)}) collective-permute-start(f16[4,64,256]{2,1,0:T(8,128)(2,1)S(1)} %get-tuple-element.48), channel_id=1, source_target_pairs={{0,6},{1,7},{2,4},{3,5},{4,2},{5,3},{6,0},{7,1},{8,14},{9,15},{10,... | collective-permute-start | bytes 393224 | tf_op jit(solution)/shard_map/ppermute | solution.py:475
  159.0 1.4 collective-permute-start.33
  160.4 6.2 %collective-permute-done.35 = f16[4,64,256]{2,1,0:T(8,128)(2,1)S(1)} collective-permute-done((f16[4,64,256]{2,1,0:T(8,128)(2,1)S(1)}, f16[4,64,256]{2,1,0:T(8,128)(2,1)S(1)}, u32[]{:S(2)}, u32[]{:S(2)}) %collective-permute-start.35) | collective-permute-done | bytes 131104 | tf_op jit(solution)/shard_map/ppermute | solution.py:475
  166.6 3.5 %collective-permute-done.34 = f16[4,64,256]{2,1,0:T(8,128)(2,1)S(1)} collective-permute-done((f16[4,64,256]{2,1,0:T(8,128)(2,1)S(1)}, f16[4,64,256]{2,1,0:T(8,128)(2,1)S(1)}, u32[]{:S(2)}, u32[]{:S(2)}) %collective-permute-start.34) | collective-permute-done | bytes 131104 | tf_op jit(solution)/shard_map/ppermute | solution.py:475
  170.2 1.6 collective-permute-start.36
  171.8 3.3 %collective-permute-start.37 = (f16[64,256]{1,0:T(8,128)(2,1)S(1)}, f16[64,256]{1,0:T(8,128)(2,1)S(1)}, u32[]{:S(2)}, u32[]{:S(2)}) collective-permute-start(f16[64,256]{1,0:T(8,128)(2,1)S(1)} %get-tuple-element.59), channel_id=1, source_target_pairs={{0,16},{4,20},{8,24},{12,28},{16,0},{20,4},{24,8},{28,12},{1,17},{... | collective-permute-start | bytes 98312 | tf_op jit(solution)/shard_map/ppermute | solution.py:465
  175.1 3.0 %all-to-all-done.1 = f16[8,32,2176]{2,1,0:T(8,128)(2,1)S(1)} async-done(((f16[8,32,2176]{2,1,0:T(8,128)(2,1)}), f16[8,32,2176]{2,1,0:T(8,128)(2,1)S(1)}, u32[]{:S(2)}, u32[]{:S(2)}) %all-to-all-start.1) | async-done | bytes 1114144 | tf_op jit(solution)/shard_map/all_to_all | solution.py:620
  178.1 0.7 multiply_reduce_fusion
  179.5 1.3 collective-permute-done.38
  180.9 0.7 collective-permute-start.40
  181.7 1.1 collective-permute-start.41
  183.1 1.5 copy.13
  184.6 1.5 collective-permute-done.40.refs_2_
  186.8 1.1 finish.1
  (85 shorter events, 8.5 us)
Async XLA Ops:
  2.1 19.1 %collective-permute-start.3 = (bf16[4,32,2048]{2,1,0:T(8,128)(2,1)S(1)}, bf16[4,32,2048]{2,1,0:T(8,128)(2,1)S(1)}, u32[]{:S(2)}, u32[]{:S(2)}) collective-permute-start(bf16[4,32,2048]{2,1,0:T(8,128)(2,1)S(1)} %pad_maximum_fusion.2), channel_id=1, source_target_pairs={{0,4},{4,0},{8,12},{12,8},{16,20},{20,16},{24,28},{28,24},{1,5},{5... | collective-permute-start | bytes 1572872 | tf_op jit(solution)/shard_map/ppermute | solution.py:465
  8.4 7.8 %collective-permute-start.2 = (bf16[192,256]{1,0:T(8,128)(2,1)}, bf16[192,256]{1,0:T(8,128)(2,1)S(1)}, u32[]{:S(2)}, u32[]{:S(2)}) collective-permute-start(bf16[192,256]{1,0:T(8,128)(2,1)} %get-tuple-element.25), channel_id=1, source_target_pairs={{0,24},{4,28},{8,16},{12,20},{16,8},{20,12},{24,0},{28,4},{1,25},{... | collective-permute-start | bytes 294920 | tf_op jit(solution)/shard_map/ppermute | solution.py:465
  12.1 8.2 %collective-permute-start.1 = (bf16[192,256]{1,0:T(8,128)(2,1)}, bf16[192,256]{1,0:T(8,128)(2,1)S(1)}, u32[]{:S(2)}, u32[]{:S(2)}) collective-permute-start(bf16[192,256]{1,0:T(8,128)(2,1)} %get-tuple-element.25), channel_id=1, source_target_pairs={{0,16},{4,20},{8,24},{12,28},{16,0},{20,4},{24,8},{28,12},{1,17},{... | collective-permute-start | bytes 294920 | tf_op jit(solution)/shard_map/ppermute | solution.py:465
  12.1 8.2 %collective-permute-start = (bf16[192,256]{1,0:T(8,128)(2,1)}, bf16[192,256]{1,0:T(8,128)(2,1)S(1)}, u32[]{:S(2)}, u32[]{:S(2)}) collective-permute-start(bf16[192,256]{1,0:T(8,128)(2,1)} %get-tuple-element.25), channel_id=1, source_target_pairs={{0,8},{4,12},{8,0},{12,4},{16,24},{20,28},{24,16},{28,20},{1,9},{5... | collective-permute-start | bytes 294920 | tf_op jit(solution)/shard_map/ppermute | solution.py:465
  21.3 30.9 %copy-start.5 = (s32[2]{0:T(128)S(1)}, s32[2]{0:T(128)}, u32[]{:S(2)}) copy-start(s32[2]{0:T(128)} %pad_add_fusion.place_ref) | copy-start | bytes 28
  22.3 28.9 %all-to-all-start = ((bf16[4,2,32,2048]{3,2,1,0:T(8,128)(2,1)}), bf16[4,2,32,2048]{3,2,1,0:T(8,128)(2,1)S(1)}, u32[]{:S(2)}, u32[]{:S(2)}) async-start(bf16[4,2,32,2048]{3,2,1,0:T(8,128)(2,1)} %pad_maximum_fusion.1), calls=%async_computation | async-start | bytes 2097152 | tf_op jit(solution)/shard_map/all_to_all | solution.py:528
  26.1 10.0 %collective-permute-start.7 = (bf16[4,192,256]{2,1,0:T(8,128)(2,1)S(1)}, bf16[4,192,256]{2,1,0:T(8,128)(2,1)S(1)}, u32[]{:S(2)}, u32[]{:S(2)}) collective-permute-start(bf16[4,192,256]{2,1,0:T(8,128)(2,1)S(1)} %pad_maximum_fusion.3.refs_0_), channel_id=1, source_target_pairs={{0,4},{4,0},{8,12},{12,8},{16,20},{20,16},{24,28},{28,24},{1,5},{5... | collective-permute-start | bytes 1179656 | tf_op jit(solution)/shard_map/ppermute | solution.py:465
  26.6 11.5 %collective-permute-start.5 = (bf16[4,192,256]{2,1,0:T(8,128)(2,1)S(1)}, bf16[4,192,256]{2,1,0:T(8,128)(2,1)S(1)}, u32[]{:S(2)}, u32[]{:S(2)}) collective-permute-start(bf16[4,192,256]{2,1,0:T(8,128)(2,1)S(1)} %pad_maximum_fusion.3.refs_0_), channel_id=1, source_target_pairs={{0,2},{1,3},{2,0},{3,1},{4,6},{5,7},{6,4},{7,5},{8,10},{9,11},{10,... | collective-permute-start | bytes 1179656 | tf_op jit(solution)/shard_map/ppermute | solution.py:468
  36.1 15.1 %copy-start.8 = (bf16[4,192,256]{2,1,0:T(8,128)(2,1)}, bf16[4,192,256]{2,1,0:T(8,128)(2,1)S(1)}, u32[]{:S(2)}) copy-start(bf16[4,192,256]{2,1,0:T(8,128)(2,1)S(1)} %collective-permute-done.7.refs_4_) | copy-start | bytes 1179652
  36.1 9.1 %collective-permute-start.9 = (bf16[4,192,256]{2,1,0:T(8,128)(2,1)S(1)}, bf16[4,192,256]{2,1,0:T(8,128)(2,1)S(1)}, u32[]{:S(2)}, u32[]{:S(2)}) collective-permute-start(bf16[4,192,256]{2,1,0:T(8,128)(2,1)S(1)} %collective-permute-done.7.refs_4_), channel_id=1, source_target_pairs={{0,2},{1,3},{2,0},{3,1},{4,6},{5,7},{6,4},{7,5},{8,10},{9,11},{10,... | collective-permute-start | bytes 1179656 | tf_op jit(solution)/shard_map/ppermute | solution.py:468
  37.6 8.3 %collective-permute-start.4 = (bf16[4,192,256]{2,1,0:T(8,128)(2,1)S(1)}, bf16[4,192,256]{2,1,0:T(8,128)(2,1)S(1)}, u32[]{:S(2)}, u32[]{:S(2)}) collective-permute-start(bf16[4,192,256]{2,1,0:T(8,128)(2,1)S(1)} %pad_maximum_fusion.3.refs_0_), channel_id=1, source_target_pairs={{0,1},{1,0},{2,3},{3,2},{4,5},{5,4},{6,7},{7,6},{8,9},{9,8},{10,11... | collective-permute-start | bytes 1179656 | tf_op jit(solution)/shard_map/ppermute | solution.py:468
  37.6 8.3 %collective-permute-start.8 = (bf16[4,192,256]{2,1,0:T(8,128)(2,1)S(1)}, bf16[4,192,256]{2,1,0:T(8,128)(2,1)S(1)}, u32[]{:S(2)}, u32[]{:S(2)}) collective-permute-start(bf16[4,192,256]{2,1,0:T(8,128)(2,1)S(1)} %collective-permute-done.7.refs_4_), channel_id=1, source_target_pairs={{0,1},{1,0},{2,3},{3,2},{4,5},{5,4},{6,7},{7,6},{8,9},{9,8},{10,11... | collective-permute-start | bytes 1179656 | tf_op jit(solution)/shard_map/ppermute | solution.py:468
  38.1 13.0 %copy-start.9 = (bf16[4,192,256]{2,1,0:T(8,128)(2,1)}, bf16[4,192,256]{2,1,0:T(8,128)(2,1)S(1)}, u32[]{:S(2)}) copy-start(bf16[4,192,256]{2,1,0:T(8,128)(2,1)S(1)} %collective-permute-done.5.refs_2_) | copy-start | bytes 1179652
  38.2 7.8 %collective-permute-start.6 = (bf16[4,192,256]{2,1,0:T(8,128)(2,1)S(1)}, bf16[4,192,256]{2,1,0:T(8,128)(2,1)S(1)}, u32[]{:S(2)}, u32[]{:S(2)}) collective-permute-start(bf16[4,192,256]{2,1,0:T(8,128)(2,1)S(1)} %collective-permute-done.5.refs_2_), channel_id=1, source_target_pairs={{0,1},{1,0},{2,3},{3,2},{4,5},{5,4},{6,7},{7,6},{8,9},{9,8},{10,11... | collective-permute-start | bytes 1179656 | tf_op jit(solution)/shard_map/ppermute | solution.py:468
  45.2 5.9 %copy-start.10 = (bf16[4,192,256]{2,1,0:T(8,128)(2,1)}, bf16[4,192,256]{2,1,0:T(8,128)(2,1)S(1)}, u32[]{:S(2)}) copy-start(bf16[4,192,256]{2,1,0:T(8,128)(2,1)S(1)} %collective-permute-done.9.refs_6_) | copy-start | bytes 1179652
  45.3 1.9 collective-permute-start.10
  45.9 0.8 copy-start.12
  46.7 4.5 %copy-start.11 = (bf16[4,192,256]{2,1,0:T(8,128)(2,1)}, bf16[4,192,256]{2,1,0:T(8,128)(2,1)S(1)}, u32[]{:S(2)}) copy-start(bf16[4,192,256]{2,1,0:T(8,128)(2,1)S(1)} %collective-permute-done.8.refs_5_) | copy-start | bytes 1179652
  51.2 1.0 copy-start.6
  69.6 1.3 collective-permute-start.11
  70.9 4.8 %collective-permute-start.14 = (f32[1,6144]{1,0:T(1,128)S(1)}, f32[1,6144]{1,0:T(1,128)S(1)}, u32[]{:S(2)}, u32[]{:S(2)}) collective-permute-start(f32[1,6144]{1,0:T(1,128)S(1)} %add.184), channel_id=1, source_target_pairs={{0,6},{1,7},{2,4},{3,5},{4,2},{5,3},{6,0},{7,1},{8,14},{9,15},{10,... | collective-permute-start | bytes 73736 | tf_op jit(solution)/shard_map/ppermute | solution.py:475
  72.4 3.8 %collective-permute-start.13 = (f32[1,6144]{1,0:T(1,128)S(1)}, f32[1,6144]{1,0:T(1,128)S(1)}, u32[]{:S(2)}, u32[]{:S(2)}) collective-permute-start(f32[1,6144]{1,0:T(1,128)S(1)} %add.184), channel_id=1, source_target_pairs={{0,4},{1,5},{2,6},{3,7},{4,0},{5,1},{6,2},{7,3},{8,12},{9,13},{10,... | collective-permute-start | bytes 73736 | tf_op jit(solution)/shard_map/ppermute | solution.py:475
  73.9 3.8 %collective-permute-start.12 = (f32[1,6144]{1,0:T(1,128)S(1)}, f32[1,6144]{1,0:T(1,128)S(1)}, u32[]{:S(2)}, u32[]{:S(2)}) collective-permute-start(f32[1,6144]{1,0:T(1,128)S(1)} %add.184), channel_id=1, source_target_pairs={{0,2},{1,3},{2,0},{3,1},{4,6},{5,7},{6,4},{7,5},{8,10},{9,11},{10,... | collective-permute-start | bytes 73736 | tf_op jit(solution)/shard_map/ppermute | solution.py:475
  77.8 4.5 %collective-permute-start.15 = (f32[1,6144]{1,0:T(1,128)S(1)}, f32[1,6144]{1,0:T(1,128)S(1)}, u32[]{:S(2)}, u32[]{:S(2)}) collective-permute-start(f32[1,6144]{1,0:T(1,128)S(1)} %add_add_fusion.1.refs_0_), channel_id=1, source_target_pairs={{0,8},{4,12},{8,0},{12,4},{16,24},{20,28},{24,16},{28,20},{1,9},{5... | collective-permute-start | bytes 73736 | tf_op jit(solution)/shard_map/ppermute | solution.py:465
  77.9 5.0 %collective-permute-start.16 = (f32[1,6144]{1,0:T(1,128)S(1)}, f32[1,6144]{1,0:T(1,128)S(1)}, u32[]{:S(2)}, u32[]{:S(2)}) collective-permute-start(f32[1,6144]{1,0:T(1,128)S(1)} %add_add_fusion.1.refs_0_), channel_id=1, source_target_pairs={{0,16},{4,20},{8,24},{12,28},{16,0},{20,4},{24,8},{28,12},{1,17},{... | collective-permute-start | bytes 73736 | tf_op jit(solution)/shard_map/ppermute | solution.py:465
  79.9 5.6 %collective-permute-start.17 = (f32[1,6144]{1,0:T(1,128)S(1)}, f32[1,6144]{1,0:T(1,128)S(1)}, u32[]{:S(2)}, u32[]{:S(2)}) collective-permute-start(f32[1,6144]{1,0:T(1,128)S(1)} %add_add_fusion.1.refs_0_), channel_id=1, source_target_pairs={{0,24},{4,28},{8,16},{12,20},{16,8},{20,12},{24,0},{28,4},{1,25},{... | collective-permute-start | bytes 73736 | tf_op jit(solution)/shard_map/ppermute | solution.py:465
  85.5 27.4 %copy-start = (bf16[6656,2048]{1,0:T(8,128)(2,1)S(1)}, bf16[6656,2048]{1,0:T(8,128)(2,1)}, u32[]{:S(2)}) copy-start(bf16[6656,2048]{1,0:T(8,128)(2,1)} %get-tuple-element.31.mass_in.mass_ref) | copy-start | bytes 81788928
  97.0 1.3 collective-permute-start.18
  98.3 4.8 %collective-permute-start.21 = (f32[1,6144]{1,0:T(1,128)S(1)}, f32[1,6144]{1,0:T(1,128)S(1)}, u32[]{:S(2)}, u32[]{:S(2)}) collective-permute-start(f32[1,6144]{1,0:T(1,128)S(1)} %add.188), channel_id=1, source_target_pairs={{0,6},{1,7},{2,4},{3,5},{4,2},{5,3},{6,0},{7,1},{8,14},{9,15},{10,... | collective-permute-start | bytes 73736 | tf_op jit(solution)/shard_map/ppermute | solution.py:475
  98.8 4.3 %collective-permute-start.20 = (f32[1,6144]{1,0:T(1,128)S(1)}, f32[1,6144]{1,0:T(1,128)S(1)}, u32[]{:S(2)}, u32[]{:S(2)}) collective-permute-start(f32[1,6144]{1,0:T(1,128)S(1)} %add.188), channel_id=1, source_target_pairs={{0,4},{1,5},{2,6},{3,7},{4,0},{5,1},{6,2},{7,3},{8,12},{9,13},{10,... | collective-permute-start | bytes 73736 | tf_op jit(solution)/shard_map/ppermute | solution.py:475
  100.4 3.8 %collective-permute-start.19 = (f32[1,6144]{1,0:T(1,128)S(1)}, f32[1,6144]{1,0:T(1,128)S(1)}, u32[]{:S(2)}, u32[]{:S(2)}) collective-permute-start(f32[1,6144]{1,0:T(1,128)S(1)} %add.188), channel_id=1, source_target_pairs={{0,2},{1,3},{2,0},{3,1},{4,6},{5,7},{6,4},{7,5},{8,10},{9,11},{10,... | collective-permute-start | bytes 73736 | tf_op jit(solution)/shard_map/ppermute | solution.py:475
  104.2 4.5 %collective-permute-start.22 = (f32[1,6144]{1,0:T(1,128)S(1)}, f32[1,6144]{1,0:T(1,128)S(1)}, u32[]{:S(2)}, u32[]{:S(2)}) collective-permute-start(f32[1,6144]{1,0:T(1,128)S(1)} %add_add_fusion.refs_0_), channel_id=1, source_target_pairs={{0,8},{4,12},{8,0},{12,4},{16,24},{20,28},{24,16},{28,20},{1,9},{5... | collective-permute-start | bytes 73736 | tf_op jit(solution)/shard_map/ppermute | solution.py:465
  104.3 4.8 %collective-permute-start.23 = (f32[1,6144]{1,0:T(1,128)S(1)}, f32[1,6144]{1,0:T(1,128)S(1)}, u32[]{:S(2)}, u32[]{:S(2)}) collective-permute-start(f32[1,6144]{1,0:T(1,128)S(1)} %add_add_fusion.refs_0_), channel_id=1, source_target_pairs={{0,16},{4,20},{8,24},{12,28},{16,0},{20,4},{24,8},{28,12},{1,17},{... | collective-permute-start | bytes 73736 | tf_op jit(solution)/shard_map/ppermute | solution.py:465
  107.2 5.6 %collective-permute-start.24 = (f32[1,6144]{1,0:T(1,128)S(1)}, f32[1,6144]{1,0:T(1,128)S(1)}, u32[]{:S(2)}, u32[]{:S(2)}) collective-permute-start(f32[1,6144]{1,0:T(1,128)S(1)} %add_add_fusion.refs_0_), channel_id=1, source_target_pairs={{0,24},{4,28},{8,16},{12,20},{16,8},{20,12},{24,0},{28,4},{1,25},{... | collective-permute-start | bytes 73736 | tf_op jit(solution)/shard_map/ppermute | solution.py:465
  112.9 21.3 %copy-start.1 = (bf16[2048,256]{1,0:T(8,128)(2,1)S(1)}, bf16[2048,256]{1,0:T(8,128)(2,1)}, u32[]{:S(2)}) copy-start(bf16[2048,256]{1,0:T(8,128)(2,1)} %get-tuple-element.28.batch_ref) | copy-start | bytes 3145732
  112.9 21.3 %copy-start.2 = (bf16[256,2048]{1,0:T(8,128)(2,1)S(1)}, bf16[256,2048]{1,0:T(8,128)(2,1)}, u32[]{:S(2)}) copy-start(bf16[256,2048]{1,0:T(8,128)(2,1)} %get-tuple-element.29.columns_ref) | copy-start | bytes 3145732
  118.5 1.2 collective-permute-start.25
  119.8 4.7 %collective-permute-start.28 = (f32[1,4224]{1,0:T(1,128)S(1)}, f32[1,4224]{1,0:T(1,128)S(1)}, u32[]{:S(2)}, u32[]{:S(2)}) collective-permute-start(f32[1,4224]{1,0:T(1,128)S(1)} %add.192), channel_id=1, source_target_pairs={{0,6},{1,7},{2,4},{3,5},{4,2},{5,3},{6,0},{7,1},{8,14},{9,15},{10,... | collective-permute-start | bytes 50696 | tf_op jit(solution)/shard_map/ppermute | solution.py:475
  121.2 3.7 %collective-permute-start.27 = (f32[1,4224]{1,0:T(1,128)S(1)}, f32[1,4224]{1,0:T(1,128)S(1)}, u32[]{:S(2)}, u32[]{:S(2)}) collective-permute-start(f32[1,4224]{1,0:T(1,128)S(1)} %add.192), channel_id=1, source_target_pairs={{0,4},{1,5},{2,6},{3,7},{4,0},{5,1},{6,2},{7,3},{8,12},{9,13},{10,... | collective-permute-start | bytes 50696 | tf_op jit(solution)/shard_map/ppermute | solution.py:475
  122.8 3.7 %collective-permute-start.26 = (f32[1,4224]{1,0:T(1,128)S(1)}, f32[1,4224]{1,0:T(1,128)S(1)}, u32[]{:S(2)}, u32[]{:S(2)}) collective-permute-start(f32[1,4224]{1,0:T(1,128)S(1)} %add.192), channel_id=1, source_target_pairs={{0,2},{1,3},{2,0},{3,1},{4,6},{5,7},{6,4},{7,5},{8,10},{9,11},{10,... | collective-permute-start | bytes 50696 | tf_op jit(solution)/shard_map/ppermute | solution.py:475
  126.6 4.5 %collective-permute-start.29 = (f32[1,4224]{1,0:T(1,128)S(1)}, f32[1,4224]{1,0:T(1,128)S(1)}, u32[]{:S(2)}, u32[]{:S(2)}) collective-permute-start(f32[1,4224]{1,0:T(1,128)S(1)} %add_add_fusion.2.refs_0_), channel_id=1, source_target_pairs={{0,8},{4,12},{8,0},{12,4},{16,24},{20,28},{24,16},{28,20},{1,9},{5... | collective-permute-start | bytes 50696 | tf_op jit(solution)/shard_map/ppermute | solution.py:465
  126.6 4.8 %collective-permute-start.30 = (f32[1,4224]{1,0:T(1,128)S(1)}, f32[1,4224]{1,0:T(1,128)S(1)}, u32[]{:S(2)}, u32[]{:S(2)}) collective-permute-start(f32[1,4224]{1,0:T(1,128)S(1)} %add_add_fusion.2.refs_0_), channel_id=1, source_target_pairs={{0,16},{4,20},{8,24},{12,28},{16,0},{20,4},{24,8},{28,12},{1,17},{... | collective-permute-start | bytes 50696 | tf_op jit(solution)/shard_map/ppermute | solution.py:465
  128.6 5.5 %collective-permute-start.31 = (f32[1,4224]{1,0:T(1,128)S(1)}, f32[1,4224]{1,0:T(1,128)S(1)}, u32[]{:S(2)}, u32[]{:S(2)}) collective-permute-start(f32[1,4224]{1,0:T(1,128)S(1)} %add_add_fusion.2.refs_0_), channel_id=1, source_target_pairs={{0,24},{4,28},{8,16},{12,20},{16,8},{20,12},{24,0},{28,4},{1,25},{... | collective-permute-start | bytes 50696 | tf_op jit(solution)/shard_map/ppermute | solution.py:465
  148.5 29.6 %all-to-all-start.1 = ((f16[8,32,2176]{2,1,0:T(8,128)(2,1)}), f16[8,32,2176]{2,1,0:T(8,128)(2,1)S(1)}, u32[]{:S(2)}, u32[]{:S(2)}) async-start(f16[8,32,2176]{2,1,0:T(8,128)(2,1)} %pad_maximum_fusion), calls=%async_computation.1 | async-start | bytes 2228224 | tf_op jit(solution)/shard_map/all_to_all | solution.py:620
  153.3 2.2 %copy-start.7 = (f32[4,2,1,2,64,256]{5,4,3,2,1,0:T(8,128)S(1)}, f32[4,2,1,2,64,256]{5,4,3,2,1,0:T(8,128)}, u32[]{:S(2)}) copy-start(f32[4,2,1,2,64,256]{5,4,3,2,1,0:T(8,128)} %get-tuple-element.46) | copy-start | bytes 3145732
  153.4 2.1 %collective-permute-start.32 = (f16[4,2,2,64,256]{4,3,0,2,1:T(8,128)(2,1)S(1)}, f16[4,2,2,64,256]{4,3,0,2,1:T(8,128)(2,1)}, u32[]{:S(2)}, u32[]{:S(2)}) collective-permute-start(f16[4,2,2,64,256]{4,3,0,2,1:T(8,128)(2,1)S(1)} %fusion), channel_id=1, source_target_pairs={{0,1},{1,0},{2,3},{3,2},{4,5},{5,4},{6,7},{7,6},{8,9},{9,8},{10,11... | collective-permute-start | bytes 1572872 | tf_op jit(solution)/shard_map/ppermute | solution.py:468
  156.8 9.8 %collective-permute-start.35 = (f16[4,64,256]{2,1,0:T(8,128)(2,1)S(1)}, f16[4,64,256]{2,1,0:T(8,128)(2,1)S(1)}, u32[]{:S(2)}, u32[]{:S(2)}) collective-permute-start(f16[4,64,256]{2,1,0:T(8,128)(2,1)S(1)} %get-tuple-element.48), channel_id=1, source_target_pairs={{0,6},{1,7},{2,4},{3,5},{4,2},{5,3},{6,0},{7,1},{8,14},{9,15},{10,... | collective-permute-start | bytes 393224 | tf_op jit(solution)/shard_map/ppermute | solution.py:475
  158.9 11.3 %collective-permute-start.34 = (f16[4,64,256]{2,1,0:T(8,128)(2,1)S(1)}, f16[4,64,256]{2,1,0:T(8,128)(2,1)S(1)}, u32[]{:S(2)}, u32[]{:S(2)}) collective-permute-start(f16[4,64,256]{2,1,0:T(8,128)(2,1)S(1)} %get-tuple-element.49), channel_id=1, source_target_pairs={{0,4},{1,5},{2,6},{3,7},{4,0},{5,1},{6,2},{7,3},{8,12},{9,13},{10,... | collective-permute-start | bytes 393224 | tf_op jit(solution)/shard_map/ppermute | solution.py:475
  159.0 11.2 %collective-permute-start.33 = (f16[4,64,256]{2,1,0:T(8,128)(2,1)S(1)}, f16[4,64,256]{2,1,0:T(8,128)(2,1)S(1)}, u32[]{:S(2)}, u32[]{:S(2)}) collective-permute-start(f16[4,64,256]{2,1,0:T(8,128)(2,1)S(1)} %get-tuple-element.47), channel_id=1, source_target_pairs={{0,2},{1,3},{2,0},{3,1},{4,6},{5,7},{6,4},{7,5},{8,10},{9,11},{10,... | collective-permute-start | bytes 393224 | tf_op jit(solution)/shard_map/ppermute | solution.py:475
  170.2 9.2 %collective-permute-start.36 = (f16[64,256]{1,0:T(8,128)(2,1)S(1)}, f16[64,256]{1,0:T(8,128)(2,1)S(1)}, u32[]{:S(2)}, u32[]{:S(2)}) collective-permute-start(f16[64,256]{1,0:T(8,128)(2,1)S(1)} %get-tuple-element.60), channel_id=1, source_target_pairs={{0,8},{4,12},{8,0},{12,4},{16,24},{20,28},{24,16},{28,20},{1,9},{5... | collective-permute-start | bytes 98312 | tf_op jit(solution)/shard_map/ppermute | solution.py:465
  171.8 7.7 %collective-permute-start.37 = (f16[64,256]{1,0:T(8,128)(2,1)S(1)}, f16[64,256]{1,0:T(8,128)(2,1)S(1)}, u32[]{:S(2)}, u32[]{:S(2)}) collective-permute-start(f16[64,256]{1,0:T(8,128)(2,1)S(1)} %get-tuple-element.59), channel_id=1, source_target_pairs={{0,16},{4,20},{8,24},{12,28},{16,0},{20,4},{24,8},{28,12},{1,17},{... | collective-permute-start | bytes 98312 | tf_op jit(solution)/shard_map/ppermute | solution.py:465
  175.1 5.7 %collective-permute-start.38 = (f16[64,256]{1,0:T(8,128)(2,1)S(1)}, f16[64,256]{1,0:T(8,128)(2,1)S(1)}, u32[]{:S(2)}, u32[]{:S(2)}) collective-permute-start(f16[64,256]{1,0:T(8,128)(2,1)S(1)} %get-tuple-element.58), channel_id=1, source_target_pairs={{0,24},{4,28},{8,16},{12,20},{16,8},{20,12},{24,0},{28,4},{1,25},{... | collective-permute-start | bytes 98312 | tf_op jit(solution)/shard_map/ppermute | solution.py:465
  180.9 3.7 %collective-permute-start.39 = (f32[72,256]{1,0:T(8,128)S(1)}, f32[72,256]{1,0:T(8,128)S(1)}, u32[]{:S(2)}, u32[]{:S(2)}) collective-permute-start(f32[72,256]{1,0:T(8,128)S(1)} %concatenate.7.refs_0_), channel_id=1, source_target_pairs={{0,1},{1,0},{2,3},{3,2},{4,5},{5,4},{6,7},{7,6},{8,9},{9,8},{10,11... | collective-permute-start | bytes 221192 | tf_op jit(solution)/shard_map/ppermute | solution.py:468
  180.9 5.1 %collective-permute-start.40 = (f32[72,256]{1,0:T(8,128)S(1)}, f32[72,256]{1,0:T(8,128)S(1)}, u32[]{:S(2)}, u32[]{:S(2)}) collective-permute-start(f32[72,256]{1,0:T(8,128)S(1)} %concatenate.7.refs_0_), channel_id=1, source_target_pairs={{0,2},{1,3},{2,0},{3,1},{4,6},{5,7},{6,4},{7,5},{8,10},{9,11},{10,... | collective-permute-start | bytes 221192 | tf_op jit(solution)/shard_map/ppermute | solution.py:468
  181.7 5.1 %collective-permute-start.41 = (f32[72,256]{1,0:T(8,128)S(1)}, f32[72,256]{1,0:T(8,128)S(1)}, u32[]{:S(2)}, u32[]{:S(2)}) collective-permute-start(f32[72,256]{1,0:T(8,128)S(1)} %concatenate.7.refs_0_), channel_id=1, source_target_pairs={{0,3},{1,2},{2,1},{3,0},{4,7},{5,6},{6,5},{7,4},{8,11},{9,10},{10,... | collective-permute-start | bytes 221192 | tf_op jit(solution)/shard_map/ppermute | solution.py:468
  183.1 3.7 %copy-start.3 = (bf16[256,256]{1,0:T(8,128)(2,1)S(1)}, bf16[256,256]{1,0:T(8,128)(2,1)}, u32[]{:S(2)}) copy-start(bf16[256,256]{1,0:T(8,128)(2,1)} %embed_ref.1) | copy-start | bytes 393220
  183.1 3.7 %copy-start.4 = (bf16[256,256]{1,0:T(8,128)(2,1)S(1)}, bf16[256,256]{1,0:T(8,128)(2,1)}, u32[]{:S(2)}) copy-start(bf16[256,256]{1,0:T(8,128)(2,1)} %get-tuple-element.24.order_ref) | copy-start | bytes 393220

commit v5 on v4

--- a/solution.py
+++ b/solution.py
@@ -58,7 +58,7 @@
 
 
 def prep_kernel(
-    place_ref, image_ref, embed_in, queue_in, unit_ref, order_ref, embed_ref, queue_ref, sorted_ref, queued_ref, sems
+    row_ref, proto_ref, image_ref, embed_in, queue_in, unit_ref, order_ref, embed_ref, queue_ref, sorted_ref, queued_ref, sems
 ):
     fetch = [
         pltpu.make_async_copy(embed_in, embed_ref, sems.at[0]),
@@ -66,7 +66,7 @@
     ]
     for copy in fetch:
         copy.start()
-    row, proto = place_ref[0], place_ref[1]
+    row, proto = row_ref[0], proto_ref[0]
     rows = embed_ref.shape[0]
     half = rows // 2
     images = half // CROPS
@@ -132,10 +132,10 @@
     return lax.div(fill + (BLOCK - 1), BLOCK)
 
 
-def make_kernel(offsets, share, total_batch, place_ref, fill_ref, *refs):
+def make_kernel(offsets, share, total_batch, row_ref, proto_ref, fill_ref, *refs):
     *inputs, mass_out, sums_ref, side_ref, batch_ref, columns_ref, mass_ref, queue_ref, col_ref, sems, strip_sems, kept_sems, out_sems = refs
     *units, strips_ref = inputs
-    row, proto = place_ref[0], place_ref[1]
+    row, proto = row_ref[0], proto_ref[0]
     fill = fill_ref[0]
     z_count, unit_rows_count, _ = units[0].shape
     queue_share = unit_rows_count - share
@@ -368,7 +368,7 @@
 def slope_kernel(crop_count, first, last, batch_ref, columns_ref, column_ref, *refs):
     *parts, normed_out, grad_ref, loss_ref, back_ref, normed_ref, sems = refs
     total_batch, width = batch_ref.shape[0], last - first
-    rows = ROWS
+    rows = min(2 * ROWS, total_batch)
     wide = min(width, WIDE)
     grad_ref[...] = jnp.zeros_like(grad_ref)
     loss_ref[...] = jnp.zeros_like(loss_ref)
@@ -489,7 +489,7 @@
         total_rows = total_batch + total_queue
         row, proto = lax.axis_index("row"), lax.axis_index("proto")
         core, x, y, z = proto % 2, proto // 2, row % y_count, row // y_count
-        place = jnp.stack([row, proto]).astype(jnp.int32)
+        places = [row.reshape(1).astype(jnp.int32), proto.reshape(1).astype(jnp.int32)]
         unit_rows_count = share + queue_share
 
         def pick(values, index, axis):
@@ -502,7 +502,7 @@
                 jax.ShapeDtypeStruct((unit_rows_count, feat), bf16),
                 jax.ShapeDtypeStruct((batch_rows, batch_rows), bf16),
             ],
-            in_specs=[SMEM, VMEM, ANY, ANY],
+            in_specs=[SMEM, SMEM, VMEM, ANY, ANY],
             out_specs=[VMEM, VMEM],
             scratch_shapes=[
                 pltpu.VMEM((batch_rows, feat), bf16),
@@ -512,9 +512,9 @@
                 pltpu.SemaphoreType.DMA((2,)),
             ],
             compiler_params=limit(56),
-        )(place, crop_image.reshape(1, batch_rows), embeddings, queue_feats)
-
-        lines = jnp.stack([unit] + [shift_row(unit, z, 0) for z in range(1, z_count)])
+        )(*places, crop_image.reshape(1, batch_rows), embeddings, queue_feats)
+
+        lines = [unit] + [shift_row(unit, z, 0) for z in range(1, z_count)]
         width = prototypes.shape[1] // row_count
         features = prototypes.shape[0]
 
@@ -524,7 +524,8 @@
 
         strips = [shift_row(strip(dy), 0, dy) if dy else strip(dy) for dy in range(y_count)]
         lanes = [[other * y_count + own for other in range(z_count)] for own in range(y_count)]
-        lines, strips = lax.optimization_barrier((lines, jnp.stack(strips, axis=1)))
+        *lines, strips = lax.optimization_barrier((*lines, jnp.stack(strips, axis=1)))
+        lines = jnp.stack(lines)
         strips = lax.all_to_all(
             strips, "row", split_axis=0, concat_axis=0, axis_index_groups=lanes, tiled=True
         )
@@ -547,7 +548,7 @@
                 jax.ShapeDtypeStruct((total_batch, feat), bf16),
                 jax.ShapeDtypeStruct((feat, width), bf16),
             ],
-            in_specs=[SMEM, SMEM] + [ANY] * (len(units) + 1),
+            in_specs=[SMEM, SMEM, SMEM] + [ANY] * (len(units) + 1),
             out_specs=[ANY, VMEM, VMEM, VMEM, VMEM],
             scratch_shapes=[
                 pltpu.VMEM((total_rows, width), bf16),
@@ -559,7 +560,7 @@
                 pltpu.SemaphoreType.DMA,
             ],
             compiler_params=limit(53),
-        )(place, fill_count, *units, strips)
+        )(*places, fill_count, *units, strips)
 
         vectors = [pltpu.VMEM((8, total_rows), bf16), pltpu.VMEM((8, width), f32), pltpu.VMEM((8, width), f32)]
         sums = pl.pallas_call(

time: 188 us -> 189 us (level)
  Pallas kernels: 51.2 us -> 54.2 us
  waiting for transfers between devices: 68.2 us -> 66.3 us
  transfers between devices with their start and end apart: 44 -> 44, of which waited for: 30 -> 32; matrix products, arithmetic and copies ran while one was open for 4% -> 3% of each run, Pallas kernels for 1% -> 1%
where the time goes in v5:
time: 189 us
  waiting for transfers between devices  66.3 us (35%)
  starting transfers between devices  54.8 us (29%)
  Pallas kernels  54.2 us (29%)
  local copies, waits for them, and re-layouts  5.79 us (3%)
  other arithmetic  5.22 us (3%)
  between operations  2.56 us (1%)
    ppermute x17, starting transfers between devices, shift_row(): lax.ppermute(values, 'row', [(i, i ^ offset) for i in range(row_count)])  26.4 us
    ppermute x17, waiting for transfers between devices, shift_row(): lax.ppermute(values, 'row', [(i, i ^ offset) for i in range(row_count)])  25.5 us
    ppermute x12, waiting for transfers between devices, shift_xy(): return lax.ppermute(values, ('row', 'proto'), pairs)  20 us
    pallas_call x1, Pallas kernels, body(): pl.pallas_call(functools.partial(make_kernel, offsets, share, total_batch...  19.1 us
    ppermute x13, waiting for transfers between devices, shift_proto(): lax.ppermute(values, 'proto', [(i, i ^ offset) for i in range(proto_count)])  15.8 us
    ppermute x12, starting transfers between devices, shift_xy(): return lax.ppermute(values, ('row', 'proto'), pairs)  14.2 us
    pallas_call x1, Pallas kernels, body(): pl.pallas_call(functools.partial(sweep_kernel, total_batch), name='sweep'...  12.8 us
    pallas_call x1, Pallas kernels, slopes(): pl.pallas_call(functools.partial(slope_kernel, CROPS, first, last), name=...  12.2 us
  transfers between devices with their start and end apart: 44, of which 32 were waited for; matrix products, arithmetic and copies ran while one was open for 3% of the time, Pallas kernels for 1%

profile of v5, /device:TPU:0, one launch (start us, length us, event | category | flops | bytes accessed | tf_op | source)
XLA Modules:
  0.0 188.9 jit_solution(1217108637062346197)
XLA Ops:
  0.7 1.4 dynamic-slice_bitcast_fusion.7
  2.1 3.0 %collective-permute-start.3 = (bf16[4,32,2048]{2,1,0:T(8,128)(2,1)S(1)}, bf16[4,32,2048]{2,1,0:T(8,128)(2,1)S(1)}, u32[]{:S(2)}, u32[]{:S(2)}) collective-permute-start(bf16[4,32,2048]{2,1,0:T(8,128)(2,1)S(1)} %pad_maximum_fusion.2), channel_id=1, source_target_pairs={{0,4},{4,0},{8,12},{12,8},{16,20},{20,16},{24,28},{28,24},{1,5},{5... | collective-permute-start | bytes 1572872 | tf_op jit(solution)/shard_map/ppermute | solution.py:465
  5.2 2.6 %prep.1 = (bf16[192,256]{1,0:T(8,128)(2,1)}, bf16[256,256]{1,0:T(8,128)(2,1)}) custom-call(s32[1]{0:T(128)} %bitcast.1.row_ref, s32[1]{0:T(128)} %bitcast.proto_ref, s32[1,256]{1,0:T(1,128)} %bitcast.72, bf16[256,256]{1,0:T(8,128)(2,1)} %embed_ref.1, bf16[512,256]{1,0:T(8,128)(2,1)} %queue_in.1), custom_call_target="tpu_custom_call" | custom-call | tf_op jit(solution)/shard_map/prep/pallas_call | solution.py:498
  7.8 1.6 collective-permute-start
  9.4 2.6 %collective-permute-start.1 = (bf16[192,256]{1,0:T(8,128)(2,1)}, bf16[192,256]{1,0:T(8,128)(2,1)S(1)}, u32[]{:S(2)}, u32[]{:S(2)}) collective-permute-start(bf16[192,256]{1,0:T(8,128)(2,1)} %get-tuple-element.29), channel_id=1, source_target_pairs={{0,16},{4,20},{8,24},{12,28},{16,0},{20,4},{24,8},{28,12},{1,17},{... | collective-permute-start | bytes 294920 | tf_op jit(solution)/shard_map/ppermute | solution.py:465
  12.3 4.8 %collective-permute-done.3 = bf16[4,32,2048]{2,1,0:T(8,128)(2,1)S(1)} collective-permute-done((bf16[4,32,2048]{2,1,0:T(8,128)(2,1)S(1)}, bf16[4,32,2048]{2,1,0:T(8,128)(2,1)S(1)}, u32[]{:S(2)}, u32[]{:S(2)}) %collective-permute-start.3) | collective-permute-done | bytes 524320 | tf_op jit(solution)/shard_map/ppermute | solution.py:465
  17.1 1.1 pad_maximum_fusion.1
  18.2 1.7 collective-permute-done.1
  19.8 3.9 %all-to-all-start = ((bf16[4,2,32,2048]{3,2,1,0:T(8,128)(2,1)}), bf16[4,2,32,2048]{3,2,1,0:T(8,128)(2,1)S(1)}, u32[]{:S(2)}, u32[]{:S(2)}) async-start(bf16[4,2,32,2048]{3,2,1,0:T(8,128)(2,1)} %pad_maximum_fusion.1), calls=%async_computation | async-start | bytes 2097152 | tf_op jit(solution)/shard_map/all_to_all | solution.py:529
  23.8 1.2 collective-permute-start.7
  24.9 1.5 collective-permute-start.5
  26.4 6.7 %collective-permute-done.7.refs_4_ = bf16[4,192,256]{2,1,0:T(8,128)(2,1)S(1)} collective-permute-done((bf16[4,192,256]{2,1,0:T(8,128)(2,1)S(1)}, bf16[4,192,256]{2,1,0:T(8,128)(2,1)S(1)}, u32[]{:S(2)}, u32[]{:S(2)}) %collective-permute-start.7) | collective-permute-done | bytes 393248 | tf_op jit(solution)/shard_map/ppermute | solution.py:465
  33.1 1.5 collective-permute-start.9
  35.6 7.2 %collective-permute-done.9.refs_6_ = bf16[4,192,256]{2,1,0:T(8,128)(2,1)S(1)} collective-permute-done((bf16[4,192,256]{2,1,0:T(8,128)(2,1)S(1)}, bf16[4,192,256]{2,1,0:T(8,128)(2,1)S(1)}, u32[]{:S(2)}, u32[]{:S(2)}) %collective-permute-start.9) | collective-permute-done | bytes 393248 | tf_op jit(solution)/shard_map/ppermute | solution.py:468
  43.5 0.7 copy-done.11
  44.6 3.5 %all-to-all-done.refs_8_ = bf16[4,2,32,2048]{3,2,1,0:T(8,128)(2,1)S(1)} async-done(((bf16[4,2,32,2048]{3,2,1,0:T(8,128)(2,1)}), bf16[4,2,32,2048]{3,2,1,0:T(8,128)(2,1)S(1)}, u32[]{:S(2)}, u32[]{:S(2)}) %all-to-all-start) | async-done | bytes 1048608 | tf_op jit(solution)/shard_map/all_to_all | solution.py:529
  48.2 1.0 copy-done.5
  49.1 19.1 %make_mass.1 = (bf16[6656,2048]{1,0:T(8,128)(2,1)}, f32[1,6144]{1,0:T(1,128)S(1)}, f32[1,2176]{1,0:T(1,128)S(1)}, bf16[2048,256]{1,0:T(8,128)(2,1)}, bf16[256,2048]{1,0:T(8,128)(2,1)}) custom-call(s32[1]{0:T(128)} %bitcast.1.row_ref, s32[1]{0:T(128)} %bitcast.proto_ref, s32[1]{0:T(128)S(6)} %copy.18.fill_ref, ...), custom_call_target="tpu_custom_call" | custom-call | tf_op jit(solution)/shard_map/make_mass/pallas_call | solution.py:541
  68.3 1.2 collective-permute-done.11
  69.5 2.5 %collective-permute-start.14 = (f32[1,6144]{1,0:T(1,128)S(1)}, f32[1,6144]{1,0:T(1,128)S(1)}, u32[]{:S(2)}, u32[]{:S(2)}) collective-permute-start(f32[1,6144]{1,0:T(1,128)S(1)} %add.184), channel_id=1, source_target_pairs={{0,6},{1,7},{2,4},{3,5},{4,2},{5,3},{6,0},{7,1},{8,14},{9,15},{10,... | collective-permute-start | bytes 73736 | tf_op jit(solution)/shard_map/ppermute | solution.py:475
  72.6 0.5 collective-permute-start.12
  73.1 1.2 collective-permute-done.14
  74.3 1.6 collective-permute-done.13
  76.5 2.0 %collective-permute-start.16 = (f32[1,6144]{1,0:T(1,128)S(1)}, f32[1,6144]{1,0:T(1,128)S(1)}, u32[]{:S(2)}, u32[]{:S(2)}) collective-permute-start(f32[1,6144]{1,0:T(1,128)S(1)} %add_add_fusion.1.refs_0_), channel_id=1, source_target_pairs={{0,16},{4,20},{8,24},{12,28},{16,0},{20,4},{24,8},{28,12},{1,17},{... | collective-permute-start | bytes 73736 | tf_op jit(solution)/shard_map/ppermute | solution.py:465
  78.5 2.4 %collective-permute-start.17 = (f32[1,6144]{1,0:T(1,128)S(1)}, f32[1,6144]{1,0:T(1,128)S(1)}, u32[]{:S(2)}, u32[]{:S(2)}) collective-permute-start(f32[1,6144]{1,0:T(1,128)S(1)} %add_add_fusion.1.refs_0_), channel_id=1, source_target_pairs={{0,24},{4,28},{8,16},{12,20},{16,8},{20,12},{24,0},{28,4},{1,25},{... | collective-permute-start | bytes 73736 | tf_op jit(solution)/shard_map/ppermute | solution.py:465
  81.3 2.8 %collective-permute-done.17.refs_3_ = f32[1,6144]{1,0:T(1,128)S(1)} collective-permute-done((f32[1,6144]{1,0:T(1,128)S(1)}, f32[1,6144]{1,0:T(1,128)S(1)}, u32[]{:S(2)}, u32[]{:S(2)}) %collective-permute-start.17) | collective-permute-done | bytes 24608 | tf_op jit(solution)/shard_map/ppermute | solution.py:465
  84.2 12.8 %sweep.1 = f32[1,6144]{1,0:T(1,128)S(1)} custom-call(s32[1]{0:T(128)S(6)} %copy.18.fill_ref, bf16[6656,2048]{1,0:T(8,128)(2,1)} %get-tuple-element.37.mass_in.mass_ref, f32[1,6144]{1,0:T(1,128)S(1)} %add_add_fusion.1.refs_0_, f32[1,6144]{1,0:T(1,128)S(1)} %collective-permute-done.15.refs_1_, f32[1,6144]{1,0:T(1,128)S(1)} %collective-permute-done.16.refs_2_, ...), custom_call_target="tpu_custom_call" | custom-call | tf_op jit(solution)/shard_map/sweep/pallas_call | solution.py:566
  97.1 1.2 collective-permute-done.18
  98.3 1.5 collective-permute-start.21
  100.4 1.5 collective-permute-start.19
  101.8 1.2 collective-permute-done.21
  103.1 0.6 collective-permute-done.20
  104.3 2.9 %collective-permute-start.23 = (f32[1,6144]{1,0:T(1,128)S(1)}, f32[1,6144]{1,0:T(1,128)S(1)}, u32[]{:S(2)}, u32[]{:S(2)}) collective-permute-start(f32[1,6144]{1,0:T(1,128)S(1)} %add_add_fusion.refs_0_), channel_id=1, source_target_pairs={{0,16},{4,20},{8,24},{12,28},{16,0},{20,4},{24,8},{28,12},{1,17},{... | collective-permute-start | bytes 73736 | tf_op jit(solution)/shard_map/ppermute | solution.py:465
  107.2 1.5 collective-permute-start.24
  109.1 3.7 %collective-permute-done.24.refs_3_ = f32[1,6144]{1,0:T(1,128)S(1)} collective-permute-done((f32[1,6144]{1,0:T(1,128)S(1)}, f32[1,6144]{1,0:T(1,128)S(1)}, u32[]{:S(2)}, u32[]{:S(2)}) %collective-permute-start.24) | collective-permute-done | bytes 24608 | tf_op jit(solution)/shard_map/ppermute | solution.py:465
  112.8 6.3 %last_sweep.1 = (f32[1,4224]{1,0:T(1,128)S(1)}, f32[1,2048]{1,0:T(1,128)S(1)}) custom-call(s32[1]{0:T(128)S(6)} %copy.18.fill_ref, f32[1,2176]{1,0:T(1,128)S(1)} %get-tuple-element.36.side_ref, bf16[6656,2048]{1,0:T(8,128)(2,1)S(1)} %copy-done, f32[1,6144]{1,0:T(1,128)S(1)} %add_add_fusion.refs_0_, f32[1,6144]{1,0:T(1,128)S(1)} %collective-permute-done.22.refs_1_, ...), custom_call_target="tpu_custom_call" | custom-call | tf_op jit(solution)/shard_map/last_sweep/pallas_call | solution.py:583
  119.1 1.2 collective-permute-done.25
  120.3 2.5 %collective-permute-start.28 = (f32[1,4224]{1,0:T(1,128)S(1)}, f32[1,4224]{1,0:T(1,128)S(1)}, u32[]{:S(2)}, u32[]{:S(2)}) collective-permute-start(f32[1,4224]{1,0:T(1,128)S(1)} %add.192), channel_id=1, source_target_pairs={{0,6},{1,7},{2,4},{3,5},{4,2},{5,3},{6,0},{7,1},{8,14},{9,15},{10,... | collective-permute-start | bytes 50696 | tf_op jit(solution)/shard_map/ppermute | solution.py:475
  123.9 1.2 collective-permute-done.28
  125.0 1.6 collective-permute-done.27
  127.2 2.0 %collective-permute-start.30 = (f32[1,4224]{1,0:T(1,128)S(1)}, f32[1,4224]{1,0:T(1,128)S(1)}, u32[]{:S(2)}, u32[]{:S(2)}) collective-permute-start(f32[1,4224]{1,0:T(1,128)S(1)} %add_add_fusion.2.refs_0_), channel_id=1, source_target_pairs={{0,16},{4,20},{8,24},{12,28},{16,0},{20,4},{24,8},{28,12},{1,17},{... | collective-permute-start | bytes 50696 | tf_op jit(solution)/shard_map/ppermute | solution.py:465
  129.2 2.4 %collective-permute-start.31 = (f32[1,4224]{1,0:T(1,128)S(1)}, f32[1,4224]{1,0:T(1,128)S(1)}, u32[]{:S(2)}, u32[]{:S(2)}) collective-permute-start(f32[1,4224]{1,0:T(1,128)S(1)} %add_add_fusion.2.refs_0_), channel_id=1, source_target_pairs={{0,24},{4,28},{8,16},{12,20},{16,8},{20,12},{24,0},{28,4},{1,25},{... | collective-permute-start | bytes 50696 | tf_op jit(solution)/shard_map/ppermute | solution.py:465
  131.9 2.8 %collective-permute-done.31.refs_3_ = f32[1,4224]{1,0:T(1,128)S(1)} collective-permute-done((f32[1,4224]{1,0:T(1,128)S(1)}, f32[1,4224]{1,0:T(1,128)S(1)}, u32[]{:S(2)}, u32[]{:S(2)}) %collective-permute-start.31) | collective-permute-done | bytes 16928 | tf_op jit(solution)/shard_map/ppermute | solution.py:465
  134.8 12.2 %slopes.1 = (f32[2048,256]{1,0:T(8,128)S(1)}, f32[256,2048]{1,0:T(8,128)S(1)}, f32[8,128]{1,0:T(8,128)S(1)}, f32[8,128]{1,0:T(8,128)S(1)}) custom-call(bf16[2048,256]{1,0:T(8,128)(2,1)S(1)} %copy-done.1, bf16[256,2048]{1,0:T(8,128)(2,1)S(1)} %copy-done.2, f32[1,2048]{1,0:T(1,128)S(1)} %get-tuple-element.39.column_ref, f32[1,4224]{1,0:T(1,128)S(1)} %add_add_fusion.2.refs_0_, ...), custom_call_target="tpu_custom_call" | custom-call | tf_op jit(solution)/shard_map/slopes/pallas_call | solution.py:599
  147.2 1.3 pad_maximum_fusion
  148.4 4.6 %all-to-all-start.1 = ((f16[8,32,2176]{2,1,0:T(8,128)(2,1)}), f16[8,32,2176]{2,1,0:T(8,128)(2,1)S(1)}, u32[]{:S(2)}, u32[]{:S(2)}) async-start(f16[8,32,2176]{2,1,0:T(8,128)(2,1)} %pad_maximum_fusion), calls=%async_computation.1 | async-start | bytes 2228224 | tf_op jit(solution)/shard_map/all_to_all | solution.py:621
  153.0 1.2 constant_dynamic-slice_fusion
  154.5 2.0 %collective-permute-done.32 = f16[4,2,2,64,256]{4,3,0,2,1:T(8,128)(2,1)} collective-permute-done((f16[4,2,2,64,256]{4,3,0,2,1:T(8,128)(2,1)S(1)}, f16[4,2,2,64,256]{4,3,0,2,1:T(8,128)(2,1)}, u32[]{:S(2)}, u32[]{:S(2)}) %collective-permute-start.32) | collective-permute-done | bytes 524320 | tf_op jit(solution)/shard_map/ppermute | solution.py:468
  156.4 1.2 bitcast_add_fusion
  157.7 2.0 %collective-permute-start.35 = (f16[4,64,256]{2,1,0:T(8,128)(2,1)S(1)}, f16[4,64,256]{2,1,0:T(8,128)(2,1)S(1)}, u32[]{:S(2)}, u32[]{:S(2)}) collective-permute-start(f16[4,64,256]{2,1,0:T(8,128)(2,1)S(1)} %get-tuple-element.54), channel_id=1, source_target_pairs={{0,6},{1,7},{2,4},{3,5},{4,2},{5,3},{6,0},{7,1},{8,14},{9,15},{10,... | collective-permute-start | bytes 393224 | tf_op jit(solution)/shard_map/ppermute | solution.py:475
  159.9 1.4 collective-permute-start.33
  161.3 6.2 %collective-permute-done.35 = f16[4,64,256]{2,1,0:T(8,128)(2,1)S(1)} collective-permute-done((f16[4,64,256]{2,1,0:T(8,128)(2,1)S(1)}, f16[4,64,256]{2,1,0:T(8,128)(2,1)S(1)}, u32[]{:S(2)}, u32[]{:S(2)}) %collective-permute-start.35) | collective-permute-done | bytes 131104 | tf_op jit(solution)/shard_map/ppermute | solution.py:475
  167.5 4.9 %collective-permute-done.34 = f16[4,64,256]{2,1,0:T(8,128)(2,1)S(1)} collective-permute-done((f16[4,64,256]{2,1,0:T(8,128)(2,1)S(1)}, f16[4,64,256]{2,1,0:T(8,128)(2,1)S(1)}, u32[]{:S(2)}, u32[]{:S(2)}) %collective-permute-start.34) | collective-permute-done | bytes 131104 | tf_op jit(solution)/shard_map/ppermute | solution.py:475
  172.6 3.3 %collective-permute-start.37 = (f16[64,256]{1,0:T(8,128)(2,1)S(1)}, f16[64,256]{1,0:T(8,128)(2,1)S(1)}, u32[]{:S(2)}, u32[]{:S(2)}) collective-permute-start(f16[64,256]{1,0:T(8,128)(2,1)S(1)} %get-tuple-element.65), channel_id=1, source_target_pairs={{0,16},{4,20},{8,24},{12,28},{16,0},{20,4},{24,8},{28,12},{1,17},{... | collective-permute-start | bytes 98312 | tf_op jit(solution)/shard_map/ppermute | solution.py:465
  175.9 1.0 collective-permute-start.38
  176.9 1.6 all-to-all-done.1
  178.5 0.7 multiply_reduce_fusion
  179.9 1.8 collective-permute-done.38
  181.8 0.7 collective-permute-start.40
  182.4 1.2 collective-permute-start.41
  183.9 1.5 copy.13
  185.4 1.5 collective-permute-done.40.refs_2_
  186.9 0.7 collective-permute-done.41.refs_3_
  187.6 1.1 finish.1
  (84 shorter events, 8.3 us)
Async XLA Ops:
  2.1 15.0 %collective-permute-start.3 = (bf16[4,32,2048]{2,1,0:T(8,128)(2,1)S(1)}, bf16[4,32,2048]{2,1,0:T(8,128)(2,1)S(1)}, u32[]{:S(2)}, u32[]{:S(2)}) collective-permute-start(bf16[4,32,2048]{2,1,0:T(8,128)(2,1)S(1)} %pad_maximum_fusion.2), channel_id=1, source_target_pairs={{0,4},{4,0},{8,12},{12,8},{16,20},{20,16},{24,28},{28,24},{1,5},{5... | collective-permute-start | bytes 1572872 | tf_op jit(solution)/shard_map/ppermute | solution.py:465
  7.8 10.4 %collective-permute-start = (bf16[192,256]{1,0:T(8,128)(2,1)}, bf16[192,256]{1,0:T(8,128)(2,1)S(1)}, u32[]{:S(2)}, u32[]{:S(2)}) collective-permute-start(bf16[192,256]{1,0:T(8,128)(2,1)} %get-tuple-element.29), channel_id=1, source_target_pairs={{0,8},{4,12},{8,0},{12,4},{16,24},{20,28},{24,16},{28,20},{1,9},{5... | collective-permute-start | bytes 294920 | tf_op jit(solution)/shard_map/ppermute | solution.py:465
  9.4 10.4 %collective-permute-start.1 = (bf16[192,256]{1,0:T(8,128)(2,1)}, bf16[192,256]{1,0:T(8,128)(2,1)S(1)}, u32[]{:S(2)}, u32[]{:S(2)}) collective-permute-start(bf16[192,256]{1,0:T(8,128)(2,1)} %get-tuple-element.29), channel_id=1, source_target_pairs={{0,16},{4,20},{8,24},{12,28},{16,0},{20,4},{24,8},{28,12},{1,17},{... | collective-permute-start | bytes 294920 | tf_op jit(solution)/shard_map/ppermute | solution.py:465
  12.0 7.8 %collective-permute-start.2 = (bf16[192,256]{1,0:T(8,128)(2,1)}, bf16[192,256]{1,0:T(8,128)(2,1)S(1)}, u32[]{:S(2)}, u32[]{:S(2)}) collective-permute-start(bf16[192,256]{1,0:T(8,128)(2,1)} %get-tuple-element.29), channel_id=1, source_target_pairs={{0,24},{4,28},{8,16},{12,20},{16,8},{20,12},{24,0},{28,4},{1,25},{... | collective-permute-start | bytes 294920 | tf_op jit(solution)/shard_map/ppermute | solution.py:465
  17.1 6.6 %copy-start.12 = (bf16[192,256]{1,0:T(8,128)(2,1)S(1)}, bf16[192,256]{1,0:T(8,128)(2,1)}, u32[]{:S(2)}) copy-start(bf16[192,256]{1,0:T(8,128)(2,1)} %get-tuple-element.29) | copy-start | bytes 294916
  19.8 28.3 %all-to-all-start = ((bf16[4,2,32,2048]{3,2,1,0:T(8,128)(2,1)}), bf16[4,2,32,2048]{3,2,1,0:T(8,128)(2,1)S(1)}, u32[]{:S(2)}, u32[]{:S(2)}) async-start(bf16[4,2,32,2048]{3,2,1,0:T(8,128)(2,1)} %pad_maximum_fusion.1), calls=%async_computation | async-start | bytes 2097152 | tf_op jit(solution)/shard_map/all_to_all | solution.py:529
  23.8 9.4 %collective-permute-start.7 = (bf16[4,192,256]{2,1,0:T(8,128)(2,1)S(1)}, bf16[4,192,256]{2,1,0:T(8,128)(2,1)S(1)}, u32[]{:S(2)}, u32[]{:S(2)}) collective-permute-start(bf16[4,192,256]{2,1,0:T(8,128)(2,1)S(1)} %pad_maximum_fusion.3.refs_0_), channel_id=1, source_target_pairs={{0,4},{4,0},{8,12},{12,8},{16,20},{20,16},{24,28},{28,24},{1,5},{5... | collective-permute-start | bytes 1179656 | tf_op jit(solution)/shard_map/ppermute | solution.py:465
  24.9 10.6 %collective-permute-start.5 = (bf16[4,192,256]{2,1,0:T(8,128)(2,1)S(1)}, bf16[4,192,256]{2,1,0:T(8,128)(2,1)S(1)}, u32[]{:S(2)}, u32[]{:S(2)}) collective-permute-start(bf16[4,192,256]{2,1,0:T(8,128)(2,1)S(1)} %pad_maximum_fusion.3.refs_0_), channel_id=1, source_target_pairs={{0,2},{1,3},{2,0},{3,1},{4,6},{5,7},{6,4},{7,5},{8,10},{9,11},{10,... | collective-permute-start | bytes 1179656 | tf_op jit(solution)/shard_map/ppermute | solution.py:468
  33.1 15.0 %copy-start.7 = (bf16[4,192,256]{2,1,0:T(8,128)(2,1)}, bf16[4,192,256]{2,1,0:T(8,128)(2,1)S(1)}, u32[]{:S(2)}) copy-start(bf16[4,192,256]{2,1,0:T(8,128)(2,1)S(1)} %collective-permute-done.7.refs_4_) | copy-start | bytes 1179652
  33.1 9.7 %collective-permute-start.9 = (bf16[4,192,256]{2,1,0:T(8,128)(2,1)S(1)}, bf16[4,192,256]{2,1,0:T(8,128)(2,1)S(1)}, u32[]{:S(2)}, u32[]{:S(2)}) collective-permute-start(bf16[4,192,256]{2,1,0:T(8,128)(2,1)S(1)} %collective-permute-done.7.refs_4_), channel_id=1, source_target_pairs={{0,2},{1,3},{2,0},{3,1},{4,6},{5,7},{6,4},{7,5},{8,10},{9,11},{10,... | collective-permute-start | bytes 1179656 | tf_op jit(solution)/shard_map/ppermute | solution.py:468
  34.6 8.8 %collective-permute-start.4 = (bf16[4,192,256]{2,1,0:T(8,128)(2,1)S(1)}, bf16[4,192,256]{2,1,0:T(8,128)(2,1)S(1)}, u32[]{:S(2)}, u32[]{:S(2)}) collective-permute-start(bf16[4,192,256]{2,1,0:T(8,128)(2,1)S(1)} %pad_maximum_fusion.3.refs_0_), channel_id=1, source_target_pairs={{0,1},{1,0},{2,3},{3,2},{4,5},{5,4},{6,7},{7,6},{8,9},{9,8},{10,11... | collective-permute-start | bytes 1179656 | tf_op jit(solution)/shard_map/ppermute | solution.py:468
  34.6 8.8 %collective-permute-start.8 = (bf16[4,192,256]{2,1,0:T(8,128)(2,1)S(1)}, bf16[4,192,256]{2,1,0:T(8,128)(2,1)S(1)}, u32[]{:S(2)}, u32[]{:S(2)}) collective-permute-start(bf16[4,192,256]{2,1,0:T(8,128)(2,1)S(1)} %collective-permute-done.7.refs_4_), channel_id=1, source_target_pairs={{0,1},{1,0},{2,3},{3,2},{4,5},{5,4},{6,7},{7,6},{8,9},{9,8},{10,11... | collective-permute-start | bytes 1179656 | tf_op jit(solution)/shard_map/ppermute | solution.py:468
  35.6 12.6 %copy-start.8 = (bf16[4,192,256]{2,1,0:T(8,128)(2,1)}, bf16[4,192,256]{2,1,0:T(8,128)(2,1)S(1)}, u32[]{:S(2)}) copy-start(bf16[4,192,256]{2,1,0:T(8,128)(2,1)S(1)} %collective-permute-done.5.refs_2_) | copy-start | bytes 1179652
  35.6 7.9 %collective-permute-start.6 = (bf16[4,192,256]{2,1,0:T(8,128)(2,1)S(1)}, bf16[4,192,256]{2,1,0:T(8,128)(2,1)S(1)}, u32[]{:S(2)}, u32[]{:S(2)}) collective-permute-start(bf16[4,192,256]{2,1,0:T(8,128)(2,1)S(1)} %collective-permute-done.5.refs_2_), channel_id=1, source_target_pairs={{0,1},{1,0},{2,3},{3,2},{4,5},{5,4},{6,7},{7,6},{8,9},{9,8},{10,11... | collective-permute-start | bytes 1179656 | tf_op jit(solution)/shard_map/ppermute | solution.py:468
  42.8 5.4 %copy-start.9 = (bf16[4,192,256]{2,1,0:T(8,128)(2,1)}, bf16[4,192,256]{2,1,0:T(8,128)(2,1)S(1)}, u32[]{:S(2)}) copy-start(bf16[4,192,256]{2,1,0:T(8,128)(2,1)S(1)} %collective-permute-done.9.refs_6_) | copy-start | bytes 1179652
  42.8 1.9 collective-permute-start.10
  43.4 0.8 copy-start.11
  44.2 3.9 %copy-start.10 = (bf16[4,192,256]{2,1,0:T(8,128)(2,1)}, bf16[4,192,256]{2,1,0:T(8,128)(2,1)S(1)}, u32[]{:S(2)}) copy-start(bf16[4,192,256]{2,1,0:T(8,128)(2,1)S(1)} %collective-permute-done.8.refs_5_) | copy-start | bytes 1179652
  48.2 1.0 copy-start.5
  68.2 1.3 collective-permute-start.11
  69.5 4.8 %collective-permute-start.14 = (f32[1,6144]{1,0:T(1,128)S(1)}, f32[1,6144]{1,0:T(1,128)S(1)}, u32[]{:S(2)}, u32[]{:S(2)}) collective-permute-start(f32[1,6144]{1,0:T(1,128)S(1)} %add.184), channel_id=1, source_target_pairs={{0,6},{1,7},{2,4},{3,5},{4,2},{5,3},{6,0},{7,1},{8,14},{9,15},{10,... | collective-permute-start | bytes 73736 | tf_op jit(solution)/shard_map/ppermute | solution.py:475
  72.1 3.8 %collective-permute-start.13 = (f32[1,6144]{1,0:T(1,128)S(1)}, f32[1,6144]{1,0:T(1,128)S(1)}, u32[]{:S(2)}, u32[]{:S(2)}) collective-permute-start(f32[1,6144]{1,0:T(1,128)S(1)} %add.184), channel_id=1, source_target_pairs={{0,4},{1,5},{2,6},{3,7},{4,0},{5,1},{6,2},{7,3},{8,12},{9,13},{10,... | collective-permute-start | bytes 73736 | tf_op jit(solution)/shard_map/ppermute | solution.py:475
  72.6 3.8 %collective-permute-start.12 = (f32[1,6144]{1,0:T(1,128)S(1)}, f32[1,6144]{1,0:T(1,128)S(1)}, u32[]{:S(2)}, u32[]{:S(2)}) collective-permute-start(f32[1,6144]{1,0:T(1,128)S(1)} %add.184), channel_id=1, source_target_pairs={{0,2},{1,3},{2,0},{3,1},{4,6},{5,7},{6,4},{7,5},{8,10},{9,11},{10,... | collective-permute-start | bytes 73736 | tf_op jit(solution)/shard_map/ppermute | solution.py:475
  76.4 4.5 %collective-permute-start.15 = (f32[1,6144]{1,0:T(1,128)S(1)}, f32[1,6144]{1,0:T(1,128)S(1)}, u32[]{:S(2)}, u32[]{:S(2)}) collective-permute-start(f32[1,6144]{1,0:T(1,128)S(1)} %add_add_fusion.1.refs_0_), channel_id=1, source_target_pairs={{0,8},{4,12},{8,0},{12,4},{16,24},{20,28},{24,16},{28,20},{1,9},{5... | collective-permute-start | bytes 73736 | tf_op jit(solution)/shard_map/ppermute | solution.py:465
  76.5 4.8 %collective-permute-start.16 = (f32[1,6144]{1,0:T(1,128)S(1)}, f32[1,6144]{1,0:T(1,128)S(1)}, u32[]{:S(2)}, u32[]{:S(2)}) collective-permute-start(f32[1,6144]{1,0:T(1,128)S(1)} %add_add_fusion.1.refs_0_), channel_id=1, source_target_pairs={{0,16},{4,20},{8,24},{12,28},{16,0},{20,4},{24,8},{28,12},{1,17},{... | collective-permute-start | bytes 73736 | tf_op jit(solution)/shard_map/ppermute | solution.py:465
  78.5 5.6 %collective-permute-start.17 = (f32[1,6144]{1,0:T(1,128)S(1)}, f32[1,6144]{1,0:T(1,128)S(1)}, u32[]{:S(2)}, u32[]{:S(2)}) collective-permute-start(f32[1,6144]{1,0:T(1,128)S(1)} %add_add_fusion.1.refs_0_), channel_id=1, source_target_pairs={{0,24},{4,28},{8,16},{12,20},{16,8},{20,12},{24,0},{28,4},{1,25},{... | collective-permute-start | bytes 73736 | tf_op jit(solution)/shard_map/ppermute | solution.py:465
  84.1 28.7 %copy-start = (bf16[6656,2048]{1,0:T(8,128)(2,1)S(1)}, bf16[6656,2048]{1,0:T(8,128)(2,1)}, u32[]{:S(2)}) copy-start(bf16[6656,2048]{1,0:T(8,128)(2,1)} %get-tuple-element.37.mass_in.mass_ref) | copy-start | bytes 81788928
  97.0 1.3 collective-permute-start.18
  98.3 4.8 %collective-permute-start.21 = (f32[1,6144]{1,0:T(1,128)S(1)}, f32[1,6144]{1,0:T(1,128)S(1)}, u32[]{:S(2)}, u32[]{:S(2)}) collective-permute-start(f32[1,6144]{1,0:T(1,128)S(1)} %add.188), channel_id=1, source_target_pairs={{0,6},{1,7},{2,4},{3,5},{4,2},{5,3},{6,0},{7,1},{8,14},{9,15},{10,... | collective-permute-start | bytes 73736 | tf_op jit(solution)/shard_map/ppermute | solution.py:475
  99.8 3.8 %collective-permute-start.20 = (f32[1,6144]{1,0:T(1,128)S(1)}, f32[1,6144]{1,0:T(1,128)S(1)}, u32[]{:S(2)}, u32[]{:S(2)}) collective-permute-start(f32[1,6144]{1,0:T(1,128)S(1)} %add.188), channel_id=1, source_target_pairs={{0,4},{1,5},{2,6},{3,7},{4,0},{5,1},{6,2},{7,3},{8,12},{9,13},{10,... | collective-permute-start | bytes 73736 | tf_op jit(solution)/shard_map/ppermute | solution.py:475
  100.4 3.8 %collective-permute-start.19 = (f32[1,6144]{1,0:T(1,128)S(1)}, f32[1,6144]{1,0:T(1,128)S(1)}, u32[]{:S(2)}, u32[]{:S(2)}) collective-permute-start(f32[1,6144]{1,0:T(1,128)S(1)} %add.188), channel_id=1, source_target_pairs={{0,2},{1,3},{2,0},{3,1},{4,6},{5,7},{6,4},{7,5},{8,10},{9,11},{10,... | collective-permute-start | bytes 73736 | tf_op jit(solution)/shard_map/ppermute | solution.py:475
  104.2 4.5 %collective-permute-start.22 = (f32[1,6144]{1,0:T(1,128)S(1)}, f32[1,6144]{1,0:T(1,128)S(1)}, u32[]{:S(2)}, u32[]{:S(2)}) collective-permute-start(f32[1,6144]{1,0:T(1,128)S(1)} %add_add_fusion.refs_0_), channel_id=1, source_target_pairs={{0,8},{4,12},{8,0},{12,4},{16,24},{20,28},{24,16},{28,20},{1,9},{5... | collective-permute-start | bytes 73736 | tf_op jit(solution)/shard_map/ppermute | solution.py:465
  104.3 4.8 %collective-permute-start.23 = (f32[1,6144]{1,0:T(1,128)S(1)}, f32[1,6144]{1,0:T(1,128)S(1)}, u32[]{:S(2)}, u32[]{:S(2)}) collective-permute-start(f32[1,6144]{1,0:T(1,128)S(1)} %add_add_fusion.refs_0_), channel_id=1, source_target_pairs={{0,16},{4,20},{8,24},{12,28},{16,0},{20,4},{24,8},{28,12},{1,17},{... | collective-permute-start | bytes 73736 | tf_op jit(solution)/shard_map/ppermute | solution.py:465
  107.2 5.6 %collective-permute-start.24 = (f32[1,6144]{1,0:T(1,128)S(1)}, f32[1,6144]{1,0:T(1,128)S(1)}, u32[]{:S(2)}, u32[]{:S(2)}) collective-permute-start(f32[1,6144]{1,0:T(1,128)S(1)} %add_add_fusion.refs_0_), channel_id=1, source_target_pairs={{0,24},{4,28},{8,16},{12,20},{16,8},{20,12},{24,0},{28,4},{1,25},{... | collective-permute-start | bytes 73736 | tf_op jit(solution)/shard_map/ppermute | solution.py:465
  112.8 21.9 %copy-start.1 = (bf16[2048,256]{1,0:T(8,128)(2,1)S(1)}, bf16[2048,256]{1,0:T(8,128)(2,1)}, u32[]{:S(2)}) copy-start(bf16[2048,256]{1,0:T(8,128)(2,1)} %get-tuple-element.34.batch_ref) | copy-start | bytes 3145732
  112.8 21.9 %copy-start.2 = (bf16[256,2048]{1,0:T(8,128)(2,1)S(1)}, bf16[256,2048]{1,0:T(8,128)(2,1)}, u32[]{:S(2)}) copy-start(bf16[256,2048]{1,0:T(8,128)(2,1)} %get-tuple-element.35.columns_ref) | copy-start | bytes 3145732
  119.1 1.2 collective-permute-start.25
  120.3 4.7 %collective-permute-start.28 = (f32[1,4224]{1,0:T(1,128)S(1)}, f32[1,4224]{1,0:T(1,128)S(1)}, u32[]{:S(2)}, u32[]{:S(2)}) collective-permute-start(f32[1,4224]{1,0:T(1,128)S(1)} %add.192), channel_id=1, source_target_pairs={{0,6},{1,7},{2,4},{3,5},{4,2},{5,3},{6,0},{7,1},{8,14},{9,15},{10,... | collective-permute-start | bytes 50696 | tf_op jit(solution)/shard_map/ppermute | solution.py:475
  122.9 3.7 %collective-permute-start.27 = (f32[1,4224]{1,0:T(1,128)S(1)}, f32[1,4224]{1,0:T(1,128)S(1)}, u32[]{:S(2)}, u32[]{:S(2)}) collective-permute-start(f32[1,4224]{1,0:T(1,128)S(1)} %add.192), channel_id=1, source_target_pairs={{0,4},{1,5},{2,6},{3,7},{4,0},{5,1},{6,2},{7,3},{8,12},{9,13},{10,... | collective-permute-start | bytes 50696 | tf_op jit(solution)/shard_map/ppermute | solution.py:475
  123.4 3.7 %collective-permute-start.26 = (f32[1,4224]{1,0:T(1,128)S(1)}, f32[1,4224]{1,0:T(1,128)S(1)}, u32[]{:S(2)}, u32[]{:S(2)}) collective-permute-start(f32[1,4224]{1,0:T(1,128)S(1)} %add.192), channel_id=1, source_target_pairs={{0,2},{1,3},{2,0},{3,1},{4,6},{5,7},{6,4},{7,5},{8,10},{9,11},{10,... | collective-permute-start | bytes 50696 | tf_op jit(solution)/shard_map/ppermute | solution.py:475
  127.1 4.5 %collective-permute-start.29 = (f32[1,4224]{1,0:T(1,128)S(1)}, f32[1,4224]{1,0:T(1,128)S(1)}, u32[]{:S(2)}, u32[]{:S(2)}) collective-permute-start(f32[1,4224]{1,0:T(1,128)S(1)} %add_add_fusion.2.refs_0_), channel_id=1, source_target_pairs={{0,8},{4,12},{8,0},{12,4},{16,24},{20,28},{24,16},{28,20},{1,9},{5... | collective-permute-start | bytes 50696 | tf_op jit(solution)/shard_map/ppermute | solution.py:465
  127.2 4.7 %collective-permute-start.30 = (f32[1,4224]{1,0:T(1,128)S(1)}, f32[1,4224]{1,0:T(1,128)S(1)}, u32[]{:S(2)}, u32[]{:S(2)}) collective-permute-start(f32[1,4224]{1,0:T(1,128)S(1)} %add_add_fusion.2.refs_0_), channel_id=1, source_target_pairs={{0,16},{4,20},{8,24},{12,28},{16,0},{20,4},{24,8},{28,12},{1,17},{... | collective-permute-start | bytes 50696 | tf_op jit(solution)/shard_map/ppermute | solution.py:465
  129.2 5.5 %collective-permute-start.31 = (f32[1,4224]{1,0:T(1,128)S(1)}, f32[1,4224]{1,0:T(1,128)S(1)}, u32[]{:S(2)}, u32[]{:S(2)}) collective-permute-start(f32[1,4224]{1,0:T(1,128)S(1)} %add_add_fusion.2.refs_0_), channel_id=1, source_target_pairs={{0,24},{4,28},{8,16},{12,20},{16,8},{20,12},{24,0},{28,4},{1,25},{... | collective-permute-start | bytes 50696 | tf_op jit(solution)/shard_map/ppermute | solution.py:465
  148.4 30.1 %all-to-all-start.1 = ((f16[8,32,2176]{2,1,0:T(8,128)(2,1)}), f16[8,32,2176]{2,1,0:T(8,128)(2,1)S(1)}, u32[]{:S(2)}, u32[]{:S(2)}) async-start(f16[8,32,2176]{2,1,0:T(8,128)(2,1)} %pad_maximum_fusion), calls=%async_computation.1 | async-start | bytes 2228224 | tf_op jit(solution)/shard_map/all_to_all | solution.py:621
  154.2 2.2 %copy-start.6 = (f32[4,2,1,2,64,256]{5,4,3,2,1,0:T(8,128)S(1)}, f32[4,2,1,2,64,256]{5,4,3,2,1,0:T(8,128)}, u32[]{:S(2)}) copy-start(f32[4,2,1,2,64,256]{5,4,3,2,1,0:T(8,128)} %get-tuple-element.52) | copy-start | bytes 3145732
  154.3 2.1 %collective-permute-start.32 = (f16[4,2,2,64,256]{4,3,0,2,1:T(8,128)(2,1)S(1)}, f16[4,2,2,64,256]{4,3,0,2,1:T(8,128)(2,1)}, u32[]{:S(2)}, u32[]{:S(2)}) collective-permute-start(f16[4,2,2,64,256]{4,3,0,2,1:T(8,128)(2,1)S(1)} %fusion), channel_id=1, source_target_pairs={{0,1},{1,0},{2,3},{3,2},{4,5},{5,4},{6,7},{7,6},{8,9},{9,8},{10,11... | collective-permute-start | bytes 1572872 | tf_op jit(solution)/shard_map/ppermute | solution.py:468
  157.7 9.8 %collective-permute-start.35 = (f16[4,64,256]{2,1,0:T(8,128)(2,1)S(1)}, f16[4,64,256]{2,1,0:T(8,128)(2,1)S(1)}, u32[]{:S(2)}, u32[]{:S(2)}) collective-permute-start(f16[4,64,256]{2,1,0:T(8,128)(2,1)S(1)} %get-tuple-element.54), channel_id=1, source_target_pairs={{0,6},{1,7},{2,4},{3,5},{4,2},{5,3},{6,0},{7,1},{8,14},{9,15},{10,... | collective-permute-start | bytes 393224 | tf_op jit(solution)/shard_map/ppermute | solution.py:475
  159.7 12.6 %collective-permute-start.34 = (f16[4,64,256]{2,1,0:T(8,128)(2,1)S(1)}, f16[4,64,256]{2,1,0:T(8,128)(2,1)S(1)}, u32[]{:S(2)}, u32[]{:S(2)}) collective-permute-start(f16[4,64,256]{2,1,0:T(8,128)(2,1)S(1)} %get-tuple-element.55), channel_id=1, source_target_pairs={{0,4},{1,5},{2,6},{3,7},{4,0},{5,1},{6,2},{7,3},{8,12},{9,13},{10,... | collective-permute-start | bytes 393224 | tf_op jit(solution)/shard_map/ppermute | solution.py:475
  159.9 12.5 %collective-permute-start.33 = (f16[4,64,256]{2,1,0:T(8,128)(2,1)S(1)}, f16[4,64,256]{2,1,0:T(8,128)(2,1)S(1)}, u32[]{:S(2)}, u32[]{:S(2)}) collective-permute-start(f16[4,64,256]{2,1,0:T(8,128)(2,1)S(1)} %get-tuple-element.53), channel_id=1, source_target_pairs={{0,2},{1,3},{2,0},{3,1},{4,6},{5,7},{6,4},{7,5},{8,10},{9,11},{10,... | collective-permute-start | bytes 393224 | tf_op jit(solution)/shard_map/ppermute | solution.py:475
  172.5 7.4 %collective-permute-start.36 = (f16[64,256]{1,0:T(8,128)(2,1)S(1)}, f16[64,256]{1,0:T(8,128)(2,1)S(1)}, u32[]{:S(2)}, u32[]{:S(2)}) collective-permute-start(f16[64,256]{1,0:T(8,128)(2,1)S(1)} %get-tuple-element.66), channel_id=1, source_target_pairs={{0,8},{4,12},{8,0},{12,4},{16,24},{20,28},{24,16},{28,20},{1,9},{5... | collective-permute-start | bytes 98312 | tf_op jit(solution)/shard_map/ppermute | solution.py:465
  172.6 7.3 %collective-permute-start.37 = (f16[64,256]{1,0:T(8,128)(2,1)S(1)}, f16[64,256]{1,0:T(8,128)(2,1)S(1)}, u32[]{:S(2)}, u32[]{:S(2)}) collective-permute-start(f16[64,256]{1,0:T(8,128)(2,1)S(1)} %get-tuple-element.65), channel_id=1, source_target_pairs={{0,16},{4,20},{8,24},{12,28},{16,0},{20,4},{24,8},{28,12},{1,17},{... | collective-permute-start | bytes 98312 | tf_op jit(solution)/shard_map/ppermute | solution.py:465
  175.9 5.7 %collective-permute-start.38 = (f16[64,256]{1,0:T(8,128)(2,1)S(1)}, f16[64,256]{1,0:T(8,128)(2,1)S(1)}, u32[]{:S(2)}, u32[]{:S(2)}) collective-permute-start(f16[64,256]{1,0:T(8,128)(2,1)S(1)} %get-tuple-element.64), channel_id=1, source_target_pairs={{0,24},{4,28},{8,16},{12,20},{16,8},{20,12},{24,0},{28,4},{1,25},{... | collective-permute-start | bytes 98312 | tf_op jit(solution)/shard_map/ppermute | solution.py:465
  181.7 3.7 %collective-permute-start.39 = (f32[72,256]{1,0:T(8,128)S(1)}, f32[72,256]{1,0:T(8,128)S(1)}, u32[]{:S(2)}, u32[]{:S(2)}) collective-permute-start(f32[72,256]{1,0:T(8,128)S(1)} %concatenate.7.refs_0_), channel_id=1, source_target_pairs={{0,1},{1,0},{2,3},{3,2},{4,5},{5,4},{6,7},{7,6},{8,9},{9,8},{10,11... | collective-permute-start | bytes 221192 | tf_op jit(solution)/shard_map/ppermute | solution.py:468
  181.8 5.1 %collective-permute-start.40 = (f32[72,256]{1,0:T(8,128)S(1)}, f32[72,256]{1,0:T(8,128)S(1)}, u32[]{:S(2)}, u32[]{:S(2)}) collective-permute-start(f32[72,256]{1,0:T(8,128)S(1)} %concatenate.7.refs_0_), channel_id=1, source_target_pairs={{0,2},{1,3},{2,0},{3,1},{4,6},{5,7},{6,4},{7,5},{8,10},{9,11},{10,... | collective-permute-start | bytes 221192 | tf_op jit(solution)/shard_map/ppermute | solution.py:468
  182.4 5.2 %collective-permute-start.41 = (f32[72,256]{1,0:T(8,128)S(1)}, f32[72,256]{1,0:T(8,128)S(1)}, u32[]{:S(2)}, u32[]{:S(2)}) collective-permute-start(f32[72,256]{1,0:T(8,128)S(1)} %concatenate.7.refs_0_), channel_id=1, source_target_pairs={{0,3},{1,2},{2,1},{3,0},{4,7},{5,6},{6,5},{7,4},{8,11},{9,10},{10,... | collective-permute-start | bytes 221192 | tf_op jit(solution)/shard_map/ppermute | solution.py:468
  183.9 3.7 %copy-start.3 = (bf16[256,256]{1,0:T(8,128)(2,1)S(1)}, bf16[256,256]{1,0:T(8,128)(2,1)}, u32[]{:S(2)}) copy-start(bf16[256,256]{1,0:T(8,128)(2,1)} %embed_ref.1) | copy-start | bytes 393220
  183.9 3.7 %copy-start.4 = (bf16[256,256]{1,0:T(8,128)(2,1)S(1)}, bf16[256,256]{1,0:T(8,128)(2,1)}, u32[]{:S(2)}) copy-start(bf16[256,256]{1,0:T(8,128)(2,1)} %get-tuple-element.27.order_ref) | copy-start | bytes 393220
